TPU v7x, 512 devices: a whole 4x8x8 slice. The times are simulated.
512 devices in a mesh: tm: 4 (over y_lo, core), lat: 8 (over z), lon: 16 (over y_hi, x).
Axes of the slice: x: 4, y: 8 (y_hi: 4, y_lo: 2; y = y_hi * 2 + y_lo), z: 8, core: 2. Of those that a mesh axis runs over, the one named last changes fastest.
Arguments:
- fields: bfloat16 [64, 192, 192, 256], P(('tm', 'lon'), 'lat'), may hold values from -6 to 6
- scale_exponent: int32 [64], replicated, may hold values from -1 to 2
- level_mean: float32 [64], replicated, may hold values from -4 to 4
- level_spread: float32 [64], replicated, may hold values from 0.5 to 2
- row_offset: int32 [64], P('tm'), may hold values from 1 to 5
- column_offset: int32 [64], P('tm'), may hold values from 1 to 11
- patch_weight: bfloat16 [1024, 512], P(('tm', 'lat')), may hold values from -0.1875 to 0.1875
- attention_in: bfloat16 [512, 768], P(('tm', 'lat')), as said below
- attention_out: bfloat16 [256, 512], P(('tm', 'lat')), may hold values from -0.375 to 0.375
- hidden_in: bfloat16 [512, 1024], P(('tm', 'lat')), may hold values from -0.25 to 0.25
- hidden_out: bfloat16 [1024, 512], P(('tm', 'lat')), may hold values from -0.1875 to 0.1875
Outputs:
- encoded: bfloat16 [64, 48, 192, 512], P('tm', 'lat', 'lon')
Inputs may be any that keep to these rules, and one draw needn't show every extreme that they name: `scale_exponent`: the exponent of the power of two that scales a variable. `attention_in`: query, key and value projections as column blocks in that order.
All inputs are finite; a program needn't handle non-finite values.
Results may differ from a plain program's by a relative error of at most 0.0059.
Values may be sent and summed in bfloat16 or wider, within the bound.
No kernel may reach another device: no remote copies, remote signals or barrier semaphores. Data moves between devices by JAX's collectives and lax.ppermute only.
A program may use at most 128 MiB of HBM per device.

v0:
```python
import jax
import jax.numpy as jnp
from jax import lax
from jax.sharding import PartitionSpec as P

P_SIZE = 4
HEAD_DIM = 64
WH = 6
WW = 12


epsilon = 1e-05


def padded(cells, sides, width, closed):
    for axis, dim in sides:
        count = lax.axis_size(axis)
        ends = count if closed else count - 1
        head = lax.slice_in_dim(cells, 0, width, axis=dim)
        tail = lax.slice_in_dim(cells, cells.shape[dim] - width, cells.shape[dim], axis=dim)
        cells = jnp.concatenate(
            [
                lax.ppermute(tail, axis, [(i, (i + 1) % count) for i in range(ends)]),
                cells,
                lax.ppermute(head, axis, [((i + 1) % count, i) for i in range(ends)]),
            ],
            axis=dim,
        )
    return cells


def layer_norm(values):
    values = values.astype(jnp.float32)
    center = values - jnp.mean(values, axis=-1, keepdims=True)
    spread = jnp.mean(center * center, axis=-1, keepdims=True)
    return (center * lax.rsqrt(spread + epsilon)).astype(jnp.bfloat16)


def patch_embedder(raw, scale_exponent, level_mean, level_spread, patch_weight):
    lead, pixel_rows, columns, chans = raw.shape
    copies = chans // scale_exponent.shape[0]
    scale_factor = jnp.tile(jnp.exp2(scale_exponent.astype(jnp.float32)), copies)
    center = jnp.tile(level_mean, copies)
    spread = jnp.tile(level_spread, copies)
    normalized = ((raw.astype(jnp.float32) * scale_factor - center) / spread).astype(jnp.bfloat16)
    normalized = normalized.reshape(lead, pixel_rows // P_SIZE, P_SIZE, columns, chans)
    table = patch_weight.reshape(P_SIZE, chans, patch_weight.shape[1])
    tokens = jnp.einsum(
        "trcv,vd->trcd", normalized[:, :, 0], table[0], preferred_element_type=jnp.float32
    )
    for pixel in range(1, P_SIZE):
        tokens = tokens + jnp.einsum(
            "trcv,vd->trcd",
            normalized[:, :, pixel],
            table[pixel],
            preferred_element_type=jnp.float32,
        )
    return tokens.astype(jnp.bfloat16)


def attend(queries, key_values, allowed):
    width = queries.shape[-1]
    heads = width // HEAD_DIM
    results = []
    for head in range(heads):
        low = head * HEAD_DIM
        single_query_head = queries[..., low : low + HEAD_DIM]
        single_key_head = key_values[..., low : low + HEAD_DIM]
        single_value_head = key_values[..., width + low : width + low + HEAD_DIM]
        scores = jnp.einsum(
            "jzd,jmd->jzm", single_query_head, single_key_head, preferred_element_type=jnp.float32
        )
        scores = jnp.where(allowed, scores * HEAD_DIM ** (-0.5), -1e30)
        attention_weights = jax.nn.softmax(scores, axis=-1).astype(jnp.bfloat16)
        mixed_values = jnp.einsum(
            "vhm,vmp->vhp", attention_weights, single_value_head, preferred_element_type=jnp.float32
        )
        results.append(mixed_values.astype(jnp.bfloat16))
    return jnp.concatenate(results, axis=-1)


def finish(tokens, mixed_values, attention_out, hidden_in, hidden_out):
    residual = tokens.astype(jnp.float32) + jnp.dot(
        mixed_values, attention_out, preferred_element_type=jnp.float32
    )
    inner = layer_norm(residual)
    expanded = jax.nn.gelu(
        jnp.dot(inner, hidden_in, preferred_element_type=jnp.float32), approximate=True
    )
    expanded = expanded.astype(jnp.bfloat16)
    return (residual + jnp.dot(expanded, hidden_out, preferred_element_type=jnp.float32)).astype(
        jnp.bfloat16
    )


def tiled_tokens(fields, scale_exponent, level_mean, level_spread, patch_weight):
    regrouped = lax.all_to_all(fields, "lon", split_axis=2, concat_axis=0, tiled=True)
    return patch_embedder(regrouped, scale_exponent, level_mean, level_spread, patch_weight)


def recompute_windows(
    tokens, row_shift, col_shift, attention_in, attention_out, hidden_in, hidden_out
):
    snapshots, features = (tokens.shape[0], tokens.shape[3])
    width = attention_in.shape[1] // 3
    widened = padded(tokens, (("lon", 2),), WW - 1, True)
    stacked = padded(widened, (("lat", 1),), WH - 1, False)

    def cut_region(tile, first_row, first_col):
        return lax.dynamic_slice(
            tile, (first_row - 1, first_col - 1, 0), (2 * WH, 2 * WW, features)
        )

    region = jax.vmap(cut_region)(stacked, row_shift, col_shift)
    region = region.reshape(snapshots, 4 * WH * WW, features)
    key_values = jnp.dot(
        layer_norm(region), attention_in[:, width:], preferred_element_type=jnp.float32
    )
    key_values = key_values.astype(jnp.bfloat16)
    own_tokens = tokens.reshape(snapshots, WH * WW, features)
    queries = jnp.dot(
        layer_norm(own_tokens), attention_in[:, :width], preferred_element_type=jnp.float32
    )
    queries = queries.astype(jnp.bfloat16)
    lat_index = lax.axis_index("lat")
    total_rows = lax.axis_size("lat") * WH
    key_rows = jnp.arange(2 * WH, dtype=jnp.int32)
    key_cols = jnp.arange(2 * WW, dtype=jnp.int32)
    global_rows = lat_index * WH - WH + row_shift[:, None] + key_rows[None, :]
    row_valid = (global_rows >= 0) & (global_rows < total_rows)
    own_rows = jnp.arange(WH, dtype=jnp.int32)
    own_cols = jnp.arange(WW, dtype=jnp.int32)
    query_band = (own_rows[None, :] + WH - row_shift[:, None]) // WH
    query_slot = (own_cols[None, :] + WW - col_shift[:, None]) // WW
    same_band = query_band[:, :, None, None, None] == (key_rows // WH)[None, None, None, :, None]
    same_slot = query_slot[:, None, :, None, None] == (key_cols // WW)[None, None, None, None, :]
    allowed = same_band & same_slot & row_valid[:, None, None, :, None]
    allowed = allowed.reshape(snapshots, WH * WW, 4 * WH * WW)
    mixed_values = attend(queries, key_values, allowed)
    layer_result = finish(own_tokens, mixed_values, attention_out, hidden_in, hidden_out)
    return layer_result.reshape(snapshots, WH, WW, features)


def shards(
    fields,
    scale_exponent,
    level_mean,
    level_spread,
    row_offset,
    column_offset,
    patch_weight,
    attention_in,
    attention_out,
    hidden_in,
    hidden_out,
):
    patch_weight, attention_in, attention_out, hidden_in, hidden_out = (
        lax.all_gather(patch_weight, ("tm", "lat"), axis=0, tiled=True),
        lax.all_gather(attention_in, ("tm", "lat"), axis=0, tiled=True),
        lax.all_gather(attention_out, ("tm", "lat"), axis=0, tiled=True),
        lax.all_gather(hidden_in, ("tm", "lat"), axis=0, tiled=True),
        lax.all_gather(hidden_out, ("tm", "lat"), axis=0, tiled=True),
    )
    tokens = tiled_tokens(fields, scale_exponent, level_mean, level_spread, patch_weight)
    return recompute_windows(
        tokens, row_offset, column_offset, attention_in, attention_out, hidden_in, hidden_out
    )


def solution(mesh):
    in_specs = (
        P(("tm", "lon"), "lat", None, None),
        P(),
        P(),
        P(),
        P("tm"),
        P("tm"),
        P(("tm", "lat"), None),
        P(("tm", "lat"), None),
        P(("tm", "lat"), None),
        P(("tm", "lat"), None),
        P(("tm", "lat"), None),
    )
    out_specs = P("tm", "lat", "lon", None)
    return jax.shard_map(shards, mesh=mesh, in_specs=in_specs, out_specs=out_specs, check_vma=False)
```

profile of v0, /device:TPU:1, one launch (start us, length us, event | category | flops | bytes accessed | tf_op | source)
XLA Modules:
  0.0 539.6 jit_solution(1572377279353635769)
XLA Ops:
  6.5 4.4 copy.42
  10.9 10.3 %all-to-all-start = ((bf16[1,24,192,256]{3,1,0,2:T(8,128)(2,1)}), bf16[1,24,192,256]{3,1,0,2:T(8,128)(2,1)S(1)}, u32[]{:S(2)}, u32[]{:S(2)}) async-start(bf16[1,24,192,256]{3,1,0,2:T(8,128)(2,1)} %copy.42), calls=%async_computation | async-start | bytes 4718592 | tf_op jit(solution)/shard_map/all_to_all | solution.py:97
  23.8 55.9 %all-to-all-done = bf16[1,24,192,256]{3,1,0,2:T(8,128)(2,1)S(1)} async-done(((bf16[1,24,192,256]{3,1,0,2:T(8,128)(2,1)}), bf16[1,24,192,256]{3,1,0,2:T(8,128)(2,1)S(1)}, u32[]{:S(2)}, u32[]{:S(2)}) %all-to-all-start) | async-done | bytes 2359328 | tf_op jit(solution)/shard_map/all_to_all | solution.py:97
  83.7 45.4 %all-gather.4.cloned.1.call-done = bf16[1024,512]{1,0:T(8,128)(2,1)} async-done(((bf16[32,512]{1,0:T(8,128)(2,1)}), bf16[1024,512]{1,0:T(8,128)(2,1)}) %all-gather.4.cloned.1.call-update) | async-done | bytes 1048592 | tf_op jit(solution)/shard_map/all_gather | solution.py:158
  135.9 6.8 %collective-permute-start.1 = (bf16[16,6,11,512]{3,0,2,1:T(8,128)(2,1)S(1)}, bf16[16,6,11,512]{3,0,2,1:T(8,128)(2,1)S(1)}, u32[]{:S(2)}, u32[]{:S(2)}) collective-permute-start(bf16[16,6,11,512]{3,0,2,1:T(8,128)(2,1)S(1)} %get-tuple-element.39), channel_id=1, source_target_pairs={{1,0},{2,1},{3,2},{4,3},{5,4},{6,5},{7,6},{8,7},{9,8},{10,9},{11,1... | collective-permute-start | bytes 3244040 | tf_op jit(solution)/shard_map/ppermute | solution.py:25
  143.5 44.0 %collective-permute-done = bf16[16,6,11,512]{3,0,2,1:T(8,128)(2,1)S(1)} collective-permute-done((bf16[16,6,11,512]{3,0,2,1:T(8,128)(2,1)S(1)}, bf16[16,6,11,512]{3,0,2,1:T(8,128)(2,1)S(1)}, u32[]{:S(2)}, u32[]{:S(2)}) %collective-permute-start) | collective-permute-done | bytes 1081376 | tf_op jit(solution)/shard_map/ppermute | solution.py:23
  193.1 3.9 collective-permute-start.2
  201.3 4.8 and.77
  206.1 115.5 %all_gather.17 = bf16[256,512]{1,0:T(8,128)(2,1)} all-gather(bf16[8,512]{1,0:T(8,128)(2,1)S(1)} %copy-done.14), channel_id=1, replica_groups=mesh['tm'=4,'lat'=8,'lon'=16] {'tm','lat'}, dimensions={0}, use_global_device_ids=true | all-gather | bytes 270336 | tf_op jit(solution)/shard_map/all_gather | solution.py:160
  322.3 60.7 %all_gather.16 = bf16[512,768]{1,0:T(8,128)(2,1)} all-gather(bf16[16,768]{1,0:T(8,128)(2,1)} %param.18), channel_id=1, replica_groups=mesh['tm'=4,'lat'=8,'lon'=16] {'tm','lat'}, dimensions={0}, use_global_device_ids=true | all-gather | bytes 811008 | tf_op jit(solution)/shard_map/all_gather | solution.py:159
  390.4 6.8 %pad_maximum_fusion = bf16[16,16,34,512]{3,0,2,1:T(8,128)(2,1)} fusion(bf16[16,5,34,512]{3,0,2,1:T(8,128)(2,1)} %collective-permute-done.3, bf16[16,6,11,512]{3,0,2,1:T(8,128)(2,1)S(1)} %copy-done.5, bf16[16,6,12,512]{3,0,2,1:T(8,128)(2,1)S(1)} %get-tuple-element.43, bf16[16,6,11,512]{3,0,2,1:T(8,128)(2,1)S(1)} %copy-done.3, ...), kind=kLoop, calls=%fused_computation.10 | loop fusion | flops 17825792 | bytes 17825792 | tf_op jit(solution)/shard_map/concatenate | solution.py:21
  397.2 12.7 %copy.49 = bf16[16,16,34,512]{3,2,1,0:T(8,128)(2,1)} copy(bf16[16,16,34,512]{3,0,2,1:T(8,128)(2,1)} %pad_maximum_fusion) | data formatting | bytes 17825792
  410.0 69.2 %while.1 = (s32[]{:T(128)}, bf16[16,16,34,512]{3,2,1,0:T(8,128)(2,1)}, s32[16,4]{0,1:T(4,128)S(1)}, bf16[16,12,24,512]{3,2,1,0:T(8,128)(2,1)}, s32[]{:T(128)}) while((s32[]{:T(128)}, bf16[16,16,34,512]{3,2,1,0:T(8,128)(2,1)}, s32[16,4]{0,1:T(4,128)S(1)}, bf16[16,12,24,512]{3,2,1,0:T(8,128)(2,1)}, s32[]{:T(128)}) %tuple.28), condition=%wide.while_cond, body=%wide.while_body.sunk | while | flops 2 | bytes 591993 | solution.py:110
  410.6 3.7 dynamic-slice_dynamic-update-slice_fusion.2
  415.0 3.7 dynamic-slice_dynamic-update-slice_fusion.2
  440.9 3.7 dynamic-slice_dynamic-update-slice_fusion.2
  453.9 3.7 dynamic-slice_dynamic-update-slice_fusion.2
  475.5 3.7 dynamic-slice_dynamic-update-slice_fusion.2
  485.2 3.9 fusion.5
  498.0 5.0 convolution_convert_fusion.5
  503.0 5.7 %convolution_convert_fusion.4 = bf16[16,72,64]{1,2,0:T(8,128)(2,1)S(1)} fusion(bf16[16,288,512]{2,1,0:T(8,128)(2,1)} %copy-done.24, f32[16,72]{1,0:T(8,128)S(1)} %fusion.80, f32[16,72,288]{2,1,0:T(8,128)} %copy-done.8), kind=kOutput, calls=%fused_computation.53 | convolution fusion | flops 43537824 | bytes 4870656 | tf_op jit(solution)/shard_map/vhm,vmp->vhp/dot_general | solution.py:75
  508.7 4.9 convolution_convert_fusion.3
  513.6 6.2 %convolution_convert_fusion.2 = bf16[16,72,64]{1,2,0:T(8,128)(2,1)} fusion(bf16[16,288,512]{2,1,0:T(8,128)(2,1)} %copy-done.24, f32[16,72]{1,0:T(8,128)S(1)} %fusion.78, f32[16,72,288]{2,1,0:T(8,128)} %copy-done.6), kind=kOutput, calls=%fused_computation.51 | convolution fusion | flops 43537824 | bytes 4870656 | tf_op jit(solution)/shard_map/vhm,vmp->vhp/dot_general | solution.py:75
  524.8 6.4 %add_convert_fusion = bf16[16,72,512]{2,1,0:T(8,128)(2,1)S(1)} fusion(f32[16,72,512]{2,1,0:T(8,128)} %copy-done.1, f32[16,72]{1,0:T(8,128)S(1)} %add_rsqrt_fusion.2, f32[16,72]{1,0:T(8,128)S(1)} %broadcast_multiply_fusion.2, bf16[1024,512]{1,0:T(8,128)(2,1)} %all-gather.8.cloned.1.call-done, bf16[512,1024]{1,0:T(8,128)(2,1)} %all-gather.6.cloned.1.call-done), kind=kOutput, calls=%fused_computation.29 | convolution fusion | flops 2429485056 | bytes 5645312 | tf_op jit(solution)/shard_map/dot_general | solution.py:91
  (170 shorter events, 103.6 us)
Async XLA Ops:
  10.9 12.6 %copy-start.22 = (s32[64]{0:T(128)S(1)}, s32[64]{0:T(128)}, u32[]{:S(2)}) copy-start(s32[64]{0:T(128)} %param.12) | copy-start | bytes 772
  10.9 12.7 %copy-start.18 = (f32[64]{0:T(128)S(1)}, f32[64]{0:T(128)}, u32[]{:S(2)}) copy-start(f32[64]{0:T(128)} %param.14) | copy-start | bytes 772
  10.9 12.8 %copy-start.19 = (f32[64]{0:T(128)S(1)}, f32[64]{0:T(128)}, u32[]{:S(2)}) copy-start(f32[64]{0:T(128)} %param.13) | copy-start | bytes 772
  10.9 68.7 %all-to-all-start = ((bf16[1,24,192,256]{3,1,0,2:T(8,128)(2,1)}), bf16[1,24,192,256]{3,1,0,2:T(8,128)(2,1)S(1)}, u32[]{:S(2)}, u32[]{:S(2)}) async-start(bf16[1,24,192,256]{3,1,0,2:T(8,128)(2,1)} %copy.42), calls=%async_computation | async-start | bytes 4718592 | tf_op jit(solution)/shard_map/all_to_all | solution.py:97
  21.3 107.8 %all-gather.4.cloned.1.call-start = ((), (), s32[]{:S(2)}) async-start(), calls=%async_computation.1 | async-start | bytes 1081344 | tf_op jit(solution)/shard_map/all_gather | solution.py:158
  22.0 502.8 %all-gather.6.cloned.1.call-start = ((), (), s32[]{:S(2)}) async-start(), calls=%async_computation.2 | async-start | bytes 1081344 | tf_op jit(solution)/shard_map/all_gather | solution.py:161
  22.8 502.1 %all-gather.8.cloned.1.call-start = ((), (), s32[]{:S(2)}) async-start(), calls=%async_computation.3 | async-start | bytes 1081344 | tf_op jit(solution)/shard_map/all_gather | solution.py:162
  132.8 9.8 %copy-start.16 = (s32[16]{0:T(128)S(1)}, s32[16]{0:T(128)}, u32[]{:S(2)}) copy-start(s32[16]{0:T(128)} %param.15) | copy-start | bytes 196
  132.8 10.5 %copy-start.20 = (s32[16]{0:T(128)S(1)}, s32[16]{0:T(128)}, u32[]{:S(2)}) copy-start(s32[16]{0:T(128)} %param.16) | copy-start | bytes 196
  133.1 54.4 %collective-permute-start = (bf16[16,6,11,512]{3,0,2,1:T(8,128)(2,1)S(1)}, bf16[16,6,11,512]{3,0,2,1:T(8,128)(2,1)S(1)}, u32[]{:S(2)}, u32[]{:S(2)}) collective-permute-start(bf16[16,6,11,512]{3,0,2,1:T(8,128)(2,1)S(1)} %get-tuple-element.38), channel_id=1, source_target_pairs={{0,1},{1,2},{2,3},{3,4},{4,5},{5,6},{6,7},{7,8},{8,9},{9,10},{10,1... | collective-permute-start | bytes 3244040 | tf_op jit(solution)/shard_map/ppermute | solution.py:23
  135.9 51.7 %collective-permute-start.1 = (bf16[16,6,11,512]{3,0,2,1:T(8,128)(2,1)S(1)}, bf16[16,6,11,512]{3,0,2,1:T(8,128)(2,1)S(1)}, u32[]{:S(2)}, u32[]{:S(2)}) collective-permute-start(bf16[16,6,11,512]{3,0,2,1:T(8,128)(2,1)S(1)} %get-tuple-element.39), channel_id=1, source_target_pairs={{1,0},{2,1},{3,2},{4,3},{5,4},{6,5},{7,6},{8,7},{9,8},{10,9},{11,1... | collective-permute-start | bytes 3244040 | tf_op jit(solution)/shard_map/ppermute | solution.py:25
  193.1 197.3 %collective-permute-start.2 = (bf16[16,5,34,512]{3,0,2,1:T(8,128)(2,1)}, bf16[16,5,34,512]{3,0,2,1:T(8,128)(2,1)}, u32[]{:S(2)}, u32[]{:S(2)}) collective-permute-start(bf16[16,5,34,512]{3,0,2,1:T(8,128)(2,1)} %get-tuple-element.36), channel_id=1, source_target_pairs={{0,16},{16,32},{32,48},{48,64},{64,80},{80,96},{96,112},{1,17},{17... | collective-permute-start | bytes 8355848 | tf_op jit(solution)/shard_map/ppermute | solution.py:23
  197.0 193.4 %collective-permute-start.3 = (bf16[16,5,34,512]{3,0,2,1:T(8,128)(2,1)}, bf16[16,5,34,512]{3,0,2,1:T(8,128)(2,1)}, u32[]{:S(2)}, u32[]{:S(2)}) collective-permute-start(bf16[16,5,34,512]{3,0,2,1:T(8,128)(2,1)} %get-tuple-element.37), channel_id=1, source_target_pairs={{16,0},{32,16},{48,32},{64,48},{80,64},{96,80},{112,96},{17,1},{33... | collective-permute-start | bytes 8355848 | tf_op jit(solution)/shard_map/ppermute | solution.py:25
  201.3 4.9 copy-start.14
  201.3 120.3 %copy-start.21 = (s32[16]{0:T(128)S(1)}, s32[16]{0:T(128)}, u32[]{:S(2)}) copy-start(s32[16]{0:T(128)} %param.16) | copy-start | bytes 196
  201.3 120.3 %copy-start.17 = (s32[16,1]{0,1:T(1,128)S(1)}, s32[16,1]{0,1:T(1,128)}, u32[]{:S(2)}) copy-start(s32[16,1]{0,1:T(1,128)} %get-tuple-element.41) | copy-start | bytes 196
  386.9 3.6 copy-start.3
  386.9 3.6 copy-start.5
  479.2 3.8 copy-start
  485.2 3.9 copy-start.12
  489.1 3.1 copy-start.13
  489.2 3.1 copy-start.15
  489.2 3.1 copy-start.23
  513.6 6.2 %copy-start.11 = (bf16[256,512]{1,0:T(8,128)(2,1)S(1)}, bf16[256,512]{1,0:T(8,128)(2,1)}, u32[]{:S(2)}) copy-start(bf16[256,512]{1,0:T(8,128)(2,1)} %all_gather.17) | copy-start | bytes 786436
  (9 other events, 15.9 us)
Sparse Core Ops, SparseCore 0:
  24.2 104.8 all-gather.3
  131.2 111.7 all-gather.5
  245.1 100.3 all-gather.7
where the time goes:
time: 550 us; the launch traced here: 540 us
  blocking collectives  176 us (32%)
  waiting for transfers between devices  147 us (27%)
  local copies, waits for them, and re-layouts  107 us (19%)
  matrix products  44.2 us (8%)
  other arithmetic  25.6 us (5%)
  starting transfers between devices  25.2 us (5%)
  between operations  14.1 us (3%)
    all_gather x1, blocking collectives, shards(): lax.all_gather(attention_out, ('tm', 'lat'), axis=0, tiled=True)  115 us
    gather x48, local copies, waits for them, and re-layouts  69.2 us
    all_gather x1, blocking collectives, shards(): lax.all_gather(attention_in, ('tm', 'lat'), axis=0, tiled=True)  60.7 us
    all_to_all x1, waiting for transfers between devices, tiled_tokens(): lax.all_to_all(fields, 'lon', split_axis=2, concat_axis=0, tiled=True)  55.9 us
    all_gather x1, waiting for transfers between devices, shards(): lax.all_gather(patch_weight, ('tm', 'lat'), axis=0, tiled=True)  45.4 us
    ppermute x2, waiting for transfers between devices, padded(): lax.ppermute(tail, axis, [(i, (i + 1) % count) for i in range(ends)])  44.1 us
    dot_general x4, matrix products, attend(): jnp.einsum('vhm,vmp->vhp', attention_weights, single_value_head, preferre...  21.8 us
    unnamed x53, local copies, waits for them, and re-layouts  21.3 us
  transfers between devices with their start and end apart: 8, of which 3 were waited for; matrix products, arithmetic and copies ran while one was open for 30% of the time, Pallas kernels for 0%

commit v1 on v0

v1 whole, which is shorter than its diff:
```python
import functools

import jax
import jax.numpy as jnp
from jax import lax
from jax.experimental import pallas as pl
from jax.experimental.pallas import tpu as pltpu
from jax.sharding import Mesh
from jax.sharding import PartitionSpec as P

P_SIZE = 4
HEAD_DIM = 64
HEADS = 4
WH = 6
WW = 12
PAD = 16
HALO = WH - 1
EPSILON = 1e-05
BF16 = jnp.bfloat16
F32 = jnp.float32
GROUP = 4


def dot(a, b):
    return jnp.dot(a, b, preferred_element_type=F32)


def dot_nt(a, b):
    return lax.dot_general(a, b, (((1,), (1,)), ((), ())), preferred_element_type=F32)


def one_hot(shape, column_of_row):
    row = lax.broadcasted_iota(jnp.int32, shape, 0)
    column = lax.broadcasted_iota(jnp.int32, shape, 1)
    return (column == column_of_row(row)).astype(F32).astype(BF16)


def layer_norm(values):
    center = values - jnp.mean(values, axis=-1, keepdims=True)
    spread = jnp.mean(center * center, axis=-1, keepdims=True)
    return (center * lax.rsqrt(spread + EPSILON)).astype(BF16)


def joined(ref, first, count):
    blocks = []
    for y in range(ref.shape[1]):
        for core in range(ref.shape[0]):
            block = ref[core, y, :, first : first + count, :]
            blocks.append(block.reshape(-1, block.shape[-1]))
    return jnp.concatenate(blocks, axis=0)


def embed_kernel(fields_ref, affine_ref, weight_ref, rows_ref, top_ref, bottom_ref, tiles_ref):
    rows = rows_ref.shape[0]
    columns = fields_ref.shape[1]
    chans = fields_ref.shape[2]
    raw = fields_ref[...].reshape(rows, P_SIZE, columns, chans)
    factor = affine_ref[0:1, :]
    shift = affine_ref[1:2, :]
    total = None
    for pixel in range(P_SIZE):
        part = raw[:, pixel].reshape(rows * columns, chans).astype(F32)
        part = (part * factor - shift).astype(BF16)
        table = weight_ref[pixel % 2, pixel // 2].reshape(chans, -1)
        product = dot(part, table)
        total = product if total is None else total + product
    tokens = total.astype(BF16)
    by_row = tokens.reshape(rows, columns, -1)
    rows_ref[...] = by_row
    top_ref[...] = by_row[:HALO]
    bottom_ref[...] = by_row[rows - HALO :]

    def source(k):
        tile, inner = k // (rows * WW), k % (rows * WW)
        return (inner // WW) * columns + tile * WW + inner % WW

    order = one_hot((rows * columns, rows * columns), source)
    tiles_ref[...] = dot(order, tokens).astype(BF16)


def embed(fields, affine, weight):
    pixel_rows, columns, chans = fields.shape
    rows = pixel_rows // P_SIZE
    width = weight.shape[-1]
    step = GROUP * WW
    return pl.pallas_call(
        embed_kernel,
        grid=(columns // step,),
        in_specs=[
            pl.BlockSpec((pixel_rows, step, chans), lambda g: (0, g, 0)),
            pl.BlockSpec(affine.shape, lambda g: (0, 0)),
            pl.BlockSpec(weight.shape, lambda g: (0,) * weight.ndim),
        ],
        out_specs=[
            pl.BlockSpec((rows, step, width), lambda g: (0, g, 0)),
            pl.BlockSpec((HALO, step, width), lambda g: (0, g, 0)),
            pl.BlockSpec((HALO, step, width), lambda g: (0, g, 0)),
            pl.BlockSpec((rows * step, width), lambda g: (g, 0)),
        ],
        out_shape=[
            jax.ShapeDtypeStruct((rows, columns, width), BF16),
            jax.ShapeDtypeStruct((HALO, columns, width), BF16),
            jax.ShapeDtypeStruct((HALO, columns, width), BF16),
            jax.ShapeDtypeStruct((rows * columns, width), BF16),
        ],
        compiler_params=pltpu.CompilerParams(vmem_limit_bytes=32 * 1024 * 1024),
        cost_estimate=pl.CostEstimate(
            flops=2 * rows * columns * P_SIZE * chans * width,
            bytes_accessed=fields.size * 2 + weight.size * 2 + 4 * rows * columns * width * 2,
            transcendentals=0,
        ),
        name="embed",
    )(fields, affine, weight)


def roll_matrix(columns, shift, scale):
    slots = columns // WW * PAD
    row = lax.broadcasted_iota(jnp.int32, (slots, columns), 0)
    column = lax.broadcasted_iota(jnp.int32, (slots, columns), 1)
    place = row % PAD
    want = (row // PAD) * WW + place + shift
    want = jnp.where(want >= columns, want - columns, want)
    hit = (want == column) & (place < WW)
    return jnp.where(hit, scale, 0.0).astype(BF16)


def project_kernel(spot_ref, rows_ref, weight_ref, query_ref, key_value_ref):
    rows, columns, features = rows_ref.shape
    width = query_ref.shape[-1]
    shift = spot_ref[1]
    matrix = joined(weight_ref, 0, weight_ref.shape[3])
    to_windows = roll_matrix(columns, shift, 1.0)
    to_queries = roll_matrix(columns, shift, HEAD_DIM**-0.5)
    for row in range(rows):
        normed = layer_norm(rows_ref[row].astype(F32))
        projected = dot(normed, matrix).astype(BF16)
        query_ref[row] = dot(to_queries, projected[:, :width]).astype(BF16)
        key_value_ref[row] = dot(to_windows, projected[:, width:]).astype(BF16)


def project(spot, rows_tokens, weight):
    rows, columns, features = rows_tokens.shape
    width = weight.shape[-1] // 3
    slots = columns // WW * PAD
    return pl.pallas_call(
        project_kernel,
        in_specs=[
            pl.BlockSpec(memory_space=pltpu.SMEM),
            pl.BlockSpec(memory_space=pltpu.VMEM),
            pl.BlockSpec(memory_space=pltpu.VMEM),
        ],
        out_shape=[
            jax.ShapeDtypeStruct((rows, slots, width), BF16),
            jax.ShapeDtypeStruct((rows, slots, 2 * width), BF16),
        ],
        compiler_params=pltpu.CompilerParams(vmem_limit_bytes=32 * 1024 * 1024),
        cost_estimate=pl.CostEstimate(
            flops=2 * rows * columns * (features + slots) * 3 * width,
            bytes_accessed=rows * columns * features * 2 + rows * slots * 3 * width * 2,
            transcendentals=0,
        ),
        name="project",
    )(spot, rows_tokens, weight)


def attend_kernel(
    spot_ref, north_ref, south_ref, query_ref, own_ref, weight_ref, mixed_ref, halo_ref, made_ref
):
    rows, slots, width = query_ref.shape
    columns = north_ref.shape[1]
    windows = slots // PAD
    split, shift, lat, last = spot_ref[0], spot_ref[1], spot_ref[2], spot_ref[3]

    matrix = joined(weight_ref, 0, weight_ref.shape[3])[:, width:]
    to_windows = roll_matrix(columns, shift, 1.0)
    for slot in range(rows):
        above = slot < rows - split
        north = north_ref[jnp.minimum(split - 1 + slot, HALO - 1)]
        south = south_ref[jnp.maximum(slot - (rows - split), 0)]
        values = jnp.where(above, north.astype(F32), south.astype(F32))
        projected = dot(layer_norm(values), matrix).astype(BF16)
        halo_ref[slot] = dot(to_windows, projected).astype(BF16)

    shape = (rows * PAD, 2 * rows * PAD)
    query = lax.broadcasted_iota(jnp.int32, shape, 0)
    key = lax.broadcasted_iota(jnp.int32, shape, 1)
    query_north = query // PAD < split
    is_halo = key >= rows * PAD
    key_row = jnp.where(is_halo, key - rows * PAD, key) // PAD
    key_north = key_row < jnp.where(is_halo, rows - split, split)
    beyond = jnp.where(is_halo, jnp.where(key_north, lat, last - lat), 1)
    same_band = query_north == key_north
    bias = jnp.where(same_band & (key % PAD < WW) & (beyond > 0), 0.0, -1e30)
    lane_head = lax.broadcasted_iota(jnp.int32, (rows * PAD, width), 1) // HEAD_DIM

    def window(m, carry):
        place = pl.ds(pl.multiple_of(m * PAD, PAD), PAD)
        queries = query_ref[:, place, :].reshape(rows * PAD, width)
        own = own_ref[:, place, :].reshape(rows * PAD, 2 * width)
        halo = halo_ref[:, place, :].reshape(rows * PAD, 2 * width)
        both = jnp.concatenate([own, halo], axis=0)
        zero = jnp.zeros_like(queries)
        stacked = jnp.concatenate(
            [jnp.where(lane_head == head, queries, zero) for head in range(HEADS)], axis=0
        )
        scores = dot_nt(stacked, both[:, :width]).reshape(HEADS, rows * PAD, -1) + bias[None]
        top = jnp.max(scores, axis=-1, keepdims=True)
        weights = jnp.exp(scores - top)
        total = jnp.sum(weights, axis=-1, keepdims=True)
        products = dot(weights.astype(BF16).reshape(HEADS * rows * PAD, -1), both[:, width:])
        products = products.reshape(HEADS, rows * PAD, width) / total
        mixed = products[0]
        for head in range(1, HEADS):
            mixed = jnp.where(lane_head == head, products[head], mixed)
        mixed = mixed.astype(BF16).reshape(rows, PAD, width)
        made_ref[:, pl.ds(pl.multiple_of((m + 1) * PAD, PAD), PAD), :] = mixed

        @pl.when(m == windows - 1)
        def _():
            made_ref[:, :PAD, :] = mixed

        return carry

    lax.fori_loop(0, windows, window, 0)

    def source(k):
        row, column = k // WW, k % WW
        inner = jnp.where(column < shift, column + WW - shift, PAD + column - shift)
        return row * (2 * PAD) + inner

    back = one_hot((rows * WW, rows * 2 * PAD), source)

    def tile(j, carry):
        pair = made_ref[:, pl.ds(pl.multiple_of(j * PAD, PAD), 2 * PAD), :]
        mixed_ref[j] = dot(back, pair.reshape(rows * 2 * PAD, width)).astype(BF16)
        return carry

    lax.fori_loop(0, windows, tile, 0)


def attend(spot, north, south, queries, own, weight):
    rows, slots, width = queries.shape
    windows = slots // PAD
    columns, features = north.shape[1:]
    vmem = pl.BlockSpec(memory_space=pltpu.VMEM)
    return pl.pallas_call(
        attend_kernel,
        in_specs=[pl.BlockSpec(memory_space=pltpu.SMEM)] + [vmem] * 5,
        out_shape=jax.ShapeDtypeStruct((windows, rows * WW, width), BF16),
        scratch_shapes=[
            pltpu.VMEM((rows, slots, 2 * width), BF16),
            pltpu.VMEM((rows, slots + PAD, width), BF16),
        ],
        compiler_params=pltpu.CompilerParams(vmem_limit_bytes=40 * 1024 * 1024),
        cost_estimate=pl.CostEstimate(
            flops=2 * rows * columns * (features + slots) * 2 * width
            + 4 * windows * HEADS * rows * PAD * 2 * rows * PAD * width,
            bytes_accessed=2 * north.size * 2 + rows * slots * 4 * width * 2,
            transcendentals=windows * HEADS * rows * PAD * 2 * rows * PAD,
        ),
        name="attend",
    )(spot, north, south, queries, own, weight)


def finish_kernel(tokens_ref, mixed_ref, out_weight_ref, shards_ref, encoded_ref, first_ref, second_ref):
    count, rows, columns, features = encoded_ref.shape
    half = features

    @pl.when(pl.program_id(0) == 0)
    def _():
        lines = 16
        first_ref[:, :half] = joined(shards_ref, 0, lines)
        first_ref[:, half:] = joined(shards_ref, lines, lines)
        second_ref[...] = joined(shards_ref, 2 * lines, 2 * lines)

    residual = tokens_ref[...].astype(F32) + dot(mixed_ref[...], out_weight_ref[...])
    inner = layer_norm(residual)
    expanded = jax.nn.gelu(dot(inner, first_ref[...]), approximate=True).astype(BF16)
    encoded = (residual + dot(expanded, second_ref[...])).astype(BF16)
    size = count * rows * columns

    def source(k):
        line, place = k // PAD, k % PAD
        return jnp.where(place < columns, line * columns + place, size)

    spread = one_hot((count * rows * PAD, size), source)
    padded = dot(spread, encoded).astype(BF16).reshape(count, rows, PAD, features)
    encoded_ref[...] = padded[:, :, :columns, :]


def finish(tokens, mixed, out_weight, shards):
    total, features = tokens.shape
    width = mixed.shape[1]
    times = total // (WH * WW)
    hidden = 2 * features
    block = GROUP * WH * WW
    return pl.pallas_call(
        finish_kernel,
        grid=(times // GROUP,),
        in_specs=[
            pl.BlockSpec((block, features), lambda g: (g, 0)),
            pl.BlockSpec((block, width), lambda g: (g, 0)),
            pl.BlockSpec(out_weight.shape, lambda g: (0, 0)),
            pl.BlockSpec(shards.shape, lambda g: (0,) * shards.ndim),
        ],
        out_specs=pl.BlockSpec((GROUP, WH, WW, features), lambda g: (g, 0, 0, 0)),
        out_shape=jax.ShapeDtypeStruct((times, WH, WW, features), BF16),
        scratch_shapes=[
            pltpu.VMEM((features, hidden), BF16),
            pltpu.VMEM((hidden, features), BF16),
        ],
        compiler_params=pltpu.CompilerParams(vmem_limit_bytes=40 * 1024 * 1024),
        cost_estimate=pl.CostEstimate(
            flops=2 * total * features * (width + 2 * hidden),
            bytes_accessed=total * (4 * features + 2 * width) + shards.size * 2,
            transcendentals=total * hidden,
        ),
        name="finish",
    )(tokens, mixed, out_weight, shards)


def copies(values, count):
    return jnp.broadcast_to(values[None], (count,) + values.shape)


def gather_far(shard):
    sizes = lax.axis_size("y_lo"), lax.axis_size("lat")
    found = lax.all_to_all(copies(shard, sizes[0] * sizes[1]), ("y_lo", "lat"), 0, 0, tiled=True)
    return found.reshape(sizes + shard.shape)


def gather_cores(shards):
    return lax.all_to_all(copies(shards, lax.axis_size("core")), "core", 0, 0, tiled=True)


def after(first, later):
    return lax.optimization_barrier((first, later))


def shards(
    fields,
    scale_exponent,
    level_mean,
    level_spread,
    row_offset,
    column_offset,
    patch_weight,
    attention_in,
    attention_out,
    hidden_in,
    hidden_out,
):
    features = patch_weight.shape[1]
    chans = fields.shape[3]
    lats = lax.axis_size("lat")
    lon = lax.axis_index(("y_hi", "x"))
    lat = lax.axis_index("lat")
    spot = jnp.stack(
        [
            lax.dynamic_index_in_dim(row_offset, lon, 0, False),
            lax.dynamic_index_in_dim(column_offset, lon, 0, False),
            lat,
            jnp.int32(lats - 1),
        ]
    )
    repeat = chans // level_mean.shape[0]
    affine = jnp.stack(
        [
            jnp.tile(jnp.exp2(scale_exponent.astype(F32)) / level_spread, repeat),
            jnp.tile(level_mean / level_spread, repeat),
        ]
    )

    patch_far = gather_far(patch_weight)
    patch_far, attention_in = after(patch_far, attention_in)
    patch_all = gather_cores(patch_far)
    project_far = gather_far(attention_in)
    patch_all, project_far = after(patch_all, project_far)
    project_all = gather_cores(project_far)

    rows_tokens, top, bottom, tiles = embed(fields[0], affine, patch_all)

    north = lax.ppermute(bottom, "lat", [(i, i + 1) for i in range(lats - 1)])
    south = lax.ppermute(top, "lat", [(i + 1, i) for i in range(lats - 1)])
    tiles = tiles.reshape((-1, WH * WW, features))
    tile_tokens = lax.all_to_all(tiles, ("y_hi", "x"), 0, 0, tiled=True)

    queries, own = project(spot, rows_tokens, project_all)

    half = hidden_in.shape[1] // 2
    packed = jnp.concatenate(
        [hidden_in[:, :half], hidden_in[:, half:], hidden_out, attention_out], axis=0
    )
    (north, south), packed = after((north, south), packed)
    hidden_far = gather_far(packed)
    mixed = attend(spot, north, south, queries, own, project_all)
    tile_mixed = lax.all_to_all(mixed, ("y_hi", "x"), 0, 0, tiled=True)

    hidden_all = gather_cores(hidden_far)
    out_rows = attention_out.shape[0]
    out_weight = hidden_all[:, :, :, -out_rows:, :].swapaxes(0, 1).reshape(-1, features)
    hidden_all = hidden_all[:, :, :, :-out_rows, :]
    return finish(
        tile_tokens.reshape(-1, features),
        tile_mixed.reshape(-1, tile_mixed.shape[-1]),
        out_weight,
        hidden_all,
    )


def solution(mesh):
    tm, lat, lon = (mesh.shape[name] for name in ("tm", "lat", "lon"))
    cores, across = 2, 4
    finer = Mesh(
        mesh.devices.reshape(tm // cores, cores, lat, lon // across, across),
        ("y_lo", "core", "lat", "y_hi", "x"),
    )
    time = ("y_lo", "core")
    in_specs = (
        P(time + ("y_hi", "x"), "lat", None, None),
        P(),
        P(),
        P(),
        P(time),
        P(time),
        P(time + ("lat",), None),
        P(time + ("lat",), None),
        P(time + ("lat",), None),
        P(time + ("lat",), None),
        P(time + ("lat",), None),
    )
    out_specs = P(time, "lat", ("y_hi", "x"), None)
    return jax.shard_map(shards, mesh=finer, in_specs=in_specs, out_specs=out_specs, check_vma=False)
```

time: 550 us -> 215 us (0.39)
  the two profiles are of different devices: /device:TPU:1 before, /device:TPU:8 now
where the time goes in v1:
time: 215 us
  blocking collectives  103 us (48%)
  waiting for transfers between devices  56.3 us (26%)
  Pallas kernels  27.1 us (13%)
  starting transfers between devices  16.5 us (8%)
  local copies, waits for them, and re-layouts  10 us (5%)
    all_to_all x2, blocking collectives, gather_far(): lax.all_to_all(copies(shard, sizes[0] * sizes[1]), ('y_lo', 'lat'), 0, 0,...  62 us
    all_to_all x1, waiting for transfers between devices, shards(): tile_tokens = lax.all_to_all(tiles, ('y_hi', 'x'), 0, 0, tiled=True)  32 us
    all_to_all x1, blocking collectives, shards(): tile_mixed = lax.all_to_all(mixed, ('y_hi', 'x'), 0, 0, tiled=True)  26.5 us
    all_to_all x3, blocking collectives, gather_cores(): lax.all_to_all(copies(shards, lax.axis_size('core')), 'core', 0, 0, tiled...  14.7 us
    pallas_call x1, Pallas kernels, attend(): pl.pallas_call(attend_kernel, in_specs=[pl.BlockSpec(memory_space=pltpu.S...  12.9 us
    all_to_all x1, waiting for transfers between devices, gather_far(): lax.all_to_all(copies(shard, sizes[0] * sizes[1]), ('y_lo', 'lat'), 0, 0,...  11.6 us
    ppermute x1, waiting for transfers between devices, shards(): north = lax.ppermute(bottom, 'lat', [(i, i + 1) for i in range(lats - 1)])  8.61 us
    pallas_call x1, Pallas kernels, finish(): pl.pallas_call(finish_kernel, grid=(times // GROUP,), in_specs=[pl.BlockS...  6.57 us
  transfers between devices with their start and end apart: 4, of which 4 were waited for; matrix products, arithmetic and copies ran while one was open for 3% of the time, Pallas kernels for 1%

profile of v1, /device:TPU:8, one launch (start us, length us, event | category | flops | bytes accessed | tf_op | source)
XLA Modules:
  0.0 214.7 jit_solution(17116709052970107933)
XLA Ops:
  0.8 26.3 %all_to_all.40 = bf16[16,32,512]{2,1,0:T(8,128)(2,1)S(1)} all-to-all(bf16[16,32,512]{2,1,0:T(8,128)(2,1)S(1)} %broadcast_in_dim.14), channel_id=1, replica_groups=mesh['y_lo'=2,'core'=2,'lat'=8,'y_hi'=4,'x'=4] {'y_lo','lat'}, dimensions={0} | all-to-all | bytes 1048576 | tf_op jit(solution)/shard_map/all_to_all | solution.py:328
  27.3 4.7 %all_to_all.41.weight_ref = bf16[2,2,8,32,512]{4,3,2,1,0:T(8,128)(2,1)S(1)} all-to-all(bf16[2,2,8,32,512]{4,3,2,1,0:T(8,128)(2,1)S(1)} %broadcast_in_dim.15), channel_id=1, replica_groups=mesh['y_lo'=2,'core'=2,'lat'=8,'y_hi'=4,'x'=4] {'core'}, dimensions={0} | all-to-all | bytes 2097152 | tf_op jit(solution)/shard_map/all_to_all | solution.py:333
  32.8 5.8 %all-to-all-start.2 = ((bf16[16,16,768]{2,1,0:T(8,128)(2,1)}), bf16[16,16,768]{2,1,0:T(8,128)(2,1)}, u32[]{:S(2)}, u32[]{:S(2)}) async-start(bf16[16,16,768]{2,1,0:T(8,128)(2,1)} %broadcast_in_dim.16), calls=%async_computation.2 | async-start | bytes 786432 | tf_op jit(solution)/shard_map/all_to_all | solution.py:328
  38.9 11.6 %all-to-all-done.2 = bf16[16,16,768]{2,1,0:T(8,128)(2,1)} async-done(((bf16[16,16,768]{2,1,0:T(8,128)(2,1)}), bf16[16,16,768]{2,1,0:T(8,128)(2,1)}, u32[]{:S(2)}, u32[]{:S(2)}) %all-to-all-start.2) | async-done | bytes 393248 | tf_op jit(solution)/shard_map/all_to_all | solution.py:328
  50.5 4.5 %embed.1 = (bf16[6,192,512]{2,1,0:T(8,128)(2,1)S(1)}, bf16[5,192,512]{2,1,0:T(8,128)(2,1)}, bf16[5,192,512]{2,1,0:T(8,128)(2,1)}, bf16[1152,512]{1,0:T(8,128)(2,1)}) custom-call(bf16[24,192,256]{2,1,0:T(8,128)(2,1)S(1)} %bitcast.14, f32[2,256]{1,0:T(2,128)S(1)} %pad_maximum_fusion.1.affine_ref, bf16[2,2,8,32,512]{4,3,2,1,0:T(8,128)(2,1)S(1)} %all_to_all.41.weight_ref), custom_call_target="tpu_custom_call" | custom-call | flops 1207959552 | bytes 8126464 | tf_op jit(solution)/shard_map/embed/pallas_call | solution.py:86
  55.0 1.0 copy-done.2
  56.0 4.9 %collective-permute-start = (bf16[5,192,512]{2,1,0:T(8,128)(2,1)}, bf16[5,192,512]{2,1,0:T(8,128)(2,1)S(1)}, u32[]{:S(2)}, u32[]{:S(2)}) collective-permute-start(bf16[5,192,512]{2,1,0:T(8,128)(2,1)} %get-tuple-element.22), channel_id=1, source_target_pairs={{0,16},{16,32},{32,48},{48,64},{64,80},{80,96},{96,112},{1,17},{17... | collective-permute-start | bytes 2949128 | tf_op jit(solution)/shard_map/ppermute | solution.py:383
  60.9 1.3 collective-permute-start.1
  63.4 1.3 pad_add_fusion.spot_ref
  64.8 1.1 broadcast_in_dim.17
  65.9 4.4 %all_to_all.42.weight_ref = bf16[2,2,8,16,768]{4,3,2,1,0:T(8,128)(2,1)S(1)} all-to-all(bf16[2,2,8,16,768]{4,3,2,1,0:T(8,128)(2,1)S(1)} %broadcast_in_dim.17), channel_id=1, replica_groups=mesh['y_lo'=2,'core'=2,'lat'=8,'y_hi'=4,'x'=4] {'core'}, dimensions={0} | all-to-all | bytes 1572864 | tf_op jit(solution)/shard_map/all_to_all | solution.py:333
  70.2 3.1 %project.1 = (bf16[6,256,256]{2,1,0:T(8,128)(2,1)S(1)}, bf16[6,256,512]{2,1,0:T(8,128)(2,1)S(1)}) custom-call(s32[4]{0:T(128)S(1)} %pad_add_fusion.spot_ref, bf16[6,192,512]{2,1,0:T(8,128)(2,1)S(1)} %copy-done.3, bf16[2,2,8,16,768]{4,3,2,1,0:T(8,128)(2,1)S(1)} %all_to_all.42.weight_ref), custom_call_target="tpu_custom_call" | custom-call | flops 1358954496 | bytes 3538944 | tf_op jit(solution)/shard_map/project/pallas_call | solution.py:145
  73.3 8.6 %collective-permute-done.north_ref = bf16[5,192,512]{2,1,0:T(8,128)(2,1)S(1)} collective-permute-done((bf16[5,192,512]{2,1,0:T(8,128)(2,1)}, bf16[5,192,512]{2,1,0:T(8,128)(2,1)S(1)}, u32[]{:S(2)}, u32[]{:S(2)}) %collective-permute-start) | collective-permute-done | bytes 983072 | tf_op jit(solution)/shard_map/ppermute | solution.py:383
  82.0 4.1 %collective-permute-done.1.south_ref = bf16[5,192,512]{2,1,0:T(8,128)(2,1)S(1)} collective-permute-done((bf16[5,192,512]{2,1,0:T(8,128)(2,1)}, bf16[5,192,512]{2,1,0:T(8,128)(2,1)S(1)}, u32[]{:S(2)}, u32[]{:S(2)}) %collective-permute-start.1) | collective-permute-done | bytes 983072 | tf_op jit(solution)/shard_map/ppermute | solution.py:384
  86.0 12.9 %attend.1 = bf16[16,72,256]{2,1,0:T(8,128)(2,1)S(1)} custom-call(s32[4]{0:T(128)S(1)} %pad_add_fusion.spot_ref, bf16[5,192,512]{2,1,0:T(8,128)(2,1)S(1)} %collective-permute-done.north_ref, bf16[5,192,512]{2,1,0:T(8,128)(2,1)S(1)} %collective-permute-done.1.south_ref, bf16[6,256,256]{2,1,0:T(8,128)(2,1)S(1)} %get-tuple-element.28.query_ref, ...), custom_call_target="tpu_custom_call" | custom-call | flops 2113929216 | bytes 5111808 | tf_op jit(solution)/shard_map/attend/pallas_call | solution.py:246
  99.0 26.5 %all_to_all.43 = bf16[16,72,256]{2,1,0:T(8,128)(2,1)} all-to-all(bf16[16,72,256]{2,1,0:T(8,128)(2,1)S(1)} %attend.1), channel_id=1, replica_groups=mesh['y_lo'=2,'core'=2,'lat'=8,'y_hi'=4,'x'=4] {'y_hi','x'}, dimensions={0} | all-to-all | bytes 1179648 | tf_op jit(solution)/shard_map/all_to_all | solution.py:397
  125.5 35.7 %all_to_all.44 = bf16[16,72,512]{2,1,0:T(8,128)(2,1)S(1)} all-to-all(bf16[16,72,512]{2,1,0:T(8,128)(2,1)S(1)} %broadcast_in_dim.18), channel_id=1, replica_groups=mesh['y_lo'=2,'core'=2,'lat'=8,'y_hi'=4,'x'=4] {'y_lo','lat'}, dimensions={0} | all-to-all | bytes 2359296 | tf_op jit(solution)/shard_map/all_to_all | solution.py:328
  161.4 5.6 %all_to_all.45 = bf16[2,2,8,72,512]{4,3,2,1,0:T(8,128)(2,1)S(1)} all-to-all(bf16[2,2,8,72,512]{4,3,2,1,0:T(8,128)(2,1)S(1)} %broadcast_in_dim.20), channel_id=1, replica_groups=mesh['y_lo'=2,'core'=2,'lat'=8,'y_hi'=4,'x'=4] {'core'}, dimensions={0} | all-to-all | bytes 4718592 | tf_op jit(solution)/shard_map/all_to_all | solution.py:333
  167.0 4.4 %all-to-all-start.3 = ((bf16[16,72,512]{2,1,0:T(8,128)(2,1)}), bf16[16,72,512]{2,1,0:T(8,128)(2,1)S(1)}, u32[]{:S(2)}, u32[]{:S(2)}) async-start(bf16[16,72,512]{2,1,0:T(8,128)(2,1)} %bitcast.3), calls=%async_computation.3 | async-start | bytes 2359296 | tf_op jit(solution)/shard_map/all_to_all | solution.py:386
  171.6 1.8 slice.17.shards_ref
  173.3 32.0 %all-to-all-done.3 = bf16[16,72,512]{2,1,0:T(8,128)(2,1)S(1)} async-done(((bf16[16,72,512]{2,1,0:T(8,128)(2,1)}), bf16[16,72,512]{2,1,0:T(8,128)(2,1)S(1)}, u32[]{:S(2)}, u32[]{:S(2)}) %all-to-all-start.3) | async-done | bytes 1179680 | tf_op jit(solution)/shard_map/all_to_all | solution.py:386
  205.3 1.1 copy-done
  206.4 6.6 %finish.1 = bf16[16,6,12,512]{3,2,1,0:T(8,128)(2,1)S(1)} custom-call(bf16[1152,512]{1,0:T(8,128)(2,1)S(1)} %bitcast.11, bf16[1152,256]{1,0:T(8,128)(2,1)S(1)} %bitcast.12, bf16[256,512]{1,0:T(8,128)(2,1)S(1)} %bitcast.13, bf16[2,2,8,64,512]{4,3,2,1,0:T(8,128)(2,1)S(1)} %slice.17.shards_ref), custom_call_target="tpu_custom_call" | custom-call | flops 2717908992 | bytes 5046272 | tf_op jit(solution)/shard_map/finish/pallas_call | solution.py:297
  213.0 1.7 copy.14
  (43 shorter events, 3.5 us)
Async XLA Ops:
  27.1 4.9 %copy-start.7 = (bf16[16,768]{1,0:T(8,128)(2,1)S(1)}, bf16[16,768]{1,0:T(8,128)(2,1)}, u32[]{:S(2)}) copy-start(bf16[16,768]{1,0:T(8,128)(2,1)} %param.18) | copy-start | bytes 73732
  27.3 11.3 %copy-start.9 = (f32[64]{0:T(128)S(1)}, f32[64]{0:T(128)}, u32[]{:S(2)}) copy-start(f32[64]{0:T(128)} %param.14) | copy-start | bytes 772
  27.3 11.3 %copy-start.10 = (s32[64]{0:T(128)S(1)}, s32[64]{0:T(128)}, u32[]{:S(2)}) copy-start(s32[64]{0:T(128)} %param.12) | copy-start | bytes 772
  27.3 11.3 %copy-start.11 = (f32[64]{0:T(128)S(1)}, f32[64]{0:T(128)}, u32[]{:S(2)}) copy-start(f32[64]{0:T(128)} %param.13) | copy-start | bytes 772
  27.3 23.1 %copy-start.1 = (bf16[1,24,192,256]{3,2,1,0:T(8,128)(2,1)S(1)}, bf16[1,24,192,256]{3,2,1,0:T(8,128)(2,1)}, u32[]{:S(2)}) copy-start(bf16[1,24,192,256]{3,2,1,0:T(8,128)(2,1)} %param.11) | copy-start | bytes 7077892
  32.8 17.6 %all-to-all-start.2 = ((bf16[16,16,768]{2,1,0:T(8,128)(2,1)}), bf16[16,16,768]{2,1,0:T(8,128)(2,1)}, u32[]{:S(2)}, u32[]{:S(2)}) async-start(bf16[16,16,768]{2,1,0:T(8,128)(2,1)} %broadcast_in_dim.16), calls=%async_computation.2 | async-start | bytes 786432 | tf_op jit(solution)/shard_map/all_to_all | solution.py:328
  50.4 11.8 %copy-start.12 = (s32[16]{0:T(128)S(1)}, s32[16]{0:T(128)}, u32[]{:S(2)}) copy-start(s32[16]{0:T(128)} %param.15) | copy-start | bytes 196
  50.4 12.4 %copy-start.13 = (s32[16]{0:T(128)S(1)}, s32[16]{0:T(128)}, u32[]{:S(2)}) copy-start(s32[16]{0:T(128)} %param.16) | copy-start | bytes 196
  50.4 14.3 %copy-start.5 = (bf16[16,1024]{1,0:T(8,128)(2,1)S(1)}, bf16[16,1024]{1,0:T(8,128)(2,1)}, u32[]{:S(2)}) copy-start(bf16[16,1024]{1,0:T(8,128)(2,1)} %param.20) | copy-start | bytes 98308
  50.4 14.3 %copy-start.6 = (bf16[32,512]{1,0:T(8,128)(2,1)S(1)}, bf16[32,512]{1,0:T(8,128)(2,1)}, u32[]{:S(2)}) copy-start(bf16[32,512]{1,0:T(8,128)(2,1)} %param.21) | copy-start | bytes 98308
  50.4 14.3 %copy-start.8 = (bf16[8,512]{1,0:T(8,128)(2,1)S(1)}, bf16[8,512]{1,0:T(8,128)(2,1)}, u32[]{:S(2)}) copy-start(bf16[8,512]{1,0:T(8,128)(2,1)} %param.19) | copy-start | bytes 24580
  55.0 1.0 copy-start.2
  56.0 14.2 %copy-start.3 = (bf16[6,192,512]{2,1,0:T(8,128)(2,1)S(1)}, bf16[6,192,512]{2,1,0:T(8,128)(2,1)}, u32[]{:S(2)}) copy-start(bf16[6,192,512]{2,1,0:T(8,128)(2,1)} %copy-done.2) | copy-start | bytes 3538948
  56.0 26.0 %collective-permute-start = (bf16[5,192,512]{2,1,0:T(8,128)(2,1)}, bf16[5,192,512]{2,1,0:T(8,128)(2,1)S(1)}, u32[]{:S(2)}, u32[]{:S(2)}) collective-permute-start(bf16[5,192,512]{2,1,0:T(8,128)(2,1)} %get-tuple-element.22), channel_id=1, source_target_pairs={{0,16},{16,32},{32,48},{48,64},{64,80},{80,96},{96,112},{1,17},{17... | collective-permute-start | bytes 2949128 | tf_op jit(solution)/shard_map/ppermute | solution.py:383
  60.9 25.1 %collective-permute-start.1 = (bf16[5,192,512]{2,1,0:T(8,128)(2,1)}, bf16[5,192,512]{2,1,0:T(8,128)(2,1)S(1)}, u32[]{:S(2)}, u32[]{:S(2)}) collective-permute-start(bf16[5,192,512]{2,1,0:T(8,128)(2,1)} %get-tuple-element.23), channel_id=1, source_target_pairs={{16,0},{32,16},{48,32},{64,48},{80,64},{96,80},{112,96},{17,1},{33... | collective-permute-start | bytes 2949128 | tf_op jit(solution)/shard_map/ppermute | solution.py:384
  167.0 4.5 %copy-start.4 = (bf16[2,2,8,72,512]{4,3,2,1,0:T(8,128)(2,1)}, bf16[2,2,8,72,512]{4,3,2,1,0:T(8,128)(2,1)S(1)}, u32[]{:S(2)}) copy-start(bf16[2,2,8,72,512]{4,3,2,1,0:T(8,128)(2,1)S(1)} %all_to_all.45) | copy-start | bytes 7077892
  167.0 38.3 %all-to-all-start.3 = ((bf16[16,72,512]{2,1,0:T(8,128)(2,1)}), bf16[16,72,512]{2,1,0:T(8,128)(2,1)S(1)}, u32[]{:S(2)}, u32[]{:S(2)}) async-start(bf16[16,72,512]{2,1,0:T(8,128)(2,1)} %bitcast.3), calls=%async_computation.3 | async-start | bytes 2359296 | tf_op jit(solution)/shard_map/all_to_all | solution.py:386
  205.3 1.1 copy-start

commit v2 on v1

v2 whole, which is shorter than its diff:
```python
import functools

import jax
import jax.numpy as jnp
from jax import lax
from jax.experimental import pallas as pl
from jax.experimental.pallas import tpu as pltpu
from jax.sharding import Mesh
from jax.sharding import PartitionSpec as P

P_SIZE = 4
HEAD_DIM = 64
HEADS = 4
WH = 6
WW = 12
PAD = 16
HALO = WH - 1
BAND = 8
EPSILON = 1e-05
BF16 = jnp.bfloat16
F32 = jnp.float32
GROUP = 4
ATTEND_COST = 1
EMBED_COST = 2 * 10**10
CHOOSE_COST = 3 * 10**10
LINES = 16


def dot(a, b):
    return jnp.dot(a, b, preferred_element_type=F32)


def dot_nt(a, b):
    return lax.dot_general(a, b, (((1,), (1,)), ((), ())), preferred_element_type=F32)


def one_hot(shape, column_of_row):
    row = lax.broadcasted_iota(jnp.int32, shape, 0)
    column = lax.broadcasted_iota(jnp.int32, shape, 1)
    return (column == column_of_row(row)).astype(F32).astype(BF16)


def layer_norm(values):
    center = values - jnp.mean(values, axis=-1, keepdims=True)
    spread = jnp.mean(center * center, axis=-1, keepdims=True)
    return (center * lax.rsqrt(spread + EPSILON)).astype(BF16)


def position():
    lon = lax.axis_index("y_hi") * lax.axis_size("x") + lax.axis_index("x")
    return {
        "core": lax.axis_index("core"),
        "y_lo": lax.axis_index("y_lo"),
        "lat": lax.axis_index("lat"),
        "last": lax.axis_size("lat") - 1,
        "lon": lon,
    }


def place(core_swapped, y_swapped):
    here = position()
    core, y = here["core"], here["y_lo"]
    core = 1 - core if core_swapped else core
    y = 1 - y if y_swapped else y
    return y * 2 + core


def collect(shards, target_ref, columns=slice(None)):
    for spot, block in shards:
        block = block.reshape(-1, block.shape[-1])
        start = pl.multiple_of(spot * block.shape[0], block.shape[0])
        target_ref[pl.ds(start, block.shape[0]), columns] = block


def parts(refs, first, count, half):
    return [
        (place(swapped, y), ref[:, y * half + first : y * half + first + count])
        for swapped, ref in enumerate(refs)
        for y in range(2)
    ]


def pack_kernel(hidden_in_ref, hidden_out_ref, attention_out_ref, attention_in_ref, packed_ref):
    lines, features = LINES, packed_ref.shape[1]
    short = lines // 2
    width = attention_in_ref.shape[1] // 3
    packed_ref[:lines] = hidden_in_ref[:, :features]
    packed_ref[lines : 2 * lines] = hidden_in_ref[:, features:]
    packed_ref[2 * lines : 4 * lines] = hidden_out_ref[...]
    packed_ref[4 * lines : 5 * lines] = attention_in_ref[:, width:]
    query = attention_in_ref[:, :width].astype(F32)
    query = jnp.concatenate([query[:short], query[short:]], axis=1)
    out = attention_out_ref[...].astype(F32)
    packed_ref[5 * lines :] = jnp.concatenate([out, query], axis=0).astype(BF16)


def pack(hidden_in, hidden_out, attention_out, attention_in):
    return pl.pallas_call(
        pack_kernel,
        in_specs=[pl.BlockSpec(memory_space=pltpu.VMEM)] * 4,
        out_shape=jax.ShapeDtypeStruct((6 * LINES, hidden_out.shape[1]), BF16),
        name="pack",
    )(hidden_in, hidden_out, attention_out, attention_in)


def join_kernel(own_ref, swapped_ref, joined_ref):
    far = 4 * LINES
    near = own_ref.shape[0] - far
    joined_ref[:far] = own_ref[:far]
    joined_ref[far : 2 * far] = swapped_ref[:far]
    joined_ref[2 * far : 2 * far + near] = own_ref[far:]
    joined_ref[2 * far + near :] = swapped_ref[far:]


def join(own, swapped):
    return pl.pallas_call(
        join_kernel,
        in_specs=[pl.BlockSpec(memory_space=pltpu.VMEM)] * 2,
        out_shape=jax.ShapeDtypeStruct((2 * own.shape[0], own.shape[1]), BF16),
        name="join",
    )(own, swapped)


def normalize_kernel(fields_ref, affine_ref, normalized_ref):
    factor = affine_ref[0:1, :]
    shift = affine_ref[1:2, :]
    normalized_ref[...] = (fields_ref[...].astype(F32) * factor - shift).astype(BF16)


def normalize(fields, affine):
    pixel_rows, columns, chans = fields.shape
    return pl.pallas_call(
        normalize_kernel,
        grid=(pixel_rows // P_SIZE,),
        in_specs=[
            pl.BlockSpec((P_SIZE, columns, chans), lambda g: (g, 0, 0)),
            pl.BlockSpec(affine.shape, lambda g: (0, 0)),
        ],
        out_specs=pl.BlockSpec((P_SIZE, columns, chans), lambda g: (g, 0, 0)),
        out_shape=jax.ShapeDtypeStruct(fields.shape, BF16),
        compiler_params=pltpu.CompilerParams(vmem_limit_bytes=12 * 1024 * 1024),
        name="normalize",
    )(fields, affine)


def embed_kernel(
    fields_ref,
    weight_ref,
    other_ref,
    rows_ref,
    top_ref,
    bottom_ref,
    tiles_ref,
    table_ref,
):
    rows = rows_ref.shape[0]

    @pl.when(pl.program_id(0) == 0)
    def _():
        for swapped, ref in enumerate((weight_ref, other_ref)):
            for y in range(ref.shape[0]):
                core = place(swapped, 0) % 2
                table_ref[2 * y + core] = ref[y].reshape(table_ref.shape[1:])

    columns = fields_ref.shape[1]
    chans = fields_ref.shape[2]
    normalized = fields_ref[...].reshape(rows, P_SIZE, columns, chans)
    total = None
    for pixel in range(P_SIZE):
        product = dot(normalized[:, pixel].reshape(rows * columns, chans), table_ref[pixel])
        total = product if total is None else total + product
    tokens = total.astype(BF16)
    by_row = tokens.reshape(rows, columns, -1)
    rows_ref[...] = by_row
    top_ref[...] = by_row[:HALO]
    bottom_ref[...] = by_row[rows - HALO :]

    def source(k):
        tile, inner = k // (rows * WW), k % (rows * WW)
        return (inner // WW) * columns + tile * WW + inner % WW

    order = one_hot((rows * columns, rows * columns), source)
    tiles_ref[...] = dot(order, tokens).astype(BF16)


def embed(fields, weight, other):
    pixel_rows, columns, chans = fields.shape
    rows = pixel_rows // P_SIZE
    width = weight.shape[-1]
    step = GROUP * WW
    return pl.pallas_call(
        embed_kernel,
        grid=(columns // step,),
        in_specs=[
            pl.BlockSpec((pixel_rows, step, chans), lambda g: (0, g, 0)),
            pl.BlockSpec(weight.shape, lambda g: (0,) * weight.ndim),
            pl.BlockSpec(weight.shape, lambda g: (0,) * weight.ndim),
        ],
        out_specs=[
            pl.BlockSpec((rows, step, width), lambda g: (0, g, 0)),
            pl.BlockSpec((HALO, step, width), lambda g: (0, g, 0)),
            pl.BlockSpec((HALO, step, width), lambda g: (0, g, 0)),
            pl.BlockSpec((rows * step, width), lambda g: (g, 0)),
        ],
        out_shape=[
            jax.ShapeDtypeStruct((rows, columns, width), BF16),
            jax.ShapeDtypeStruct((HALO, columns, width), BF16),
            jax.ShapeDtypeStruct((HALO, columns, width), BF16),
            jax.ShapeDtypeStruct((rows * columns, width), BF16),
        ],
        scratch_shapes=[pltpu.VMEM((P_SIZE, chans, width), BF16)],
        compiler_params=pltpu.CompilerParams(vmem_limit_bytes=16 * 1024 * 1024),
        cost_estimate=pl.CostEstimate(
            flops=EMBED_COST,
            bytes_accessed=0,
            transcendentals=0,
        ),
        name="embed",
    )(fields, weight, other)


def roll_matrix(columns, shift, scale):
    slots = columns // WW * PAD
    row = lax.broadcasted_iota(jnp.int32, (slots, columns), 0)
    column = lax.broadcasted_iota(jnp.int32, (slots, columns), 1)
    place = row % PAD
    want = (row // PAD) * WW + place + shift
    want = jnp.where(want >= columns, want - columns, want)
    hit = (want == column) & (place < WW)
    return jnp.where(hit, scale, 0.0).astype(BF16)


def project_kernel(
    column_offset_ref,
    rows_ref,
    weight_ref,
    other_ref,
    query_ref,
    key_value_ref,
    matrix_ref,
    query_matrix_ref,
):
    rows, columns, features = rows_ref.shape
    width = query_ref.shape[-1]
    shift = column_offset_ref[position()["lon"]]
    refs = weight_ref, other_ref
    collect(parts(refs, 0, LINES, 2 * LINES), matrix_ref)
    for spot, block in parts(refs, LINES, LINES, 2 * LINES):
        block = block.astype(F32)[:, LINES // 2 :]
        block = jnp.concatenate([block[..., :width], block[..., width:]], axis=1)
        collect([(spot, block.reshape(-1, width).astype(BF16))], query_matrix_ref)
    matrix = jnp.concatenate([query_matrix_ref[...], matrix_ref[...]], axis=1)
    to_windows = roll_matrix(columns, shift, 1.0)
    to_queries = roll_matrix(columns, shift, HEAD_DIM**-0.5)
    for row in range(rows):
        normed = layer_norm(rows_ref[row].astype(F32))
        projected = dot(normed, matrix).astype(BF16)
        query_ref[row] = dot(to_queries, projected[:, :width]).astype(BF16)
        key_value_ref[row] = dot(to_windows, projected[:, width:]).astype(BF16)


def project(column_offset, rows_tokens, weights):
    rows, columns, features = rows_tokens.shape
    width = HEADS * HEAD_DIM
    slots = columns // WW * PAD
    return pl.pallas_call(
        project_kernel,
        in_specs=[pl.BlockSpec(memory_space=pltpu.SMEM)]
        + [pl.BlockSpec(memory_space=pltpu.VMEM)] * 3,
        out_shape=[
            jax.ShapeDtypeStruct((rows, slots, width), BF16),
            jax.ShapeDtypeStruct((rows, slots, 2 * width), BF16),
            jax.ShapeDtypeStruct((features, 2 * width), BF16),
        ],
        scratch_shapes=[pltpu.VMEM((features, width), BF16)],
        compiler_params=pltpu.CompilerParams(vmem_limit_bytes=20 * 1024 * 1024),
        cost_estimate=pl.CostEstimate(
            flops=2 * rows * columns * (features + slots) * 3 * width,
            bytes_accessed=rows * columns * features * 2 + rows * slots * 3 * width * 2,
            transcendentals=0,
        ),
        name="project",
    )(column_offset, rows_tokens, *weights)


def choose_kernel(row_offset_ref, north_ref, south_ref, normed_ref):
    rows = normed_ref.shape[0]
    split = row_offset_ref[position()["lon"]]
    for slot in range(rows):
        north = north_ref[jnp.minimum(split - 1 + slot, HALO - 1)]
        south = south_ref[jnp.maximum(slot - (rows - split), 0)]
        values = jnp.where(slot < rows - split, north.astype(F32), south.astype(F32))
        normed_ref[slot] = layer_norm(values)


def choose(row_offset, north, south):
    columns, features = north.shape[1:]
    vmem = pl.BlockSpec(memory_space=pltpu.VMEM)
    return pl.pallas_call(
        choose_kernel,
        in_specs=[pl.BlockSpec(memory_space=pltpu.SMEM), vmem, vmem],
        out_shape=jax.ShapeDtypeStruct((WH, columns, features), BF16),
        compiler_params=pltpu.CompilerParams(vmem_limit_bytes=8 * 1024 * 1024),
        cost_estimate=pl.CostEstimate(flops=CHOOSE_COST, bytes_accessed=0, transcendentals=0),
        name="choose",
    )(row_offset, north, south)


def attend_kernel(
    row_offset_ref,
    column_offset_ref,
    normed_ref,
    query_ref,
    own_ref,
    matrix_ref,
    mixed_ref,
    keys_ref,
    made_ref,
):
    rows, slots, width = query_ref.shape
    columns = normed_ref.shape[1]
    windows = slots // PAD
    here = position()
    lat, last = here["lat"], here["last"]
    split, shift = row_offset_ref[here["lon"]], column_offset_ref[here["lon"]]
    half = keys_ref.shape[0] // 2
    for band in range(2):
        for slot in range(rows, half):
            keys_ref[band * half + slot] = jnp.zeros(keys_ref.shape[1:], BF16)
    for row in range(rows):
        spot = jnp.where(row < split, row + rows - split, half + row - split)
        keys_ref[spot] = own_ref[row]

    matrix = matrix_ref[...]
    to_windows = roll_matrix(columns, shift, 1.0)
    for slot in range(rows):
        projected = dot(normed_ref[slot], matrix).astype(BF16)
        spot = jnp.where(slot < rows - split, slot, half + slot)
        keys_ref[spot] = dot(to_windows, projected).astype(BF16)

    shape = (rows, PAD, half * PAD)
    north_query = lax.broadcasted_iota(jnp.int32, shape, 0) < split
    key = lax.broadcasted_iota(jnp.int32, shape, 2)
    key_row = key // PAD
    from_north = key_row < rows - split
    beyond = jnp.where(
        north_query, jnp.where(from_north, lat, 1), jnp.where(from_north, 1, last - lat)
    )
    bias = jnp.where((key_row < rows) & (key % PAD < WW) & (beyond > 0), 0.0, -1e30)
    lane_head = lax.broadcasted_iota(jnp.int32, (rows * PAD, width), 1) // HEAD_DIM

    def window(m):
        here = pl.ds(pl.multiple_of(m * PAD, PAD), PAD)
        queries = query_ref[:, here, :].reshape(rows * PAD, width)
        keys = keys_ref[:, here, :].reshape(2 * half * PAD, 2 * width)
        zero = jnp.zeros_like(queries)
        stacked = jnp.concatenate(
            [jnp.where(lane_head == head, queries, zero) for head in range(HEADS)], axis=0
        )
        scores = dot_nt(stacked, keys[:, :width]).reshape(HEADS, rows, PAD, 2 * half * PAD)
        scores = jnp.where(north_query[None], scores[..., : half * PAD], scores[..., half * PAD :])
        scores = scores + bias[None]
        weights = jnp.exp(scores - jnp.max(scores, axis=-1, keepdims=True))
        weights = weights * (1.0 / jnp.sum(weights, axis=-1, keepdims=True))
        weights = jnp.concatenate(
            [jnp.where(north_query[None], weights, 0.0), jnp.where(north_query[None], 0.0, weights)],
            axis=-1,
        ).astype(BF16)
        products = dot(weights.reshape(HEADS * rows * PAD, -1), keys[:, width:])
        products = products.reshape(HEADS, rows * PAD, width)
        mixed = products[0]
        for head in range(1, HEADS):
            mixed = jnp.where(lane_head == head, products[head], mixed)
        mixed = mixed.astype(BF16).reshape(rows, PAD, width)
        made_ref[:, pl.ds(pl.multiple_of((m + 1) * PAD, PAD), PAD), :] = mixed

    def some_windows(step, carry):
        for inner in range(GROUP):
            window(step * GROUP + inner)
        return carry

    lax.fori_loop(0, windows // GROUP, some_windows, 0)
    made_ref[:, :PAD, :] = made_ref[:, windows * PAD :, :]

    def source(k):
        row, column = k // WW, k % WW
        inner = jnp.where(column < shift, column + WW - shift, PAD + column - shift)
        return row * (2 * PAD) + inner

    back = one_hot((rows * WW, rows * 2 * PAD), source)
    for j in range(windows):
        pair = made_ref[:, j * PAD : (j + 2) * PAD, :]
        mixed_ref[j] = dot(back, pair.reshape(rows * 2 * PAD, width)).astype(BF16)


def attend(row_offset, column_offset, normed, queries, own, matrix):
    rows, slots, width = queries.shape
    windows = slots // PAD
    columns, features = normed.shape[1:]
    vmem = pl.BlockSpec(memory_space=pltpu.VMEM)
    return pl.pallas_call(
        attend_kernel,
        in_specs=[pl.BlockSpec(memory_space=pltpu.SMEM)] * 2 + [vmem] * 4,
        out_shape=jax.ShapeDtypeStruct((windows, rows * WW, width), BF16),
        scratch_shapes=[
            pltpu.VMEM((2 * BAND, slots, 2 * width), BF16),
            pltpu.VMEM((rows, slots + PAD, width), BF16),
        ],
        compiler_params=pltpu.CompilerParams(vmem_limit_bytes=24 * 1024 * 1024),
        cost_estimate=pl.CostEstimate(
            flops=ATTEND_COST * 2 * rows * columns * (features + slots) * 2 * width
            + ATTEND_COST * 4 * windows * HEADS * rows * PAD * 2 * rows * PAD * width,
            bytes_accessed=normed.size * 2 + rows * slots * 4 * width * 2,
            transcendentals=windows * HEADS * rows * PAD * 2 * rows * PAD,
        ),
        name="attend",
    )(row_offset, column_offset, normed, queries, own, matrix)


def finish_kernel(
    tokens_ref,
    mixed_ref,
    hidden_ref,
    hidden_other_ref,
    near_ref,
    near_other_ref,
    encoded_ref,
    out_ref,
    first_ref,
    second_ref,
):
    count, cells, features = tokens_ref.shape
    lines = LINES

    @pl.when(pl.program_id(0) == 0)
    def _():
        refs = hidden_ref, hidden_other_ref
        collect(parts(refs, 0, lines, 4 * lines), first_ref, slice(0, features))
        collect(parts(refs, lines, lines, 4 * lines), first_ref, slice(features, 2 * features))
        collect(parts(refs, 2 * lines, 2 * lines, 4 * lines), second_ref)
        for spot, block in parts((near_ref, near_other_ref), lines, lines, 2 * lines):
            block = block.astype(F32)[:, : lines // 2].reshape(-1, features)
            collect([(spot, block.astype(BF16))], out_ref)

    tokens = tokens_ref[...].reshape(count * cells, features).astype(F32)
    mixed = mixed_ref[...].reshape(count * cells, -1)
    residual = tokens + dot(mixed, out_ref[...])
    inner = layer_norm(residual)
    expanded = jax.nn.gelu(dot(inner, first_ref[...]), approximate=True).astype(BF16)
    encoded = (residual + dot(expanded, second_ref[...])).astype(BF16)
    encoded_ref[...] = encoded.reshape(count, cells, features)


def finish(tokens, mixed, weights):
    tiles, cells, features = tokens.shape
    width = mixed.shape[2]
    hidden = 2 * features
    return pl.pallas_call(
        finish_kernel,
        grid=(tiles // GROUP,),
        in_specs=[
            pl.BlockSpec((GROUP, cells, features), lambda g: (g, 0, 0)),
            pl.BlockSpec((GROUP, cells, width), lambda g: (g, 0, 0)),
        ]
        + [pl.BlockSpec(weight.shape, lambda g: (0, 0, 0)) for weight in weights],
        out_specs=pl.BlockSpec((GROUP, cells, features), lambda g: (g, 0, 0)),
        out_shape=jax.ShapeDtypeStruct((tiles, cells, features), BF16),
        scratch_shapes=[
            pltpu.VMEM((width, features), BF16),
            pltpu.VMEM((features, hidden), BF16),
            pltpu.VMEM((hidden, features), BF16),
        ],
        compiler_params=pltpu.CompilerParams(vmem_limit_bytes=24 * 1024 * 1024),
        cost_estimate=pl.CostEstimate(
            flops=2 * tiles * cells * features * (width + 2 * hidden),
            bytes_accessed=tiles * cells * (4 * features + 2 * width) + weights[0].size * 6,
            transcendentals=tiles * cells * hidden,
        ),
        name="finish",
    )(tokens, mixed, *weights)


def turn_kernel(encoded_ref, turned_ref):
    count, cells, features = encoded_ref.shape
    size = count * cells
    order = one_hot((size, size), lambda k: (k % count) * cells + k // count)
    flat = encoded_ref[...].astype(F32).reshape(size, features).astype(BF16)
    turned_ref[...] = dot(order, flat).astype(BF16).reshape(cells, count, features)


def turn(encoded):
    count, cells, features = encoded.shape
    block = 24
    return pl.pallas_call(
        turn_kernel,
        grid=(cells // block,),
        in_specs=[pl.BlockSpec((count, block, features), lambda g: (0, g, 0))],
        out_specs=pl.BlockSpec((block, count, features), lambda g: (g, 0, 0)),
        out_shape=jax.ShapeDtypeStruct((cells, count, features), BF16),
        compiler_params=pltpu.CompilerParams(vmem_limit_bytes=12 * 1024 * 1024),
        name="turn",
    )(encoded)


def copies(values, count):
    return jnp.broadcast_to(values[None], (count,) + values.shape)


def gather_far(shard):
    sizes = lax.axis_size("y_lo"), lax.axis_size("lat")
    found = lax.all_to_all(copies(shard, sizes[0] * sizes[1]), ("y_lo", "lat"), 0, 0, tiled=True)
    return found.reshape(sizes + shard.shape)


def swap(values, axis):
    return lax.ppermute(values, axis, [(0, 1), (1, 0)])


def after(first, *later):
    return lax.optimization_barrier((first,) + later)


def shards(
    fields,
    scale_exponent,
    level_mean,
    level_spread,
    row_offset,
    column_offset,
    patch_weight,
    attention_in,
    attention_out,
    hidden_in,
    hidden_out,
):
    features = patch_weight.shape[1]
    chans = fields.shape[3]
    lats = lax.axis_size("lat")
    repeat = chans // level_mean.shape[0]
    affine = jnp.stack(
        [
            jnp.tile(jnp.exp2(scale_exponent.astype(F32)) / level_spread, repeat),
            jnp.tile(level_mean / level_spread, repeat),
        ]
    )

    normalized = normalize(fields[0], affine)
    packed = pack(hidden_in, hidden_out, attention_out, attention_in)
    packed = join(packed, swap(packed, "y_lo"))
    rest = lax.all_gather(packed, "lat", axis=0)
    patch = gather_far(patch_weight)
    patch, normalized = after(patch, normalized)

    rows_tokens, top, bottom, tiles = embed(normalized, patch, swap(patch, "core"))
    _, rest = after(rows_tokens, rest)
    north = lax.ppermute(bottom, "lat", [(i, i + 1) for i in range(lats - 1)])
    south = lax.ppermute(top, "lat", [(i + 1, i) for i in range(lats - 1)])
    near = rest[:, 8 * LINES :]
    near = near, swap(near, "core")
    window_queries, own, matrix = project(column_offset, rows_tokens, near)
    normed = choose(row_offset, north, south)
    _, hidden_weight = after(matrix, rest[:, : 8 * LINES])
    mixed = attend(row_offset, column_offset, normed, window_queries, own, matrix)
    encoded = finish(tiles.reshape(-1, WH * WW, features), mixed, (hidden_weight, swap(hidden_weight, "core")) + near)
    encoded = turn(lax.all_to_all(encoded, ("y_hi", "x"), 0, 0, tiled=True))
    return encoded.reshape(WH, WW, -1, features).transpose(2, 0, 1, 3)


def solution(mesh):
    tm, lat, lon = (mesh.shape[name] for name in ("tm", "lat", "lon"))
    cores, across = 2, 4
    finer = Mesh(
        mesh.devices.reshape(tm // cores, cores, lat, lon // across, across),
        ("y_lo", "core", "lat", "y_hi", "x"),
    )
    time = ("y_lo", "core")
    in_specs = (
        P(time + ("y_hi", "x"), "lat", None, None),
        P(),
        P(),
        P(),
        P(time),
        P(time),
        P(time + ("lat",), None),
        P(time + ("lat",), None),
        P(time + ("lat",), None),
        P(time + ("lat",), None),
        P(time + ("lat",), None),
    )
    out_specs = P(time, "lat", ("y_hi", "x"), None)
    return jax.shard_map(shards, mesh=finer, in_specs=in_specs, out_specs=out_specs, check_vma=False)
```

time: 215 us -> 157 us (0.73)
  the two profiles are of different devices: /device:TPU:8 before, /device:TPU:1 now
where the time goes in v2:
time: 157 us
  blocking collectives  40.5 us (26%)
  waiting for transfers between devices  32.5 us (21%)
  starting transfers between devices  31.3 us (20%)
  Pallas kernels  28.6 us (18%)
  between operations  13.7 us (9%)
  local copies, waits for them, and re-layouts  10.1 us (6%)
    all_to_all x1, blocking collectives, shards(): encoded = turn(lax.all_to_all(encoded, ('y_hi', 'x'), 0, 0, tiled=True))  40.5 us
    all_gather x1, waiting for transfers between devices, shards(): rest = lax.all_gather(packed, 'lat', axis=0)  26.6 us
    ppermute x4, starting transfers between devices, swap(): return lax.ppermute(values, axis, [(0, 1), (1, 0)])  13.5 us
    all_to_all x1, starting transfers between devices, gather_far(): lax.all_to_all(copies(shard, sizes[0] * sizes[1]), ('y_lo', 'lat'), 0, 0,...  12 us
    pallas_call x1, Pallas kernels, attend(): pl.pallas_call(attend_kernel, in_specs=[pl.BlockSpec(memory_space=pltpu.S...  8.33 us
    unnamed x26, local copies, waits for them, and re-layouts  5.84 us
    ppermute x4, waiting for transfers between devices, swap(): return lax.ppermute(values, axis, [(0, 1), (1, 0)])  5.82 us
    pallas_call x1, Pallas kernels, finish(): pl.pallas_call(finish_kernel, grid=(tiles // GROUP,), in_specs=[pl.BlockS...  5.41 us
  transfers between devices with their start and end apart: 8, of which 4 were waited for; matrix products, arithmetic and copies ran while one was open for 2% of the time, Pallas kernels for 13%

profile of v2, /device:TPU:1, one launch (start us, length us, event | category | flops | bytes accessed | tf_op | source)
XLA Modules:
  0.0 156.6 jit_solution(11036305598550177565)
XLA Ops:
  6.5 1.8 %broadcast_in_dim.2 = bf16[16,32,512]{2,1,0:T(8,128)(2,1)} broadcast(bf16[32,512]{1,0:T(8,128)(2,1)} %param.17), dimensions={1,2} | broadcast | bytes 557056 | tf_op jit(solution)/shard_map/broadcast_in_dim | solution.py:506
  8.3 12.0 %all-to-all-start = ((bf16[16,32,512]{2,1,0:T(8,128)(2,1)}), bf16[16,32,512]{2,1,0:T(8,128)(2,1)S(1)}, u32[]{:S(2)}, u32[]{:S(2)}) async-start(bf16[16,32,512]{2,1,0:T(8,128)(2,1)} %broadcast_in_dim.2), calls=%async_computation | async-start | bytes 1048576 | tf_op jit(solution)/shard_map/all_to_all | solution.py:511
  20.3 1.4 pack.1.own_ref
  21.8 3.3 %collective-permute-start.3 = (bf16[96,512]{1,0:T(8,128)(2,1)}, bf16[96,512]{1,0:T(8,128)(2,1)S(1)}, u32[]{:S(2)}, u32[]{:S(2)}) collective-permute-start(bf16[96,512]{1,0:T(8,128)(2,1)} %pack.1.own_ref), channel_id=1, source_target_pairs={{0,256},{256,0},{1,257},{257,1},{2,258},{258,2},{3,259},{259,3},{4... | collective-permute-start | bytes 294920 | tf_op jit(solution)/shard_map/ppermute | solution.py:516
  25.3 4.1 %collective-permute-done.3.swapped_ref = bf16[96,512]{1,0:T(8,128)(2,1)S(1)} collective-permute-done((bf16[96,512]{1,0:T(8,128)(2,1)}, bf16[96,512]{1,0:T(8,128)(2,1)S(1)}, u32[]{:S(2)}, u32[]{:S(2)}) %collective-permute-start.3) | collective-permute-done | bytes 98336 | tf_op jit(solution)/shard_map/ppermute | solution.py:516
  30.0 1.6 %join.1 = bf16[192,512]{1,0:T(8,128)(2,1)} custom-call(bf16[96,512]{1,0:T(8,128)(2,1)} %pack.1.own_ref, bf16[96,512]{1,0:T(8,128)(2,1)} %copy-done.9), custom_call_target="tpu_custom_call" | custom-call | tf_op jit(solution)/shard_map/join/pallas_call | solution.py:116
  32.3 1.4 copy-done.1
  33.8 3.8 %collective-permute-start = (bf16[2,8,32,512]{3,2,1,0:T(8,128)(2,1)S(1)}, bf16[2,8,32,512]{3,2,1,0:T(8,128)(2,1)S(1)}, u32[]{:S(2)}, u32[]{:S(2)}) collective-permute-start(bf16[2,8,32,512]{3,2,1,0:T(8,128)(2,1)S(1)} %bitcast.8), channel_id=1, source_target_pairs={{0,128},{128,0},{1,129},{129,1},{2,130},{130,2},{3,131},{131,3},{4... | collective-permute-start | bytes 1572872 | tf_op jit(solution)/shard_map/ppermute | solution.py:516
  37.5 1.5 collective-permute-done.other_ref
  39.1 1.7 %copy-done.2 = bf16[24,192,256]{2,1,0:T(8,128)(2,1)S(1)} copy-done((bf16[24,192,256]{2,1,0:T(8,128)(2,1)S(1)}, bf16[24,192,256]{2,1,0:T(8,128)(2,1)}, u32[]{:S(2)}) %copy-start.2) | copy-done | bytes 2359320
  40.7 3.8 %embed.1 = (bf16[6,192,512]{2,1,0:T(8,128)(2,1)S(1)}, bf16[5,192,512]{2,1,0:T(8,128)(2,1)S(1)}, bf16[5,192,512]{2,1,0:T(8,128)(2,1)S(1)}, bf16[1152,512]{1,0:T(8,128)(2,1)S(1)}) custom-call(bf16[24,192,256]{2,1,0:T(8,128)(2,1)S(1)} %copy-done.2, bf16[2,8,32,512]{3,2,1,0:T(8,128)(2,1)S(1)} %bitcast.9, bf16[2,8,32,512]{3,2,1,0:T(8,128)(2,1)S(1)} %collective-permute-done.other_ref), custom_call_target="tpu_custom_call" | custom-call | flops 20000000000 | tf_op jit(solution)/shard_map/embed/pallas_call | solution.py:191
  46.6 4.4 %collective-permute-start.1 = (bf16[5,192,512]{2,1,0:T(8,128)(2,1)S(1)}, bf16[5,192,512]{2,1,0:T(8,128)(2,1)S(1)}, u32[]{:S(2)}, u32[]{:S(2)}) collective-permute-start(bf16[5,192,512]{2,1,0:T(8,128)(2,1)S(1)} %get-tuple-element.19), channel_id=1, source_target_pairs={{0,16},{16,32},{32,48},{48,64},{64,80},{80,96},{96,112},{1,17},{17... | collective-permute-start | bytes 2949128 | tf_op jit(solution)/shard_map/ppermute | solution.py:556
  51.0 1.3 collective-permute-start.2
  52.3 26.6 %all-gather.3.cloned.1.call-done = bf16[1536,512]{1,0:T(8,128)(2,1)} async-done(((bf16[192,512]{1,0:T(8,128)(2,1)}), bf16[1536,512]{1,0:T(8,128)(2,1)}) %all-gather.3.cloned.1.call-update) | async-done | bytes 1572880 | tf_op jit(solution)/shard_map/all_gather | solution.py:550
  78.9 1.1 slice.6.weight_ref.near_ref
  80.0 4.2 %collective-permute-start.4 = (bf16[8,64,512]{2,1,0:T(8,128)(2,1)S(1)}, bf16[8,64,512]{2,1,0:T(8,128)(2,1)S(1)}, u32[]{:S(2)}, u32[]{:S(2)}) collective-permute-start(bf16[8,64,512]{2,1,0:T(8,128)(2,1)S(1)} %slice.6.weight_ref.near_ref), channel_id=1, source_target_pairs={{0,128},{128,0},{1,129},{129,1},{2,130},{130,2},{3,131},{131,3},{4... | collective-permute-start | bytes 1572872 | tf_op jit(solution)/shard_map/ppermute | solution.py:516
  84.3 1.3 slice.7.hidden_ref
  85.8 3.1 %project.1 = (bf16[6,256,256]{2,1,0:T(8,128)(2,1)S(1)}, bf16[6,256,512]{2,1,0:T(8,128)(2,1)S(1)}, bf16[512,512]{1,0:T(8,128)(2,1)S(1)}) custom-call(s32[16]{0:T(128)S(1)} %copy-done.4, bf16[6,192,512]{2,1,0:T(8,128)(2,1)S(1)} %copy-done.8, bf16[8,64,512]{2,1,0:T(8,128)(2,1)S(1)} %slice.6.weight_ref.near_ref, ...), custom_call_target="tpu_custom_call" | custom-call | flops 1358954496 | bytes 3538944 | tf_op jit(solution)/shard_map/project/pallas_call | solution.py:266
  88.9 2.3 %collective-permute-start.5 = (bf16[8,128,512]{2,1,0:T(8,128)(2,1)S(1)}, bf16[8,128,512]{2,1,0:T(8,128)(2,1)S(1)}, u32[]{:S(2)}, u32[]{:S(2)}) collective-permute-start(bf16[8,128,512]{2,1,0:T(8,128)(2,1)S(1)} %slice.7.hidden_ref), channel_id=1, source_target_pairs={{0,128},{128,0},{1,129},{129,1},{2,130},{130,2},{3,131},{131,3},{4... | collective-permute-start | bytes 3145736 | tf_op jit(solution)/shard_map/ppermute | solution.py:516
  91.2 2.0 %choose.1.normed_ref = bf16[6,192,512]{2,1,0:T(8,128)(2,1)S(1)} custom-call(s32[16]{0:T(128)S(1)} %copy-done.3, bf16[5,192,512]{2,1,0:T(8,128)(2,1)S(1)} %collective-permute-done.1.north_ref, bf16[5,192,512]{2,1,0:T(8,128)(2,1)} %collective-permute-done.2.south_ref), custom_call_target="tpu_custom_call" | custom-call | flops 30000001024 | tf_op jit(solution)/shard_map/choose/pallas_call | solution.py:299
  93.2 8.3 %attend.1.mixed_ref = bf16[16,72,256]{2,1,0:T(8,128)(2,1)S(1)} custom-call(s32[16]{0:T(128)S(1)} %copy-done.3, s32[16]{0:T(128)S(1)} %copy-done.4, bf16[6,192,512]{2,1,0:T(8,128)(2,1)S(1)} %choose.1.normed_ref, bf16[6,256,256]{2,1,0:T(8,128)(2,1)S(1)} %get-tuple-element.23.query_ref, bf16[6,256,512]{2,1,0:T(8,128)(2,1)S(1)} %get-tuple-element.24.own_ref, ...), custom_call_target="tpu_custom_call" | custom-call | flops 2113929216 | bytes 4325376 | tf_op jit(solution)/shard_map/attend/pallas_call | solution.py:401
  101.6 5.4 %finish.1 = bf16[16,72,512]{2,1,0:T(8,128)(2,1)S(1)} custom-call(bf16[16,72,512]{2,1,0:T(8,128)(2,1)S(1)} %bitcast.10, bf16[16,72,256]{2,1,0:T(8,128)(2,1)S(1)} %attend.1.mixed_ref, bf16[8,128,512]{2,1,0:T(8,128)(2,1)S(1)} %slice.7.hidden_ref, bf16[8,128,512]{2,1,0:T(8,128)(2,1)S(1)} %collective-permute-done.5.hidden_other_ref, ...), custom_call_target="tpu_custom_call" | custom-call | flops 2717908992 | bytes 6094848 | tf_op jit(solution)/shard_map/finish/pallas_call | solution.py:458
  107.0 40.5 %all_to_all.10.encoded_ref = bf16[16,72,512]{2,1,0:T(8,128)(2,1)S(1)} all-to-all(bf16[16,72,512]{2,1,0:T(8,128)(2,1)S(1)} %finish.1), channel_id=1, replica_groups=mesh['y_lo'=2,'core'=2,'lat'=8,'y_hi'=4,'x'=4] {'y_hi','x'}, dimensions={0} | all-to-all | bytes 2359296 | tf_op jit(solution)/shard_map/all_to_all | solution.py:565
  147.5 2.3 %turn.1 = bf16[72,16,512]{2,1,0:T(8,128)(2,1)} custom-call(bf16[16,72,512]{2,1,0:T(8,128)(2,1)S(1)} %all_to_all.10.encoded_ref), custom_call_target="tpu_custom_call" | custom-call | tf_op jit(solution)/shard_map/turn/pallas_call | solution.py:494
  (38 shorter events, 3.8 us)
Async XLA Ops:
  6.5 18.5 %copy-start.10 = (f32[64]{0:T(128)S(1)}, f32[64]{0:T(128)}, u32[]{:S(2)}) copy-start(f32[64]{0:T(128)} %param.14) | copy-start | bytes 772
  6.5 18.5 %copy-start.11 = (s32[64]{0:T(128)S(1)}, s32[64]{0:T(128)}, u32[]{:S(2)}) copy-start(s32[64]{0:T(128)} %param.12) | copy-start | bytes 772
  6.5 18.5 %copy-start.12 = (f32[64]{0:T(128)S(1)}, f32[64]{0:T(128)}, u32[]{:S(2)}) copy-start(f32[64]{0:T(128)} %param.13) | copy-start | bytes 772
  6.5 25.1 %copy-start = (bf16[1,24,192,256]{3,2,1,0:T(8,128)(2,1)S(1)}, bf16[1,24,192,256]{3,2,1,0:T(8,128)(2,1)}, u32[]{:S(2)}) copy-start(bf16[1,24,192,256]{3,2,1,0:T(8,128)(2,1)} %param.11) | copy-start | bytes 7077892
  8.3 25.5 %all-to-all-start = ((bf16[16,32,512]{2,1,0:T(8,128)(2,1)}), bf16[16,32,512]{2,1,0:T(8,128)(2,1)S(1)}, u32[]{:S(2)}, u32[]{:S(2)}) async-start(bf16[16,32,512]{2,1,0:T(8,128)(2,1)} %broadcast_in_dim.2), calls=%async_computation | async-start | bytes 1048576 | tf_op jit(solution)/shard_map/all_to_all | solution.py:511
  20.3 58.7 %all-gather.3.cloned.1.call-start = ((), (), s32[]{:S(2)}) async-start(), calls=%async_computation.2 | async-start | bytes 1769472 | tf_op jit(solution)/shard_map/all_gather | solution.py:550
  21.8 7.6 %collective-permute-start.3 = (bf16[96,512]{1,0:T(8,128)(2,1)}, bf16[96,512]{1,0:T(8,128)(2,1)S(1)}, u32[]{:S(2)}, u32[]{:S(2)}) collective-permute-start(bf16[96,512]{1,0:T(8,128)(2,1)} %pack.1.own_ref), channel_id=1, source_target_pairs={{0,256},{256,0},{1,257},{257,1},{2,258},{258,2},{3,259},{259,3},{4... | collective-permute-start | bytes 294920 | tf_op jit(solution)/shard_map/ppermute | solution.py:516
  29.4 0.6 copy-start.9
  32.3 1.4 copy-start.1
  33.8 5.3 %collective-permute-start = (bf16[2,8,32,512]{3,2,1,0:T(8,128)(2,1)S(1)}, bf16[2,8,32,512]{3,2,1,0:T(8,128)(2,1)S(1)}, u32[]{:S(2)}, u32[]{:S(2)}) collective-permute-start(bf16[2,8,32,512]{3,2,1,0:T(8,128)(2,1)S(1)} %bitcast.8), channel_id=1, source_target_pairs={{0,128},{128,0},{1,129},{129,1},{2,130},{130,2},{3,131},{131,3},{4... | collective-permute-start | bytes 1572872 | tf_op jit(solution)/shard_map/ppermute | solution.py:516
  39.1 1.7 %copy-start.2 = (bf16[24,192,256]{2,1,0:T(8,128)(2,1)S(1)}, bf16[24,192,256]{2,1,0:T(8,128)(2,1)}, u32[]{:S(2)}) copy-start(bf16[24,192,256]{2,1,0:T(8,128)(2,1)} %copy-done.1) | copy-start | bytes 7077892
  44.5 1.0 copy-start.5
  45.5 1.1 copy-start.7
  46.6 44.6 %collective-permute-start.1 = (bf16[5,192,512]{2,1,0:T(8,128)(2,1)S(1)}, bf16[5,192,512]{2,1,0:T(8,128)(2,1)S(1)}, u32[]{:S(2)}, u32[]{:S(2)}) collective-permute-start(bf16[5,192,512]{2,1,0:T(8,128)(2,1)S(1)} %get-tuple-element.19), channel_id=1, source_target_pairs={{0,16},{16,32},{32,48},{48,64},{64,80},{80,96},{96,112},{1,17},{17... | collective-permute-start | bytes 2949128 | tf_op jit(solution)/shard_map/ppermute | solution.py:556
  51.0 40.2 %collective-permute-start.2 = (bf16[5,192,512]{2,1,0:T(8,128)(2,1)S(1)}, bf16[5,192,512]{2,1,0:T(8,128)(2,1)}, u32[]{:S(2)}, u32[]{:S(2)}) collective-permute-start(bf16[5,192,512]{2,1,0:T(8,128)(2,1)S(1)} %get-tuple-element.20), channel_id=1, source_target_pairs={{16,0},{32,16},{48,32},{64,48},{80,64},{96,80},{112,96},{17,1},{33... | collective-permute-start | bytes 2949128 | tf_op jit(solution)/shard_map/ppermute | solution.py:557
  80.0 5.8 %copy-start.4 = (s32[16]{0:T(128)S(1)}, s32[16]{0:T(128)}, u32[]{:S(2)}) copy-start(s32[16]{0:T(128)} %column_offset_ref.3) | copy-start | bytes 196
  80.0 5.8 %copy-start.8 = (bf16[6,192,512]{2,1,0:T(8,128)(2,1)S(1)}, bf16[6,192,512]{2,1,0:T(8,128)(2,1)}, u32[]{:S(2)}) copy-start(bf16[6,192,512]{2,1,0:T(8,128)(2,1)} %copy-done.7) | copy-start | bytes 3538948
  80.0 5.8 %collective-permute-start.4 = (bf16[8,64,512]{2,1,0:T(8,128)(2,1)S(1)}, bf16[8,64,512]{2,1,0:T(8,128)(2,1)S(1)}, u32[]{:S(2)}, u32[]{:S(2)}) collective-permute-start(bf16[8,64,512]{2,1,0:T(8,128)(2,1)S(1)} %slice.6.weight_ref.near_ref), channel_id=1, source_target_pairs={{0,128},{128,0},{1,129},{129,1},{2,130},{130,2},{3,131},{131,3},{4... | collective-permute-start | bytes 1572872 | tf_op jit(solution)/shard_map/ppermute | solution.py:516
  85.6 5.6 %copy-start.3 = (s32[16]{0:T(128)S(1)}, s32[16]{0:T(128)}, u32[]{:S(2)}) copy-start(s32[16]{0:T(128)} %row_offset_ref.3) | copy-start | bytes 196
  88.9 12.7 %collective-permute-start.5 = (bf16[8,128,512]{2,1,0:T(8,128)(2,1)S(1)}, bf16[8,128,512]{2,1,0:T(8,128)(2,1)S(1)}, u32[]{:S(2)}, u32[]{:S(2)}) collective-permute-start(bf16[8,128,512]{2,1,0:T(8,128)(2,1)S(1)} %slice.7.hidden_ref), channel_id=1, source_target_pairs={{0,128},{128,0},{1,129},{129,1},{2,130},{130,2},{3,131},{131,3},{4... | collective-permute-start | bytes 3145736 | tf_op jit(solution)/shard_map/ppermute | solution.py:516
  93.2 8.4 %copy-start.6 = (bf16[1152,512]{1,0:T(8,128)(2,1)S(1)}, bf16[1152,512]{1,0:T(8,128)(2,1)}, u32[]{:S(2)}) copy-start(bf16[1152,512]{1,0:T(8,128)(2,1)} %copy-done.5) | copy-start | bytes 3538948
Sparse Core Ops, SparseCore 0:
  31.8 47.1 all-gather.2

commit v3 on v2

--- a/solution.py
+++ b/solution.py
@@ -21,8 +21,8 @@
 F32 = jnp.float32
 GROUP = 4
 ATTEND_COST = 1
-EMBED_COST = 2 * 10**10
-CHOOSE_COST = 3 * 10**10
+EMBED_COST = 6 * 10**9
+CHOOSE_COST = 8 * 10**9
 LINES = 16
 
 
@@ -103,48 +103,28 @@
     )(hidden_in, hidden_out, attention_out, attention_in)
 
 
-def join_kernel(own_ref, swapped_ref, joined_ref):
-    far = 4 * LINES
-    near = own_ref.shape[0] - far
-    joined_ref[:far] = own_ref[:far]
-    joined_ref[far : 2 * far] = swapped_ref[:far]
-    joined_ref[2 * far : 2 * far + near] = own_ref[far:]
-    joined_ref[2 * far + near :] = swapped_ref[far:]
+def join_kernel(own_ref, swapped_ref, early_ref, late_ref):
+    size = 2 * LINES
+    for y, ref in enumerate((own_ref, swapped_ref)):
+        early_ref[y * size : (y + 1) * size] = ref[2 * size :]
+        early_ref[(2 + y) * size : (3 + y) * size] = ref[:size]
+        late_ref[y * size : (y + 1) * size] = ref[size : 2 * size]
+    late_ref[2 * size :] = jnp.zeros((2 * size, own_ref.shape[1]), BF16)
 
 
 def join(own, swapped):
+    shape = jax.ShapeDtypeStruct((8 * LINES, own.shape[1]), BF16)
     return pl.pallas_call(
         join_kernel,
         in_specs=[pl.BlockSpec(memory_space=pltpu.VMEM)] * 2,
-        out_shape=jax.ShapeDtypeStruct((2 * own.shape[0], own.shape[1]), BF16),
+        out_shape=[shape, shape],
         name="join",
     )(own, swapped)
 
 
-def normalize_kernel(fields_ref, affine_ref, normalized_ref):
-    factor = affine_ref[0:1, :]
-    shift = affine_ref[1:2, :]
-    normalized_ref[...] = (fields_ref[...].astype(F32) * factor - shift).astype(BF16)
-
-
-def normalize(fields, affine):
-    pixel_rows, columns, chans = fields.shape
-    return pl.pallas_call(
-        normalize_kernel,
-        grid=(pixel_rows // P_SIZE,),
-        in_specs=[
-            pl.BlockSpec((P_SIZE, columns, chans), lambda g: (g, 0, 0)),
-            pl.BlockSpec(affine.shape, lambda g: (0, 0)),
-        ],
-        out_specs=pl.BlockSpec((P_SIZE, columns, chans), lambda g: (g, 0, 0)),
-        out_shape=jax.ShapeDtypeStruct(fields.shape, BF16),
-        compiler_params=pltpu.CompilerParams(vmem_limit_bytes=12 * 1024 * 1024),
-        name="normalize",
-    )(fields, affine)
-
-
 def embed_kernel(
     fields_ref,
+    affine_ref,
     weight_ref,
     other_ref,
     rows_ref,
@@ -164,10 +144,14 @@
 
     columns = fields_ref.shape[1]
     chans = fields_ref.shape[2]
-    normalized = fields_ref[...].reshape(rows, P_SIZE, columns, chans)
+    raw = fields_ref[...].reshape(rows, P_SIZE, columns, chans)
+    factor = affine_ref[0:1, :]
+    shift = affine_ref[1:2, :]
     total = None
     for pixel in range(P_SIZE):
-        product = dot(normalized[:, pixel].reshape(rows * columns, chans), table_ref[pixel])
+        part = raw[:, pixel].reshape(rows * columns, chans).astype(F32)
+        part = (part * factor - shift).astype(BF16)
+        product = dot(part, table_ref[pixel])
         total = product if total is None else total + product
     tokens = total.astype(BF16)
     by_row = tokens.reshape(rows, columns, -1)
@@ -183,7 +167,7 @@
     tiles_ref[...] = dot(order, tokens).astype(BF16)
 
 
-def embed(fields, weight, other):
+def embed(fields, affine, weight, other):
     pixel_rows, columns, chans = fields.shape
     rows = pixel_rows // P_SIZE
     width = weight.shape[-1]
@@ -193,6 +177,7 @@
         grid=(columns // step,),
         in_specs=[
             pl.BlockSpec((pixel_rows, step, chans), lambda g: (0, g, 0)),
+            pl.BlockSpec(affine.shape, lambda g: (0, 0)),
             pl.BlockSpec(weight.shape, lambda g: (0,) * weight.ndim),
             pl.BlockSpec(weight.shape, lambda g: (0,) * weight.ndim),
         ],
@@ -216,7 +201,7 @@
             transcendentals=0,
         ),
         name="embed",
-    )(fields, weight, other)
+    )(fields, affine, weight, other)
 
 
 def roll_matrix(columns, shift, scale):
@@ -420,8 +405,10 @@
 def finish_kernel(
     tokens_ref,
     mixed_ref,
-    hidden_ref,
-    hidden_other_ref,
+    first_own_ref,
+    first_other_ref,
+    second_own_ref,
+    second_other_ref,
     near_ref,
     near_other_ref,
     encoded_ref,
@@ -434,37 +421,41 @@
 
     @pl.when(pl.program_id(0) == 0)
     def _():
-        refs = hidden_ref, hidden_other_ref
-        collect(parts(refs, 0, lines, 4 * lines), first_ref, slice(0, features))
-        collect(parts(refs, lines, lines, 4 * lines), first_ref, slice(features, 2 * features))
-        collect(parts(refs, 2 * lines, 2 * lines, 4 * lines), second_ref)
+        refs = first_own_ref, first_other_ref
+        collect(parts(refs, 0, lines, 2 * lines), first_ref, slice(0, features))
+        collect(parts(refs, lines, lines, 2 * lines), first_ref, slice(features, 2 * features))
+        refs = second_own_ref, second_other_ref
+        collect(parts(refs, 0, 2 * lines, 2 * lines), second_ref)
         for spot, block in parts((near_ref, near_other_ref), lines, lines, 2 * lines):
             block = block.astype(F32)[:, : lines // 2].reshape(-1, features)
             collect([(spot, block.astype(BF16))], out_ref)
 
-    tokens = tokens_ref[...].reshape(count * cells, features).astype(F32)
-    mixed = mixed_ref[...].reshape(count * cells, -1)
+    tokens = tokens_ref[...].astype(F32).reshape(count * cells, features)
+    mixed = mixed_ref[...].astype(F32).reshape(count * cells, -1).astype(BF16)
     residual = tokens + dot(mixed, out_ref[...])
     inner = layer_norm(residual)
     expanded = jax.nn.gelu(dot(inner, first_ref[...]), approximate=True).astype(BF16)
     encoded = (residual + dot(expanded, second_ref[...])).astype(BF16)
-    encoded_ref[...] = encoded.reshape(count, cells, features)
+    size = count * cells
+    order = one_hot((size, size), lambda k: (k % count) * cells + k // count)
+    encoded_ref[...] = dot(order, encoded).astype(BF16).reshape(cells, count, features)
 
 
 def finish(tokens, mixed, weights):
-    tiles, cells, features = tokens.shape
+    count, cells, features = tokens.shape
     width = mixed.shape[2]
     hidden = 2 * features
+    block = 24
     return pl.pallas_call(
         finish_kernel,
-        grid=(tiles // GROUP,),
+        grid=(cells // block,),
         in_specs=[
-            pl.BlockSpec((GROUP, cells, features), lambda g: (g, 0, 0)),
-            pl.BlockSpec((GROUP, cells, width), lambda g: (g, 0, 0)),
+            pl.BlockSpec((count, block, features), lambda g: (0, g, 0)),
+            pl.BlockSpec((count, block, width), lambda g: (0, g, 0)),
         ]
         + [pl.BlockSpec(weight.shape, lambda g: (0, 0, 0)) for weight in weights],
-        out_specs=pl.BlockSpec((GROUP, cells, features), lambda g: (g, 0, 0)),
-        out_shape=jax.ShapeDtypeStruct((tiles, cells, features), BF16),
+        out_specs=pl.BlockSpec((block, count, features), lambda g: (g, 0, 0)),
+        out_shape=jax.ShapeDtypeStruct((cells, count, features), BF16),
         scratch_shapes=[
             pltpu.VMEM((width, features), BF16),
             pltpu.VMEM((features, hidden), BF16),
@@ -472,34 +463,12 @@
         ],
         compiler_params=pltpu.CompilerParams(vmem_limit_bytes=24 * 1024 * 1024),
         cost_estimate=pl.CostEstimate(
-            flops=2 * tiles * cells * features * (width + 2 * hidden),
-            bytes_accessed=tiles * cells * (4 * features + 2 * width) + weights[0].size * 6,
-            transcendentals=tiles * cells * hidden,
+            flops=2 * count * cells * features * (width + 2 * hidden),
+            bytes_accessed=count * cells * (4 * features + 2 * width) + weights[0].size * 12,
+            transcendentals=count * cells * hidden,
         ),
         name="finish",
     )(tokens, mixed, *weights)
-
-
-def turn_kernel(encoded_ref, turned_ref):
-    count, cells, features = encoded_ref.shape
-    size = count * cells
-    order = one_hot((size, size), lambda k: (k % count) * cells + k // count)
-    flat = encoded_ref[...].astype(F32).reshape(size, features).astype(BF16)
-    turned_ref[...] = dot(order, flat).astype(BF16).reshape(cells, count, features)
-
-
-def turn(encoded):
-    count, cells, features = encoded.shape
-    block = 24
-    return pl.pallas_call(
-        turn_kernel,
-        grid=(cells // block,),
-        in_specs=[pl.BlockSpec((count, block, features), lambda g: (0, g, 0))],
-        out_specs=pl.BlockSpec((block, count, features), lambda g: (g, 0, 0)),
-        out_shape=jax.ShapeDtypeStruct((cells, count, features), BF16),
-        compiler_params=pltpu.CompilerParams(vmem_limit_bytes=12 * 1024 * 1024),
-        name="turn",
-    )(encoded)
 
 
 def copies(values, count):
@@ -544,25 +513,31 @@
         ]
     )
 
-    normalized = normalize(fields[0], affine)
     packed = pack(hidden_in, hidden_out, attention_out, attention_in)
-    packed = join(packed, swap(packed, "y_lo"))
-    rest = lax.all_gather(packed, "lat", axis=0)
+    early, late = join(packed, swap(packed, "y_lo"))
+    early = lax.all_gather(early, "lat", axis=0)
     patch = gather_far(patch_weight)
-    patch, normalized = after(patch, normalized)
-
-    rows_tokens, top, bottom, tiles = embed(normalized, patch, swap(patch, "core"))
-    _, rest = after(rows_tokens, rest)
+
+    rows_tokens, top, bottom, tiles = embed(fields[0], affine, patch, swap(patch, "core"))
+    _, early = after(rows_tokens, early)
+    _, late = after(rows_tokens, late)
+    late = lax.all_gather(late, "lat", axis=0)
     north = lax.ppermute(bottom, "lat", [(i, i + 1) for i in range(lats - 1)])
     south = lax.ppermute(top, "lat", [(i + 1, i) for i in range(lats - 1)])
-    near = rest[:, 8 * LINES :]
+    tiles = tiles.reshape(-1, WH * WW, features)
+    tile_tokens = lax.all_to_all(tiles, ("y_hi", "x"), 0, 0, tiled=True)
+
+    half = 4 * LINES
+    near = early[:, :half]
     near = near, swap(near, "core")
     window_queries, own, matrix = project(column_offset, rows_tokens, near)
     normed = choose(row_offset, north, south)
-    _, hidden_weight = after(matrix, rest[:, : 8 * LINES])
     mixed = attend(row_offset, column_offset, normed, window_queries, own, matrix)
-    encoded = finish(tiles.reshape(-1, WH * WW, features), mixed, (hidden_weight, swap(hidden_weight, "core")) + near)
-    encoded = turn(lax.all_to_all(encoded, ("y_hi", "x"), 0, 0, tiled=True))
+    _, mixed = after(tile_tokens, mixed)
+    _, first, second = after(mixed, early[:, half:], late[:, :half])
+    tile_mixed = lax.all_to_all(mixed, ("y_hi", "x"), 0, 0, tiled=True)
+    weights = (first, swap(first, "core"), second, swap(second, "core")) + near
+    encoded = finish(tile_tokens, tile_mixed, weights)
     return encoded.reshape(WH, WW, -1, features).transpose(2, 0, 1, 3)
 
 

time: 157 us -> 146 us (0.930)
  blocking collectives: 40.5 us -> 0 us
  starting transfers between devices: 31.3 us -> 60.2 us
  waiting for transfers between devices: 32.5 us -> 28.5 us
  local copies, waits for them, and re-layouts: 10.1 us -> 12.5 us
  Pallas kernels: 28.6 us -> 30.6 us
    all_to_all x1 -> x0, blocking collectives: 40.5 us -> none  [shards(): encoded = turn(lax.all_to_all(encoded, ('y_hi', 'x'), 0, 0, tiled=True))]
    all_to_all x0 -> x2, starting transfers between devices: none -> 17.4 us  [the longest x1 8.89 us: shards(): tile_mixed = lax.all_to_all(mixed, ('y_hi', 'x'), 0, 0, tiled=True)]
    ppermute x4 -> x5, starting transfers between devices: 13.5 us -> 24.1 us  [swap(): return lax.ppermute(values, axis, [(0, 1), (1, 0)])]
    all_gather x1 -> x2, waiting for transfers between devices: 26.6 us -> 16.9 us  [the longest x1 10.1 us: shards(): early = lax.all_gather(early, 'lat', axis=0)]
    ppermute x1, waiting for transfers between devices: 0.01 us -> 2.51 us  [shards(): south = lax.ppermute(top, 'lat', [(i + 1, i) for i in range(lats - 1)])]
    unnamed x26, local copies, waits for them, and re-layouts: 5.84 us -> 8.3 us
    ppermute x4 -> x5, waiting for transfers between devices: 5.82 us -> 8.26 us  [swap(): return lax.ppermute(values, axis, [(0, 1), (1, 0)])]
    pallas_call x3 -> x1, Pallas kernels: 8.35 us -> 7.7 us  [finish(): pl.pallas_call(finish_kernel, grid=(cells // block,), in_specs=[pl.BlockS...]
  transfers between devices with their start and end apart: 8 -> 12, of which waited for: 4 -> 8; matrix products, arithmetic and copies ran while one was open for 2% -> 2% of each run, Pallas kernels for 13% -> 16%
where the time goes in v3:
time: 146 us; the launch traced here: 145 us
  starting transfers between devices  60.2 us (41%)
  Pallas kernels  30.6 us (21%)
  waiting for transfers between devices  28.5 us (20%)
  between operations  13.6 us (9%)
  local copies, waits for them, and re-layouts  12.5 us (9%)
    ppermute x5, starting transfers between devices, swap(): return lax.ppermute(values, axis, [(0, 1), (1, 0)])  24.1 us
    all_to_all x1, starting transfers between devices, gather_far(): lax.all_to_all(copies(shard, sizes[0] * sizes[1]), ('y_lo', 'lat'), 0, 0,...  12 us
    all_gather x1, waiting for transfers between devices, shards(): early = lax.all_gather(early, 'lat', axis=0)  10.1 us
    pallas_call x1, Pallas kernels, attend(): pl.pallas_call(attend_kernel, in_specs=[pl.BlockSpec(memory_space=pltpu.S...  9.2 us
    all_to_all x1, starting transfers between devices, shards(): tile_mixed = lax.all_to_all(mixed, ('y_hi', 'x'), 0, 0, tiled=True)  8.89 us
    all_to_all x1, starting transfers between devices, shards(): tile_tokens = lax.all_to_all(tiles, ('y_hi', 'x'), 0, 0, tiled=True)  8.47 us
    unnamed x26, local copies, waits for them, and re-layouts  8.3 us
    ppermute x5, waiting for transfers between devices, swap(): return lax.ppermute(values, axis, [(0, 1), (1, 0)])  8.26 us
  transfers between devices with their start and end apart: 12, of which 8 were waited for; matrix products, arithmetic and copies ran while one was open for 2% of the time, Pallas kernels for 16%

profile of v3, /device:TPU:1, one launch (start us, length us, event | category | flops | bytes accessed | tf_op | source)
XLA Modules:
  0.0 145.4 jit_solution(16895430313802713101)
XLA Ops:
  6.5 1.6 %broadcast_in_dim.2 = bf16[16,32,512]{2,1,0:T(8,128)(2,1)} broadcast(bf16[32,512]{1,0:T(8,128)(2,1)} %param.17), dimensions={1,2} | broadcast | bytes 557056 | tf_op jit(solution)/shard_map/broadcast_in_dim | solution.py:475
  8.2 12.0 %all-to-all-start = ((bf16[16,32,512]{2,1,0:T(8,128)(2,1)}), bf16[16,32,512]{2,1,0:T(8,128)(2,1)S(1)}, u32[]{:S(2)}, u32[]{:S(2)}) async-start(bf16[16,32,512]{2,1,0:T(8,128)(2,1)} %broadcast_in_dim.2), calls=%async_computation | async-start | bytes 1048576 | tf_op jit(solution)/shard_map/all_to_all | solution.py:480
  20.2 1.4 pack.1.own_ref
  21.7 3.3 %collective-permute-start.3 = (bf16[96,512]{1,0:T(8,128)(2,1)}, bf16[96,512]{1,0:T(8,128)(2,1)S(1)}, u32[]{:S(2)}, u32[]{:S(2)}) collective-permute-start(bf16[96,512]{1,0:T(8,128)(2,1)} %pack.1.own_ref), channel_id=1, source_target_pairs={{0,256},{256,0},{1,257},{257,1},{2,258},{258,2},{3,259},{259,3},{4... | collective-permute-start | bytes 294920 | tf_op jit(solution)/shard_map/ppermute | solution.py:485
  24.9 4.3 %collective-permute-done.3.swapped_ref = bf16[96,512]{1,0:T(8,128)(2,1)S(1)} collective-permute-done((bf16[96,512]{1,0:T(8,128)(2,1)}, bf16[96,512]{1,0:T(8,128)(2,1)S(1)}, u32[]{:S(2)}, u32[]{:S(2)}) %collective-permute-start.3) | collective-permute-done | bytes 98336 | tf_op jit(solution)/shard_map/ppermute | solution.py:485
  29.9 1.7 %join.1 = (bf16[128,512]{1,0:T(8,128)(2,1)}, bf16[128,512]{1,0:T(8,128)(2,1)}) custom-call(bf16[96,512]{1,0:T(8,128)(2,1)} %pack.1.own_ref, bf16[96,512]{1,0:T(8,128)(2,1)} %copy-done.9), custom_call_target="tpu_custom_call" | custom-call | tf_op jit(solution)/shard_map/join/pallas_call | solution.py:117
  32.3 5.0 %collective-permute-start = (bf16[2,8,32,512]{3,2,1,0:T(8,128)(2,1)S(1)}, bf16[2,8,32,512]{3,2,1,0:T(8,128)(2,1)S(1)}, u32[]{:S(2)}, u32[]{:S(2)}) collective-permute-start(bf16[2,8,32,512]{3,2,1,0:T(8,128)(2,1)S(1)} %bitcast.8), channel_id=1, source_target_pairs={{0,128},{128,0},{1,129},{129,1},{2,130},{130,2},{3,131},{131,3},{4... | collective-permute-start | bytes 1572872 | tf_op jit(solution)/shard_map/ppermute | solution.py:485
  38.9 1.7 %copy-done = bf16[1,24,192,256]{3,2,1,0:T(8,128)(2,1)S(1)} copy-done((bf16[1,24,192,256]{3,2,1,0:T(8,128)(2,1)S(1)}, bf16[1,24,192,256]{3,2,1,0:T(8,128)(2,1)}, u32[]{:S(2)}) %copy-start) | copy-done | bytes 2359320
  40.5 4.6 %embed.1 = (bf16[6,192,512]{2,1,0:T(8,128)(2,1)S(1)}, bf16[5,192,512]{2,1,0:T(8,128)(2,1)S(1)}, bf16[5,192,512]{2,1,0:T(8,128)(2,1)}, bf16[1152,512]{1,0:T(8,128)(2,1)}) custom-call(bf16[24,192,256]{2,1,0:T(8,128)(2,1)S(1)} %bitcast.10, f32[2,256]{1,0:T(2,128)S(1)} %pad_maximum_fusion.affine_ref, bf16[2,8,32,512]{3,2,1,0:T(8,128)(2,1)S(1)} %bitcast.9, ...), custom_call_target="tpu_custom_call" | custom-call | flops 6000000000 | tf_op jit(solution)/shard_map/embed/pallas_call | solution.py:175
  46.2 8.5 %all-to-all-start.1 = ((bf16[16,72,512]{2,1,0:T(8,128)(2,1)}), bf16[16,72,512]{2,1,0:T(8,128)(2,1)S(1)}, u32[]{:S(2)}, u32[]{:S(2)}) async-start(bf16[16,72,512]{2,1,0:T(8,128)(2,1)} %bitcast.2), calls=%async_computation.1 | async-start | bytes 2359296 | tf_op jit(solution)/shard_map/all_to_all | solution.py:528
  54.7 5.4 %collective-permute-start.1 = (bf16[5,192,512]{2,1,0:T(8,128)(2,1)}, bf16[5,192,512]{2,1,0:T(8,128)(2,1)}, u32[]{:S(2)}, u32[]{:S(2)}) collective-permute-start(bf16[5,192,512]{2,1,0:T(8,128)(2,1)} %get-tuple-element.20), channel_id=1, source_target_pairs={{0,16},{16,32},{32,48},{48,64},{64,80},{80,96},{96,112},{1,17},{17... | collective-permute-start | bytes 2949128 | tf_op jit(solution)/shard_map/ppermute | solution.py:525
  61.5 10.1 %all-gather.5.cloned.1.call-done = bf16[1024,512]{1,0:T(8,128)(2,1)} async-done(((bf16[128,512]{1,0:T(8,128)(2,1)}), bf16[1024,512]{1,0:T(8,128)(2,1)}) %all-gather.5.cloned.1.call-update) | async-done | bytes 1048592 | tf_op jit(solution)/shard_map/all_gather | solution.py:518
  71.6 1.3 fusion
  72.9 6.7 %collective-permute-start.4 = (bf16[8,64,512]{2,1,0:T(8,128)(2,1)S(1)}, bf16[8,64,512]{2,1,0:T(8,128)(2,1)}, u32[]{:S(2)}, u32[]{:S(2)}) collective-permute-start(bf16[8,64,512]{2,1,0:T(8,128)(2,1)S(1)} %get-tuple-element.34.weight_ref.near_ref), channel_id=1, source_target_pairs={{0,128},{128,0},{1,129},{129,1},{2,130},{130,2},{3,131},{131,3},{4... | collective-permute-start | bytes 1572872 | tf_op jit(solution)/shard_map/ppermute | solution.py:485
  79.6 1.6 %collective-permute-done.4.other_ref.near_other_ref = bf16[8,64,512]{2,1,0:T(8,128)(2,1)} collective-permute-done((bf16[8,64,512]{2,1,0:T(8,128)(2,1)S(1)}, bf16[8,64,512]{2,1,0:T(8,128)(2,1)}, u32[]{:S(2)}, u32[]{:S(2)}) %collective-permute-start.4) | collective-permute-done | bytes 524320 | tf_op jit(solution)/shard_map/ppermute | solution.py:485
  82.5 3.6 %project.1 = (bf16[6,256,256]{2,1,0:T(8,128)(2,1)S(1)}, bf16[6,256,512]{2,1,0:T(8,128)(2,1)S(1)}, bf16[512,512]{1,0:T(8,128)(2,1)S(1)}) custom-call(s32[16]{0:T(128)S(1)} %copy-done.6, bf16[6,192,512]{2,1,0:T(8,128)(2,1)S(1)} %copy-done.8, bf16[8,64,512]{2,1,0:T(8,128)(2,1)S(1)} %get-tuple-element.34.weight_ref.near_ref, ...), custom_call_target="tpu_custom_call" | custom-call | flops 1358954496 | bytes 3538944 | tf_op jit(solution)/shard_map/project/pallas_call | solution.py:251
  86.2 2.5 %collective-permute-done.2.south_ref = bf16[5,192,512]{2,1,0:T(8,128)(2,1)} collective-permute-done((bf16[5,192,512]{2,1,0:T(8,128)(2,1)S(1)}, bf16[5,192,512]{2,1,0:T(8,128)(2,1)}, u32[]{:S(2)}, u32[]{:S(2)}) %collective-permute-start.2) | collective-permute-done | bytes 983072 | tf_op jit(solution)/shard_map/ppermute | solution.py:526
  88.7 2.3 %choose.1.normed_ref = bf16[6,192,512]{2,1,0:T(8,128)(2,1)S(1)} custom-call(s32[16]{0:T(128)S(1)} %copy-done.5, bf16[5,192,512]{2,1,0:T(8,128)(2,1)} %collective-permute-done.1.north_ref, bf16[5,192,512]{2,1,0:T(8,128)(2,1)} %collective-permute-done.2.south_ref), custom_call_target="tpu_custom_call" | custom-call | flops 8000000000 | tf_op jit(solution)/shard_map/choose/pallas_call | solution.py:284
  91.0 9.2 %attend.1 = bf16[16,72,256]{2,1,0:T(8,128)(2,1)} custom-call(s32[16]{0:T(128)S(1)} %copy-done.5, s32[16]{0:T(128)S(1)} %copy-done.6, bf16[6,192,512]{2,1,0:T(8,128)(2,1)S(1)} %choose.1.normed_ref, bf16[6,256,256]{2,1,0:T(8,128)(2,1)S(1)} %get-tuple-element.25.query_ref, bf16[6,256,512]{2,1,0:T(8,128)(2,1)S(1)} %get-tuple-element.26.own_ref, ...), custom_call_target="tpu_custom_call" | custom-call | flops 2113929216 | bytes 4325376 | tf_op jit(solution)/shard_map/attend/pallas_call | solution.py:386
  100.2 8.9 %all-to-all-start.2 = ((bf16[16,72,256]{2,1,0:T(8,128)(2,1)}), bf16[16,72,256]{2,1,0:T(8,128)(2,1)S(1)}, u32[]{:S(2)}, u32[]{:S(2)}) async-start(bf16[16,72,256]{2,1,0:T(8,128)(2,1)} %attend.1), calls=%async_computation.2 | async-start | bytes 1179648 | tf_op jit(solution)/shard_map/all_to_all | solution.py:538
  109.1 6.7 %all-gather.7.cloned.1.call-done = bf16[1024,512]{1,0:T(8,128)(2,1)} async-done(((bf16[128,512]{1,0:T(8,128)(2,1)}), bf16[1024,512]{1,0:T(8,128)(2,1)}) %all-gather.7.cloned.1.call-update) | async-done | bytes 1048592 | tf_op jit(solution)/shard_map/all_gather | solution.py:524
  116.9 7.2 %collective-permute-start.5 = (bf16[8,64,512]{2,1,0:T(8,128)(2,1)S(1)}, bf16[8,64,512]{2,1,0:T(8,128)(2,1)S(1)}, u32[]{:S(2)}, u32[]{:S(2)}) collective-permute-start(bf16[8,64,512]{2,1,0:T(8,128)(2,1)S(1)} %get-tuple-element.31.first_own_ref), channel_id=1, source_target_pairs={{0,128},{128,0},{1,129},{129,1},{2,130},{130,2},{3,131},{131,3},{4... | collective-permute-start | bytes 1572872 | tf_op jit(solution)/shard_map/ppermute | solution.py:485
  124.1 1.9 %collective-permute-start.6 = (bf16[8,64,512]{2,1,0:T(8,128)(2,1)S(1)}, bf16[8,64,512]{2,1,0:T(8,128)(2,1)S(1)}, u32[]{:S(2)}, u32[]{:S(2)}) collective-permute-start(bf16[8,64,512]{2,1,0:T(8,128)(2,1)S(1)} %slice.12.second_own_ref), channel_id=1, source_target_pairs={{0,128},{128,0},{1,129},{129,1},{2,130},{130,2},{3,131},{131,3},{4... | collective-permute-start | bytes 1572872 | tf_op jit(solution)/shard_map/ppermute | solution.py:485
  130.8 7.7 %finish.1 = bf16[72,16,512]{2,1,0:T(8,128)(2,1)} custom-call(bf16[16,72,512]{2,1,0:T(8,128)(2,1)S(1)} %all-to-all-done.1.tokens_ref, bf16[16,72,256]{2,1,0:T(8,128)(2,1)S(1)} %all-to-all-done.2.mixed_ref, bf16[8,64,512]{2,1,0:T(8,128)(2,1)S(1)} %get-tuple-element.31.first_own_ref, bf16[8,64,512]{2,1,0:T(8,128)(2,1)S(1)} %copy-done.2, ...), custom_call_target="tpu_custom_call" | custom-call | flops 2717908992 | bytes 6094848 | tf_op jit(solution)/shard_map/finish/pallas_call | solution.py:449
  (44 shorter events, 12.4 us)
Async XLA Ops:
  6.5 30.8 %copy-start.10 = (f32[64]{0:T(128)S(1)}, f32[64]{0:T(128)}, u32[]{:S(2)}) copy-start(f32[64]{0:T(128)} %param.14) | copy-start | bytes 772
  6.5 30.8 %copy-start.12 = (f32[64]{0:T(128)S(1)}, f32[64]{0:T(128)}, u32[]{:S(2)}) copy-start(f32[64]{0:T(128)} %param.13) | copy-start | bytes 772
  6.5 30.8 %copy-start.11 = (s32[64]{0:T(128)S(1)}, s32[64]{0:T(128)}, u32[]{:S(2)}) copy-start(s32[64]{0:T(128)} %param.12) | copy-start | bytes 772
  8.2 24.1 %all-to-all-start = ((bf16[16,32,512]{2,1,0:T(8,128)(2,1)}), bf16[16,32,512]{2,1,0:T(8,128)(2,1)S(1)}, u32[]{:S(2)}, u32[]{:S(2)}) async-start(bf16[16,32,512]{2,1,0:T(8,128)(2,1)} %broadcast_in_dim.2), calls=%async_computation | async-start | bytes 1048576 | tf_op jit(solution)/shard_map/all_to_all | solution.py:480
  20.2 51.4 %all-gather.5.cloned.1.call-start = ((), (), s32[]{:S(2)}) async-start(), calls=%async_computation.3 | async-start | bytes 1179648 | tf_op jit(solution)/shard_map/all_gather | solution.py:518
  21.7 7.6 %collective-permute-start.3 = (bf16[96,512]{1,0:T(8,128)(2,1)}, bf16[96,512]{1,0:T(8,128)(2,1)S(1)}, u32[]{:S(2)}, u32[]{:S(2)}) collective-permute-start(bf16[96,512]{1,0:T(8,128)(2,1)} %pack.1.own_ref), channel_id=1, source_target_pairs={{0,256},{256,0},{1,257},{257,1},{2,258},{258,2},{3,259},{259,3},{4... | collective-permute-start | bytes 294920 | tf_op jit(solution)/shard_map/ppermute | solution.py:485
  32.3 6.5 %collective-permute-start = (bf16[2,8,32,512]{3,2,1,0:T(8,128)(2,1)S(1)}, bf16[2,8,32,512]{3,2,1,0:T(8,128)(2,1)S(1)}, u32[]{:S(2)}, u32[]{:S(2)}) collective-permute-start(bf16[2,8,32,512]{3,2,1,0:T(8,128)(2,1)S(1)} %bitcast.8), channel_id=1, source_target_pairs={{0,128},{128,0},{1,129},{129,1},{2,130},{130,2},{3,131},{131,3},{4... | collective-permute-start | bytes 1572872 | tf_op jit(solution)/shard_map/ppermute | solution.py:485
  38.9 1.7 %copy-start = (bf16[1,24,192,256]{3,2,1,0:T(8,128)(2,1)S(1)}, bf16[1,24,192,256]{3,2,1,0:T(8,128)(2,1)}, u32[]{:S(2)}) copy-start(bf16[1,24,192,256]{3,2,1,0:T(8,128)(2,1)} %param.11) | copy-start | bytes 7077892
  45.2 1.0 copy-start.7
  46.2 54.0 %all-to-all-start.1 = ((bf16[16,72,512]{2,1,0:T(8,128)(2,1)}), bf16[16,72,512]{2,1,0:T(8,128)(2,1)S(1)}, u32[]{:S(2)}, u32[]{:S(2)}) async-start(bf16[16,72,512]{2,1,0:T(8,128)(2,1)} %bitcast.2), calls=%async_computation.1 | async-start | bytes 2359296 | tf_op jit(solution)/shard_map/all_to_all | solution.py:528
  54.7 26.6 %copy-start.6 = (s32[16]{0:T(128)S(1)}, s32[16]{0:T(128)}, u32[]{:S(2)}) copy-start(s32[16]{0:T(128)} %column_offset_ref.3) | copy-start | bytes 196
  54.7 61.2 %all-gather.7.cloned.1.call-start = ((), (), s32[]{:S(2)}) async-start(), calls=%async_computation.4 | async-start | bytes 1179648 | tf_op jit(solution)/shard_map/all_gather | solution.py:524
  54.7 31.5 %collective-permute-start.1 = (bf16[5,192,512]{2,1,0:T(8,128)(2,1)}, bf16[5,192,512]{2,1,0:T(8,128)(2,1)}, u32[]{:S(2)}, u32[]{:S(2)}) collective-permute-start(bf16[5,192,512]{2,1,0:T(8,128)(2,1)} %get-tuple-element.20), channel_id=1, source_target_pairs={{0,16},{16,32},{32,48},{48,64},{64,80},{80,96},{96,112},{1,17},{17... | collective-permute-start | bytes 2949128 | tf_op jit(solution)/shard_map/ppermute | solution.py:525
  60.2 28.5 %collective-permute-start.2 = (bf16[5,192,512]{2,1,0:T(8,128)(2,1)S(1)}, bf16[5,192,512]{2,1,0:T(8,128)(2,1)}, u32[]{:S(2)}, u32[]{:S(2)}) collective-permute-start(bf16[5,192,512]{2,1,0:T(8,128)(2,1)S(1)} %get-tuple-element.21), channel_id=1, source_target_pairs={{16,0},{32,16},{48,32},{64,48},{80,64},{96,80},{112,96},{17,1},{33... | collective-permute-start | bytes 2949128 | tf_op jit(solution)/shard_map/ppermute | solution.py:526
  72.9 8.4 %collective-permute-start.4 = (bf16[8,64,512]{2,1,0:T(8,128)(2,1)S(1)}, bf16[8,64,512]{2,1,0:T(8,128)(2,1)}, u32[]{:S(2)}, u32[]{:S(2)}) collective-permute-start(bf16[8,64,512]{2,1,0:T(8,128)(2,1)S(1)} %get-tuple-element.34.weight_ref.near_ref), channel_id=1, source_target_pairs={{0,128},{128,0},{1,129},{129,1},{2,130},{130,2},{3,131},{131,3},{4... | collective-permute-start | bytes 1572872 | tf_op jit(solution)/shard_map/ppermute | solution.py:485
  79.6 9.1 %copy-start.5 = (s32[16]{0:T(128)S(1)}, s32[16]{0:T(128)}, u32[]{:S(2)}) copy-start(s32[16]{0:T(128)} %row_offset_ref.3) | copy-start | bytes 196
  81.3 1.3 copy-start.8
  100.2 28.5 %all-to-all-start.2 = ((bf16[16,72,256]{2,1,0:T(8,128)(2,1)}), bf16[16,72,256]{2,1,0:T(8,128)(2,1)S(1)}, u32[]{:S(2)}, u32[]{:S(2)}) async-start(bf16[16,72,256]{2,1,0:T(8,128)(2,1)} %attend.1), calls=%async_computation.2 | async-start | bytes 1179648 | tf_op jit(solution)/shard_map/all_to_all | solution.py:538
  116.9 9.1 %collective-permute-start.5 = (bf16[8,64,512]{2,1,0:T(8,128)(2,1)S(1)}, bf16[8,64,512]{2,1,0:T(8,128)(2,1)S(1)}, u32[]{:S(2)}, u32[]{:S(2)}) collective-permute-start(bf16[8,64,512]{2,1,0:T(8,128)(2,1)S(1)} %get-tuple-element.31.first_own_ref), channel_id=1, source_target_pairs={{0,128},{128,0},{1,129},{129,1},{2,130},{130,2},{3,131},{131,3},{4... | collective-permute-start | bytes 1572872 | tf_op jit(solution)/shard_map/ppermute | solution.py:485
  124.1 3.8 %collective-permute-start.6 = (bf16[8,64,512]{2,1,0:T(8,128)(2,1)S(1)}, bf16[8,64,512]{2,1,0:T(8,128)(2,1)S(1)}, u32[]{:S(2)}, u32[]{:S(2)}) collective-permute-start(bf16[8,64,512]{2,1,0:T(8,128)(2,1)S(1)} %slice.12.second_own_ref), channel_id=1, source_target_pairs={{0,128},{128,0},{1,129},{129,1},{2,130},{130,2},{3,131},{131,3},{4... | collective-permute-start | bytes 1572872 | tf_op jit(solution)/shard_map/ppermute | solution.py:485
  126.1 0.8 copy-start.1
  127.9 0.8 copy-start.3
  128.7 1.0 copy-start.2
  129.8 1.0 copy-start.4
  (1 other events, 0.6 us)
Sparse Core Ops, SparseCore 0:
  31.7 39.8 all-gather.4
  79.7 36.0 all-gather.6

commit v4 on v3

--- a/solution.py
+++ b/solution.py
@@ -21,8 +21,8 @@
 F32 = jnp.float32
 GROUP = 4
 ATTEND_COST = 1
-EMBED_COST = 6 * 10**9
-CHOOSE_COST = 8 * 10**9
+EMBED_COST = 3 * 10**9
+CHOOSE_COST = 3 * 10**10
 LINES = 16
 
 
@@ -35,9 +35,9 @@
 
 
 def one_hot(shape, column_of_row):
-    row = lax.broadcasted_iota(jnp.int32, shape, 0)
+    row = lax.broadcasted_iota(jnp.int32, (shape[0], 1), 0)
     column = lax.broadcasted_iota(jnp.int32, shape, 1)
-    return (column == column_of_row(row)).astype(F32).astype(BF16)
+    return jnp.where(column == column_of_row(row), 1.0, 0.0).astype(BF16)
 
 
 def layer_norm(values):
@@ -80,7 +80,11 @@
     ]
 
 
-def pack_kernel(hidden_in_ref, hidden_out_ref, attention_out_ref, attention_in_ref, packed_ref):
+def pack_kernel(
+    patch_ref, hidden_in_ref, hidden_out_ref, attention_out_ref, attention_in_ref, copies_ref, packed_ref
+):
+    for k in range(copies_ref.shape[0]):
+        copies_ref[k] = patch_ref[...]
     lines, features = LINES, packed_ref.shape[1]
     short = lines // 2
     width = attention_in_ref.shape[1] // 3
@@ -94,30 +98,32 @@
     packed_ref[5 * lines :] = jnp.concatenate([out, query], axis=0).astype(BF16)
 
 
-def pack(hidden_in, hidden_out, attention_out, attention_in):
+def pack(count, patch, hidden_in, hidden_out, attention_out, attention_in):
     return pl.pallas_call(
         pack_kernel,
-        in_specs=[pl.BlockSpec(memory_space=pltpu.VMEM)] * 4,
-        out_shape=jax.ShapeDtypeStruct((6 * LINES, hidden_out.shape[1]), BF16),
+        in_specs=[pl.BlockSpec(memory_space=pltpu.VMEM)] * 5,
+        out_shape=[
+            jax.ShapeDtypeStruct((count,) + patch.shape, BF16),
+            jax.ShapeDtypeStruct((6 * LINES, hidden_out.shape[1]), BF16),
+        ],
         name="pack",
-    )(hidden_in, hidden_out, attention_out, attention_in)
-
-
-def join_kernel(own_ref, swapped_ref, early_ref, late_ref):
-    size = 2 * LINES
-    for y, ref in enumerate((own_ref, swapped_ref)):
-        early_ref[y * size : (y + 1) * size] = ref[2 * size :]
-        early_ref[(2 + y) * size : (3 + y) * size] = ref[:size]
-        late_ref[y * size : (y + 1) * size] = ref[size : 2 * size]
-    late_ref[2 * size :] = jnp.zeros((2 * size, own_ref.shape[1]), BF16)
+    )(patch, hidden_in, hidden_out, attention_out, attention_in)
+
+
+def join_kernel(own_ref, swapped_ref, joined_ref):
+    far = 4 * LINES
+    near = own_ref.shape[0] - far
+    joined_ref[:far] = own_ref[:far]
+    joined_ref[far : 2 * far] = swapped_ref[:far]
+    joined_ref[2 * far : 2 * far + near] = own_ref[far:]
+    joined_ref[2 * far + near :] = swapped_ref[far:]
 
 
 def join(own, swapped):
-    shape = jax.ShapeDtypeStruct((8 * LINES, own.shape[1]), BF16)
     return pl.pallas_call(
         join_kernel,
         in_specs=[pl.BlockSpec(memory_space=pltpu.VMEM)] * 2,
-        out_shape=[shape, shape],
+        out_shape=jax.ShapeDtypeStruct((2 * own.shape[0], own.shape[1]), BF16),
         name="join",
     )(own, swapped)
 
@@ -132,8 +138,14 @@
     bottom_ref,
     tiles_ref,
     table_ref,
+    order_ref,
 ):
     rows = rows_ref.shape[0]
+    columns = fields_ref.shape[1]
+
+    def source(k):
+        tile, inner = k // (rows * WW), k % (rows * WW)
+        return (inner // WW) * columns + tile * WW + inner % WW
 
     @pl.when(pl.program_id(0) == 0)
     def _():
@@ -141,8 +153,8 @@
             for y in range(ref.shape[0]):
                 core = place(swapped, 0) % 2
                 table_ref[2 * y + core] = ref[y].reshape(table_ref.shape[1:])
-
-    columns = fields_ref.shape[1]
+        order_ref[...] = one_hot(order_ref.shape, source)
+
     chans = fields_ref.shape[2]
     raw = fields_ref[...].reshape(rows, P_SIZE, columns, chans)
     factor = affine_ref[0:1, :]
@@ -159,12 +171,7 @@
     top_ref[...] = by_row[:HALO]
     bottom_ref[...] = by_row[rows - HALO :]
 
-    def source(k):
-        tile, inner = k // (rows * WW), k % (rows * WW)
-        return (inner // WW) * columns + tile * WW + inner % WW
-
-    order = one_hot((rows * columns, rows * columns), source)
-    tiles_ref[...] = dot(order, tokens).astype(BF16)
+    tiles_ref[...] = dot(order_ref[...], tokens).astype(BF16)
 
 
 def embed(fields, affine, weight, other):
@@ -193,7 +200,10 @@
             jax.ShapeDtypeStruct((HALO, columns, width), BF16),
             jax.ShapeDtypeStruct((rows * columns, width), BF16),
         ],
-        scratch_shapes=[pltpu.VMEM((P_SIZE, chans, width), BF16)],
+        scratch_shapes=[
+            pltpu.VMEM((P_SIZE, chans, width), BF16),
+            pltpu.VMEM((rows * step, rows * step), BF16),
+        ],
         compiler_params=pltpu.CompilerParams(vmem_limit_bytes=16 * 1024 * 1024),
         cost_estimate=pl.CostEstimate(
             flops=EMBED_COST,
@@ -206,13 +216,13 @@
 
 def roll_matrix(columns, shift, scale):
     slots = columns // WW * PAD
-    row = lax.broadcasted_iota(jnp.int32, (slots, columns), 0)
+    row = lax.broadcasted_iota(jnp.int32, (slots, 1), 0)
     column = lax.broadcasted_iota(jnp.int32, (slots, columns), 1)
     place = row % PAD
     want = (row // PAD) * WW + place + shift
     want = jnp.where(want >= columns, want - columns, want)
-    hit = (want == column) & (place < WW)
-    return jnp.where(hit, scale, 0.0).astype(BF16)
+    want = jnp.where(place < WW, want, columns)
+    return jnp.where(column == want, scale, 0.0).astype(BF16)
 
 
 def project_kernel(
@@ -405,30 +415,29 @@
 def finish_kernel(
     tokens_ref,
     mixed_ref,
-    first_own_ref,
-    first_other_ref,
-    second_own_ref,
-    second_other_ref,
+    hidden_ref,
+    hidden_other_ref,
     near_ref,
     near_other_ref,
     encoded_ref,
     out_ref,
     first_ref,
     second_ref,
+    order_ref,
 ):
     count, cells, features = tokens_ref.shape
     lines = LINES
 
     @pl.when(pl.program_id(0) == 0)
     def _():
-        refs = first_own_ref, first_other_ref
-        collect(parts(refs, 0, lines, 2 * lines), first_ref, slice(0, features))
-        collect(parts(refs, lines, lines, 2 * lines), first_ref, slice(features, 2 * features))
-        refs = second_own_ref, second_other_ref
-        collect(parts(refs, 0, 2 * lines, 2 * lines), second_ref)
+        refs = hidden_ref, hidden_other_ref
+        collect(parts(refs, 0, lines, 4 * lines), first_ref, slice(0, features))
+        collect(parts(refs, lines, lines, 4 * lines), first_ref, slice(features, 2 * features))
+        collect(parts(refs, 2 * lines, 2 * lines, 4 * lines), second_ref)
         for spot, block in parts((near_ref, near_other_ref), lines, lines, 2 * lines):
             block = block.astype(F32)[:, : lines // 2].reshape(-1, features)
             collect([(spot, block.astype(BF16))], out_ref)
+        order_ref[...] = one_hot(order_ref.shape, lambda k: (k % count) * cells + k // count)
 
     tokens = tokens_ref[...].astype(F32).reshape(count * cells, features)
     mixed = mixed_ref[...].astype(F32).reshape(count * cells, -1).astype(BF16)
@@ -436,9 +445,7 @@
     inner = layer_norm(residual)
     expanded = jax.nn.gelu(dot(inner, first_ref[...]), approximate=True).astype(BF16)
     encoded = (residual + dot(expanded, second_ref[...])).astype(BF16)
-    size = count * cells
-    order = one_hot((size, size), lambda k: (k % count) * cells + k // count)
-    encoded_ref[...] = dot(order, encoded).astype(BF16).reshape(cells, count, features)
+    encoded_ref[...] = dot(order_ref[...], encoded).astype(BF16).reshape(cells, count, features)
 
 
 def finish(tokens, mixed, weights):
@@ -460,25 +467,16 @@
             pltpu.VMEM((width, features), BF16),
             pltpu.VMEM((features, hidden), BF16),
             pltpu.VMEM((hidden, features), BF16),
+            pltpu.VMEM((count * block, count * block), BF16),
         ],
         compiler_params=pltpu.CompilerParams(vmem_limit_bytes=24 * 1024 * 1024),
         cost_estimate=pl.CostEstimate(
             flops=2 * count * cells * features * (width + 2 * hidden),
-            bytes_accessed=count * cells * (4 * features + 2 * width) + weights[0].size * 12,
+            bytes_accessed=count * cells * (4 * features + 2 * width) + weights[0].size * 6,
             transcendentals=count * cells * hidden,
         ),
         name="finish",
     )(tokens, mixed, *weights)
-
-
-def copies(values, count):
-    return jnp.broadcast_to(values[None], (count,) + values.shape)
-
-
-def gather_far(shard):
-    sizes = lax.axis_size("y_lo"), lax.axis_size("lat")
-    found = lax.all_to_all(copies(shard, sizes[0] * sizes[1]), ("y_lo", "lat"), 0, 0, tiled=True)
-    return found.reshape(sizes + shard.shape)
 
 
 def swap(values, axis):
@@ -513,31 +511,31 @@
         ]
     )
 
-    packed = pack(hidden_in, hidden_out, attention_out, attention_in)
-    early, late = join(packed, swap(packed, "y_lo"))
-    early = lax.all_gather(early, "lat", axis=0)
-    patch = gather_far(patch_weight)
+    far = lax.axis_size("y_lo"), lats
+    patch, packed = pack(
+        far[0] * far[1], patch_weight, hidden_in, hidden_out, attention_out, attention_in
+    )
+    packed = join(packed, swap(packed, "y_lo"))
+    rest = lax.all_gather(packed, "lat", axis=0)
+    patch = lax.all_to_all(patch, ("y_lo", "lat"), 0, 0, tiled=True)
+    patch = patch.reshape(far + patch_weight.shape)
 
     rows_tokens, top, bottom, tiles = embed(fields[0], affine, patch, swap(patch, "core"))
-    _, early = after(rows_tokens, early)
-    _, late = after(rows_tokens, late)
-    late = lax.all_gather(late, "lat", axis=0)
+    _, rest = after(rows_tokens, rest)
     north = lax.ppermute(bottom, "lat", [(i, i + 1) for i in range(lats - 1)])
     south = lax.ppermute(top, "lat", [(i + 1, i) for i in range(lats - 1)])
     tiles = tiles.reshape(-1, WH * WW, features)
     tile_tokens = lax.all_to_all(tiles, ("y_hi", "x"), 0, 0, tiled=True)
 
-    half = 4 * LINES
-    near = early[:, :half]
+    near = rest[:, 8 * LINES :]
     near = near, swap(near, "core")
     window_queries, own, matrix = project(column_offset, rows_tokens, near)
     normed = choose(row_offset, north, south)
     mixed = attend(row_offset, column_offset, normed, window_queries, own, matrix)
     _, mixed = after(tile_tokens, mixed)
-    _, first, second = after(mixed, early[:, half:], late[:, :half])
+    _, hidden_weight = after(mixed, rest[:, : 8 * LINES])
     tile_mixed = lax.all_to_all(mixed, ("y_hi", "x"), 0, 0, tiled=True)
-    weights = (first, swap(first, "core"), second, swap(second, "core")) + near
-    encoded = finish(tile_tokens, tile_mixed, weights)
+    encoded = finish(tile_tokens, tile_mixed, (hidden_weight, swap(hidden_weight, "core")) + near)
     return encoded.reshape(WH, WW, -1, features).transpose(2, 0, 1, 3)
 
 

time: 146 us -> 143 us (0.979)
  waiting for transfers between devices: 28.5 us -> 35 us
  starting transfers between devices: 60.2 us -> 54 us
  local copies, waits for them, and re-layouts: 12.5 us -> 9.18 us
  Pallas kernels: 30.6 us -> 29.1 us
    all_gather x2 -> x1, waiting for transfers between devices: 16.9 us -> 5.42 us  [shards(): rest = lax.all_gather(packed, 'lat', axis=0)]
    all_to_all x1, waiting for transfers between devices: 0.76 us -> 9.72 us  [shards(): patch = lax.all_to_all(patch, ('y_lo', 'lat'), 0, 0, tiled=True)]
    all_to_all x1, waiting for transfers between devices: 0.01 us -> 8.6 us  [shards(): tile_mixed = lax.all_to_all(mixed, ('y_hi', 'x'), 0, 0, tiled=True)]
    ppermute x5 -> x4, starting transfers between devices: 24.1 us -> 19.2 us  [swap(): return lax.ppermute(values, axis, [(0, 1), (1, 0)])]
    ppermute x5 -> x4, waiting for transfers between devices: 8.26 us -> 3.55 us  [swap(): return lax.ppermute(values, axis, [(0, 1), (1, 0)])]
    ppermute x1, waiting for transfers between devices: 0.01 us -> 4.6 us  [shards(): north = lax.ppermute(bottom, 'lat', [(i, i + 1) for i in range(lats - 1)])]
    all_to_all x1, starting transfers between devices: 12 us -> 10.2 us  [shards(): patch = lax.all_to_all(patch, ('y_lo', 'lat'), 0, 0, tiled=True)]
    unnamed x26, local copies, waits for them, and re-layouts: 8.3 us -> 6.59 us
  transfers between devices with their start and end apart: 12 -> 10, of which waited for: 8 -> 7; matrix products, arithmetic and copies ran while one was open for 2% -> 2% of each run, Pallas kernels for 16% -> 15%
where the time goes in v4:
time: 143 us; the launch traced here: 141 us
  starting transfers between devices  54 us (38%)
  waiting for transfers between devices  35 us (24%)
  Pallas kernels  29.1 us (20%)
  between operations  13.6 us (10%)
  local copies, waits for them, and re-layouts  9.18 us (6%)
    ppermute x4, starting transfers between devices, swap(): return lax.ppermute(values, axis, [(0, 1), (1, 0)])  19.2 us
    all_to_all x1, starting transfers between devices, shards(): patch = lax.all_to_all(patch, ('y_lo', 'lat'), 0, 0, tiled=True)  10.2 us
    all_to_all x1, waiting for transfers between devices, shards(): patch = lax.all_to_all(patch, ('y_lo', 'lat'), 0, 0, tiled=True)  9.72 us
    all_to_all x1, starting transfers between devices, shards(): tile_tokens = lax.all_to_all(tiles, ('y_hi', 'x'), 0, 0, tiled=True)  9.3 us
    pallas_call x1, Pallas kernels, attend(): pl.pallas_call(attend_kernel, in_specs=[pl.BlockSpec(memory_space=pltpu.S...  9.19 us
    all_to_all x1, starting transfers between devices, shards(): tile_mixed = lax.all_to_all(mixed, ('y_hi', 'x'), 0, 0, tiled=True)  8.84 us
    all_to_all x1, waiting for transfers between devices, shards(): tile_mixed = lax.all_to_all(mixed, ('y_hi', 'x'), 0, 0, tiled=True)  8.6 us
    pallas_call x1, Pallas kernels, finish(): pl.pallas_call(finish_kernel, grid=(cells // block,), in_specs=[pl.BlockS...  6.71 us
  transfers between devices with their start and end apart: 10, of which 7 were waited for; matrix products, arithmetic and copies ran while one was open for 2% of the time, Pallas kernels for 15%

profile of v4, /device:TPU:1, one launch (start us, length us, event | category | flops | bytes accessed | tf_op | source)
XLA Modules:
  0.0 140.9 jit_solution(11102763111728038423)
XLA Ops:
  6.5 1.7 %pack.1 = (bf16[16,32,512]{2,1,0:T(8,128)(2,1)}, bf16[96,512]{1,0:T(8,128)(2,1)}) custom-call(bf16[32,512]{1,0:T(8,128)(2,1)} %patch_ref.1, bf16[16,1024]{1,0:T(8,128)(2,1)} %hidden_in_ref.1, bf16[32,512]{1,0:T(8,128)(2,1)} %hidden_out_ref.1, bf16[8,512]{1,0:T(8,128)(2,1)} %attention_out_ref.1, bf16[16,768]{1,0:T(8,128)(2,1)} %attention_in_ref.1), custom_call_target="tpu_custom_call" | custom-call | tf_op jit(solution)/shard_map/pack/pallas_call | solution.py:102
  8.2 4.0 %collective-permute-start.3 = (bf16[96,512]{1,0:T(8,128)(2,1)}, bf16[96,512]{1,0:T(8,128)(2,1)S(1)}, u32[]{:S(2)}, u32[]{:S(2)}) collective-permute-start(bf16[96,512]{1,0:T(8,128)(2,1)} %get-tuple-element.22.own_ref), channel_id=1, source_target_pairs={{0,256},{256,0},{1,257},{257,1},{2,258},{258,2},{3,259},{259,3},{4... | collective-permute-start | bytes 294920 | tf_op jit(solution)/shard_map/ppermute | solution.py:483
  12.3 10.2 %all-to-all-start = ((bf16[16,32,512]{2,1,0:T(8,128)(2,1)}), bf16[16,32,512]{2,1,0:T(8,128)(2,1)S(1)}, u32[]{:S(2)}, u32[]{:S(2)}) async-start(bf16[16,32,512]{2,1,0:T(8,128)(2,1)} %get-tuple-element.17), calls=%async_computation | async-start | bytes 1048576 | tf_op jit(solution)/shard_map/all_to_all | solution.py:520
  23.1 1.6 %join.1 = bf16[192,512]{1,0:T(8,128)(2,1)} custom-call(bf16[96,512]{1,0:T(8,128)(2,1)} %get-tuple-element.22.own_ref, bf16[96,512]{1,0:T(8,128)(2,1)} %copy-done.9), custom_call_target="tpu_custom_call" | custom-call | tf_op jit(solution)/shard_map/join/pallas_call | solution.py:123
  24.8 9.7 %all-to-all-done = bf16[16,32,512]{2,1,0:T(8,128)(2,1)S(1)} async-done(((bf16[16,32,512]{2,1,0:T(8,128)(2,1)}), bf16[16,32,512]{2,1,0:T(8,128)(2,1)S(1)}, u32[]{:S(2)}, u32[]{:S(2)}) %all-to-all-start) | async-done | bytes 524320 | tf_op jit(solution)/shard_map/all_to_all | solution.py:520
  34.5 5.2 %collective-permute-start = (bf16[2,8,32,512]{3,2,1,0:T(8,128)(2,1)S(1)}, bf16[2,8,32,512]{3,2,1,0:T(8,128)(2,1)S(1)}, u32[]{:S(2)}, u32[]{:S(2)}) collective-permute-start(bf16[2,8,32,512]{3,2,1,0:T(8,128)(2,1)S(1)} %bitcast.7), channel_id=1, source_target_pairs={{0,128},{128,0},{1,129},{129,1},{2,130},{130,2},{3,131},{131,3},{4... | collective-permute-start | bytes 1572872 | tf_op jit(solution)/shard_map/ppermute | solution.py:483
  41.2 1.7 %copy-done = bf16[1,24,192,256]{3,2,1,0:T(8,128)(2,1)S(1)} copy-done((bf16[1,24,192,256]{3,2,1,0:T(8,128)(2,1)S(1)}, bf16[1,24,192,256]{3,2,1,0:T(8,128)(2,1)}, u32[]{:S(2)}) %copy-start) | copy-done | bytes 2359320
  42.9 4.5 %embed.1 = (bf16[6,192,512]{2,1,0:T(8,128)(2,1)S(1)}, bf16[5,192,512]{2,1,0:T(8,128)(2,1)S(1)}, bf16[5,192,512]{2,1,0:T(8,128)(2,1)}, bf16[1152,512]{1,0:T(8,128)(2,1)}) custom-call(bf16[24,192,256]{2,1,0:T(8,128)(2,1)S(1)} %bitcast.9, f32[2,256]{1,0:T(2,128)S(1)} %pad_maximum_fusion.affine_ref, bf16[2,8,32,512]{3,2,1,0:T(8,128)(2,1)S(1)} %bitcast.8, ...), custom_call_target="tpu_custom_call" | custom-call | flops 3000000000 | tf_op jit(solution)/shard_map/embed/pallas_call | solution.py:182
  48.4 5.1 %collective-permute-start.1 = (bf16[5,192,512]{2,1,0:T(8,128)(2,1)}, bf16[5,192,512]{2,1,0:T(8,128)(2,1)}, u32[]{:S(2)}, u32[]{:S(2)}) collective-permute-start(bf16[5,192,512]{2,1,0:T(8,128)(2,1)} %get-tuple-element.19), channel_id=1, source_target_pairs={{0,16},{16,32},{32,48},{48,64},{64,80},{80,96},{96,112},{1,17},{17... | collective-permute-start | bytes 2949128 | tf_op jit(solution)/shard_map/ppermute | solution.py:525
  53.6 1.3 collective-permute-start.2
  54.9 9.3 %all-to-all-start.1 = ((bf16[16,72,512]{2,1,0:T(8,128)(2,1)}), bf16[16,72,512]{2,1,0:T(8,128)(2,1)S(1)}, u32[]{:S(2)}, u32[]{:S(2)}) async-start(bf16[16,72,512]{2,1,0:T(8,128)(2,1)} %bitcast.2), calls=%async_computation.1 | async-start | bytes 2359296 | tf_op jit(solution)/shard_map/all_to_all | solution.py:528
  64.2 5.4 %all-gather.3.cloned.1.call-done = bf16[1536,512]{1,0:T(8,128)(2,1)} async-done(((bf16[192,512]{1,0:T(8,128)(2,1)}), bf16[1536,512]{1,0:T(8,128)(2,1)}) %all-gather.3.cloned.1.call-update) | async-done | bytes 1572880 | tf_op jit(solution)/shard_map/all_gather | solution.py:519
  70.7 6.9 %collective-permute-start.4 = (bf16[8,64,512]{2,1,0:T(8,128)(2,1)S(1)}, bf16[8,64,512]{2,1,0:T(8,128)(2,1)S(1)}, u32[]{:S(2)}, u32[]{:S(2)}) collective-permute-start(bf16[8,64,512]{2,1,0:T(8,128)(2,1)S(1)} %slice.6.weight_ref.near_ref), channel_id=1, source_target_pairs={{0,128},{128,0},{1,129},{129,1},{2,130},{130,2},{3,131},{131,3},{4... | collective-permute-start | bytes 1572872 | tf_op jit(solution)/shard_map/ppermute | solution.py:483
  77.6 4.6 %collective-permute-done.1.north_ref = bf16[5,192,512]{2,1,0:T(8,128)(2,1)} collective-permute-done((bf16[5,192,512]{2,1,0:T(8,128)(2,1)}, bf16[5,192,512]{2,1,0:T(8,128)(2,1)}, u32[]{:S(2)}, u32[]{:S(2)}) %collective-permute-start.1) | collective-permute-done | bytes 983072 | tf_op jit(solution)/shard_map/ppermute | solution.py:525
  82.2 3.1 %collective-permute-done.2.south_ref = bf16[5,192,512]{2,1,0:T(8,128)(2,1)} collective-permute-done((bf16[5,192,512]{2,1,0:T(8,128)(2,1)S(1)}, bf16[5,192,512]{2,1,0:T(8,128)(2,1)}, u32[]{:S(2)}, u32[]{:S(2)}) %collective-permute-start.2) | collective-permute-done | bytes 983072 | tf_op jit(solution)/shard_map/ppermute | solution.py:526
  85.2 2.3 %choose.1.normed_ref = bf16[6,192,512]{2,1,0:T(8,128)(2,1)S(1)} custom-call(s32[16]{0:T(128)S(1)} %copy-done.5, bf16[5,192,512]{2,1,0:T(8,128)(2,1)} %collective-permute-done.1.north_ref, bf16[5,192,512]{2,1,0:T(8,128)(2,1)} %collective-permute-done.2.south_ref), custom_call_target="tpu_custom_call" | custom-call | flops 30000001024 | tf_op jit(solution)/shard_map/choose/pallas_call | solution.py:294
  87.6 3.1 %project.1 = (bf16[6,256,256]{2,1,0:T(8,128)(2,1)S(1)}, bf16[6,256,512]{2,1,0:T(8,128)(2,1)S(1)}, bf16[512,512]{1,0:T(8,128)(2,1)S(1)}) custom-call(s32[16]{0:T(128)S(1)} %copy-done.6, bf16[6,192,512]{2,1,0:T(8,128)(2,1)S(1)} %copy-done.8, bf16[8,64,512]{2,1,0:T(8,128)(2,1)S(1)} %slice.6.weight_ref.near_ref, ...), custom_call_target="tpu_custom_call" | custom-call | flops 1358954496 | bytes 3538944 | tf_op jit(solution)/shard_map/project/pallas_call | solution.py:261
  90.7 9.2 %attend.1 = bf16[16,72,256]{2,1,0:T(8,128)(2,1)} custom-call(s32[16]{0:T(128)S(1)} %copy-done.5, s32[16]{0:T(128)S(1)} %copy-done.6, bf16[6,192,512]{2,1,0:T(8,128)(2,1)S(1)} %choose.1.normed_ref, bf16[6,256,256]{2,1,0:T(8,128)(2,1)S(1)} %get-tuple-element.24.query_ref, bf16[6,256,512]{2,1,0:T(8,128)(2,1)S(1)} %get-tuple-element.25.own_ref, ...), custom_call_target="tpu_custom_call" | custom-call | flops 2113929216 | bytes 4325376 | tf_op jit(solution)/shard_map/attend/pallas_call | solution.py:396
  99.9 8.8 %all-to-all-start.2 = ((bf16[16,72,256]{2,1,0:T(8,128)(2,1)}), bf16[16,72,256]{2,1,0:T(8,128)(2,1)S(1)}, u32[]{:S(2)}, u32[]{:S(2)}) async-start(bf16[16,72,256]{2,1,0:T(8,128)(2,1)} %attend.1), calls=%async_computation.2 | async-start | bytes 1179648 | tf_op jit(solution)/shard_map/all_to_all | solution.py:537
  108.8 1.3 slice.7.hidden_ref
  110.1 3.1 %collective-permute-start.5 = (bf16[8,128,512]{2,1,0:T(8,128)(2,1)S(1)}, bf16[8,128,512]{2,1,0:T(8,128)(2,1)S(1)}, u32[]{:S(2)}, u32[]{:S(2)}) collective-permute-start(bf16[8,128,512]{2,1,0:T(8,128)(2,1)S(1)} %slice.7.hidden_ref), channel_id=1, source_target_pairs={{0,128},{128,0},{1,129},{129,1},{2,130},{130,2},{3,131},{131,3},{4... | collective-permute-start | bytes 3145736 | tf_op jit(solution)/shard_map/ppermute | solution.py:483
  113.2 2.3 %collective-permute-done.5.hidden_other_ref = bf16[8,128,512]{2,1,0:T(8,128)(2,1)S(1)} collective-permute-done((bf16[8,128,512]{2,1,0:T(8,128)(2,1)S(1)}, bf16[8,128,512]{2,1,0:T(8,128)(2,1)S(1)}, u32[]{:S(2)}, u32[]{:S(2)}) %collective-permute-start.5) | collective-permute-done | bytes 1048608 | tf_op jit(solution)/shard_map/ppermute | solution.py:483
  116.5 8.6 %all-to-all-done.2.mixed_ref = bf16[16,72,256]{2,1,0:T(8,128)(2,1)S(1)} async-done(((bf16[16,72,256]{2,1,0:T(8,128)(2,1)}), bf16[16,72,256]{2,1,0:T(8,128)(2,1)S(1)}, u32[]{:S(2)}, u32[]{:S(2)}) %all-to-all-start.2) | async-done | bytes 589856 | tf_op jit(solution)/shard_map/all_to_all | solution.py:537
  127.4 6.7 %finish.1 = bf16[72,16,512]{2,1,0:T(8,128)(2,1)} custom-call(bf16[16,72,512]{2,1,0:T(8,128)(2,1)S(1)} %all-to-all-done.1.tokens_ref, bf16[16,72,256]{2,1,0:T(8,128)(2,1)S(1)} %all-to-all-done.2.mixed_ref, bf16[8,128,512]{2,1,0:T(8,128)(2,1)S(1)} %slice.7.hidden_ref, bf16[8,128,512]{2,1,0:T(8,128)(2,1)S(1)} %copy-done.2, ...), custom_call_target="tpu_custom_call" | custom-call | flops 2717908992 | bytes 6094848 | tf_op jit(solution)/shard_map/finish/pallas_call | solution.py:456
  (38 shorter events, 7.5 us)
Async XLA Ops:
  6.5 33.2 %copy-start.10 = (f32[64]{0:T(128)S(1)}, f32[64]{0:T(128)}, u32[]{:S(2)}) copy-start(f32[64]{0:T(128)} %param.14) | copy-start | bytes 772
  6.5 33.2 %copy-start.12 = (f32[64]{0:T(128)S(1)}, f32[64]{0:T(128)}, u32[]{:S(2)}) copy-start(f32[64]{0:T(128)} %param.13) | copy-start | bytes 772
  6.5 33.2 %copy-start.11 = (s32[64]{0:T(128)S(1)}, s32[64]{0:T(128)}, u32[]{:S(2)}) copy-start(s32[64]{0:T(128)} %param.12) | copy-start | bytes 772
  8.2 14.2 %collective-permute-start.3 = (bf16[96,512]{1,0:T(8,128)(2,1)}, bf16[96,512]{1,0:T(8,128)(2,1)S(1)}, u32[]{:S(2)}, u32[]{:S(2)}) collective-permute-start(bf16[96,512]{1,0:T(8,128)(2,1)} %get-tuple-element.22.own_ref), channel_id=1, source_target_pairs={{0,256},{256,0},{1,257},{257,1},{2,258},{258,2},{3,259},{259,3},{4... | collective-permute-start | bytes 294920 | tf_op jit(solution)/shard_map/ppermute | solution.py:483
  12.3 22.2 %all-to-all-start = ((bf16[16,32,512]{2,1,0:T(8,128)(2,1)}), bf16[16,32,512]{2,1,0:T(8,128)(2,1)S(1)}, u32[]{:S(2)}, u32[]{:S(2)}) async-start(bf16[16,32,512]{2,1,0:T(8,128)(2,1)} %get-tuple-element.17), calls=%async_computation | async-start | bytes 1048576 | tf_op jit(solution)/shard_map/all_to_all | solution.py:520
  22.4 47.2 %all-gather.3.cloned.1.call-start = ((), (), s32[]{:S(2)}) async-start(), calls=%async_computation.3 | async-start | bytes 1769472 | tf_op jit(solution)/shard_map/all_gather | solution.py:519
  22.5 0.6 copy-start.9
  34.5 6.8 %collective-permute-start = (bf16[2,8,32,512]{3,2,1,0:T(8,128)(2,1)S(1)}, bf16[2,8,32,512]{3,2,1,0:T(8,128)(2,1)S(1)}, u32[]{:S(2)}, u32[]{:S(2)}) collective-permute-start(bf16[2,8,32,512]{3,2,1,0:T(8,128)(2,1)S(1)} %bitcast.7), channel_id=1, source_target_pairs={{0,128},{128,0},{1,129},{129,1},{2,130},{130,2},{3,131},{131,3},{4... | collective-permute-start | bytes 1572872 | tf_op jit(solution)/shard_map/ppermute | solution.py:483
  41.2 1.7 %copy-start = (bf16[1,24,192,256]{3,2,1,0:T(8,128)(2,1)S(1)}, bf16[1,24,192,256]{3,2,1,0:T(8,128)(2,1)}, u32[]{:S(2)}) copy-start(bf16[1,24,192,256]{3,2,1,0:T(8,128)(2,1)} %param.11) | copy-start | bytes 7077892
  47.4 1.0 copy-start.7
  48.4 33.7 %collective-permute-start.1 = (bf16[5,192,512]{2,1,0:T(8,128)(2,1)}, bf16[5,192,512]{2,1,0:T(8,128)(2,1)}, u32[]{:S(2)}, u32[]{:S(2)}) collective-permute-start(bf16[5,192,512]{2,1,0:T(8,128)(2,1)} %get-tuple-element.19), channel_id=1, source_target_pairs={{0,16},{16,32},{32,48},{48,64},{64,80},{80,96},{96,112},{1,17},{17... | collective-permute-start | bytes 2949128 | tf_op jit(solution)/shard_map/ppermute | solution.py:525
  53.6 31.7 %collective-permute-start.2 = (bf16[5,192,512]{2,1,0:T(8,128)(2,1)S(1)}, bf16[5,192,512]{2,1,0:T(8,128)(2,1)}, u32[]{:S(2)}, u32[]{:S(2)}) collective-permute-start(bf16[5,192,512]{2,1,0:T(8,128)(2,1)S(1)} %get-tuple-element.20), channel_id=1, source_target_pairs={{16,0},{32,16},{48,32},{64,48},{80,64},{96,80},{112,96},{17,1},{33... | collective-permute-start | bytes 2949128 | tf_op jit(solution)/shard_map/ppermute | solution.py:526
  54.8 30.4 %copy-start.5 = (s32[16]{0:T(128)S(1)}, s32[16]{0:T(128)}, u32[]{:S(2)}) copy-start(s32[16]{0:T(128)} %row_offset_ref.3) | copy-start | bytes 196
  54.9 45.1 %all-to-all-start.1 = ((bf16[16,72,512]{2,1,0:T(8,128)(2,1)}), bf16[16,72,512]{2,1,0:T(8,128)(2,1)S(1)}, u32[]{:S(2)}, u32[]{:S(2)}) async-start(bf16[16,72,512]{2,1,0:T(8,128)(2,1)} %bitcast.2), calls=%async_computation.1 | async-start | bytes 2359296 | tf_op jit(solution)/shard_map/all_to_all | solution.py:528
  70.7 16.9 %copy-start.6 = (s32[16]{0:T(128)S(1)}, s32[16]{0:T(128)}, u32[]{:S(2)}) copy-start(s32[16]{0:T(128)} %column_offset_ref.3) | copy-start | bytes 196
  70.7 16.9 %copy-start.8 = (bf16[6,192,512]{2,1,0:T(8,128)(2,1)S(1)}, bf16[6,192,512]{2,1,0:T(8,128)(2,1)}, u32[]{:S(2)}) copy-start(bf16[6,192,512]{2,1,0:T(8,128)(2,1)} %copy-done.7) | copy-start | bytes 3538948
  70.7 16.8 %collective-permute-start.4 = (bf16[8,64,512]{2,1,0:T(8,128)(2,1)S(1)}, bf16[8,64,512]{2,1,0:T(8,128)(2,1)S(1)}, u32[]{:S(2)}, u32[]{:S(2)}) collective-permute-start(bf16[8,64,512]{2,1,0:T(8,128)(2,1)S(1)} %slice.6.weight_ref.near_ref), channel_id=1, source_target_pairs={{0,128},{128,0},{1,129},{129,1},{2,130},{130,2},{3,131},{131,3},{4... | collective-permute-start | bytes 1572872 | tf_op jit(solution)/shard_map/ppermute | solution.py:483
  87.6 3.2 %copy-start.3 = (bf16[8,64,512]{2,1,0:T(8,128)(2,1)}, bf16[8,64,512]{2,1,0:T(8,128)(2,1)S(1)}, u32[]{:S(2)}) copy-start(bf16[8,64,512]{2,1,0:T(8,128)(2,1)S(1)} %collective-permute-done.4.other_ref.near_other_ref) | copy-start | bytes 1572868
  99.9 25.2 %all-to-all-start.2 = ((bf16[16,72,256]{2,1,0:T(8,128)(2,1)}), bf16[16,72,256]{2,1,0:T(8,128)(2,1)S(1)}, u32[]{:S(2)}, u32[]{:S(2)}) async-start(bf16[16,72,256]{2,1,0:T(8,128)(2,1)} %attend.1), calls=%async_computation.2 | async-start | bytes 1179648 | tf_op jit(solution)/shard_map/all_to_all | solution.py:537
  110.1 5.4 %collective-permute-start.5 = (bf16[8,128,512]{2,1,0:T(8,128)(2,1)S(1)}, bf16[8,128,512]{2,1,0:T(8,128)(2,1)S(1)}, u32[]{:S(2)}, u32[]{:S(2)}) collective-permute-start(bf16[8,128,512]{2,1,0:T(8,128)(2,1)S(1)} %slice.7.hidden_ref), channel_id=1, source_target_pairs={{0,128},{128,0},{1,129},{129,1},{2,130},{130,2},{3,131},{131,3},{4... | collective-permute-start | bytes 3145736 | tf_op jit(solution)/shard_map/ppermute | solution.py:483
  115.5 1.0 copy-start.1
  125.1 1.2 copy-start.2
  126.3 1.0 copy-start.4
Sparse Core Ops, SparseCore 0:
  25.3 44.1 all-gather.2

commit v5 on v4

--- a/solution.py
+++ b/solution.py
@@ -20,9 +20,8 @@
 BF16 = jnp.bfloat16
 F32 = jnp.float32
 GROUP = 4
-ATTEND_COST = 1
-EMBED_COST = 3 * 10**9
-CHOOSE_COST = 3 * 10**10
+ATTEND_COST = 5
+EMBED_COST = 8 * 10**9
 LINES = 16
 
 
@@ -133,14 +132,13 @@
     affine_ref,
     weight_ref,
     other_ref,
-    rows_ref,
     top_ref,
     bottom_ref,
     tiles_ref,
     table_ref,
     order_ref,
 ):
-    rows = rows_ref.shape[0]
+    rows = fields_ref.shape[0] // P_SIZE
     columns = fields_ref.shape[1]
 
     def source(k):
@@ -167,7 +165,6 @@
         total = product if total is None else total + product
     tokens = total.astype(BF16)
     by_row = tokens.reshape(rows, columns, -1)
-    rows_ref[...] = by_row
     top_ref[...] = by_row[:HALO]
     bottom_ref[...] = by_row[rows - HALO :]
 
@@ -189,13 +186,11 @@
             pl.BlockSpec(weight.shape, lambda g: (0,) * weight.ndim),
         ],
         out_specs=[
-            pl.BlockSpec((rows, step, width), lambda g: (0, g, 0)),
             pl.BlockSpec((HALO, step, width), lambda g: (0, g, 0)),
             pl.BlockSpec((HALO, step, width), lambda g: (0, g, 0)),
             pl.BlockSpec((rows * step, width), lambda g: (g, 0)),
         ],
         out_shape=[
-            jax.ShapeDtypeStruct((rows, columns, width), BF16),
             jax.ShapeDtypeStruct((HALO, columns, width), BF16),
             jax.ShapeDtypeStruct((HALO, columns, width), BF16),
             jax.ShapeDtypeStruct((rows * columns, width), BF16),
@@ -227,7 +222,8 @@
 
 def project_kernel(
     column_offset_ref,
-    rows_ref,
+    top_ref,
+    bottom_ref,
     weight_ref,
     other_ref,
     query_ref,
@@ -235,7 +231,8 @@
     matrix_ref,
     query_matrix_ref,
 ):
-    rows, columns, features = rows_ref.shape
+    rows = query_ref.shape[0]
+    columns, features = top_ref.shape[1:]
     width = query_ref.shape[-1]
     shift = column_offset_ref[position()["lon"]]
     refs = weight_ref, other_ref
@@ -248,20 +245,22 @@
     to_windows = roll_matrix(columns, shift, 1.0)
     to_queries = roll_matrix(columns, shift, HEAD_DIM**-0.5)
     for row in range(rows):
-        normed = layer_norm(rows_ref[row].astype(F32))
+        values = top_ref[row] if row < HALO else bottom_ref[row - rows + HALO]
+        normed = layer_norm(values.astype(F32))
         projected = dot(normed, matrix).astype(BF16)
         query_ref[row] = dot(to_queries, projected[:, :width]).astype(BF16)
         key_value_ref[row] = dot(to_windows, projected[:, width:]).astype(BF16)
 
 
-def project(column_offset, rows_tokens, weights):
-    rows, columns, features = rows_tokens.shape
+def project(column_offset, top, bottom, weights):
+    rows = WH
+    columns, features = top.shape[1:]
     width = HEADS * HEAD_DIM
     slots = columns // WW * PAD
     return pl.pallas_call(
         project_kernel,
         in_specs=[pl.BlockSpec(memory_space=pltpu.SMEM)]
-        + [pl.BlockSpec(memory_space=pltpu.VMEM)] * 3,
+        + [pl.BlockSpec(memory_space=pltpu.VMEM)] * 4,
         out_shape=[
             jax.ShapeDtypeStruct((rows, slots, width), BF16),
             jax.ShapeDtypeStruct((rows, slots, 2 * width), BF16),
@@ -275,36 +274,14 @@
             transcendentals=0,
         ),
         name="project",
-    )(column_offset, rows_tokens, *weights)
-
-
-def choose_kernel(row_offset_ref, north_ref, south_ref, normed_ref):
-    rows = normed_ref.shape[0]
-    split = row_offset_ref[position()["lon"]]
-    for slot in range(rows):
-        north = north_ref[jnp.minimum(split - 1 + slot, HALO - 1)]
-        south = south_ref[jnp.maximum(slot - (rows - split), 0)]
-        values = jnp.where(slot < rows - split, north.astype(F32), south.astype(F32))
-        normed_ref[slot] = layer_norm(values)
-
-
-def choose(row_offset, north, south):
-    columns, features = north.shape[1:]
-    vmem = pl.BlockSpec(memory_space=pltpu.VMEM)
-    return pl.pallas_call(
-        choose_kernel,
-        in_specs=[pl.BlockSpec(memory_space=pltpu.SMEM), vmem, vmem],
-        out_shape=jax.ShapeDtypeStruct((WH, columns, features), BF16),
-        compiler_params=pltpu.CompilerParams(vmem_limit_bytes=8 * 1024 * 1024),
-        cost_estimate=pl.CostEstimate(flops=CHOOSE_COST, bytes_accessed=0, transcendentals=0),
-        name="choose",
-    )(row_offset, north, south)
+    )(column_offset, top, bottom, *weights)
 
 
 def attend_kernel(
     row_offset_ref,
     column_offset_ref,
-    normed_ref,
+    north_ref,
+    south_ref,
     query_ref,
     own_ref,
     matrix_ref,
@@ -313,7 +290,7 @@
     made_ref,
 ):
     rows, slots, width = query_ref.shape
-    columns = normed_ref.shape[1]
+    columns = north_ref.shape[1]
     windows = slots // PAD
     here = position()
     lat, last = here["lat"], here["last"]
@@ -329,8 +306,12 @@
     matrix = matrix_ref[...]
     to_windows = roll_matrix(columns, shift, 1.0)
     for slot in range(rows):
-        projected = dot(normed_ref[slot], matrix).astype(BF16)
-        spot = jnp.where(slot < rows - split, slot, half + slot)
+        above = slot < rows - split
+        north = north_ref[jnp.minimum(split - 1 + slot, HALO - 1)]
+        south = south_ref[jnp.maximum(slot - (rows - split), 0)]
+        values = jnp.where(above, north.astype(F32), south.astype(F32))
+        projected = dot(layer_norm(values), matrix).astype(BF16)
+        spot = jnp.where(above, slot, half + slot)
         keys_ref[spot] = dot(to_windows, projected).astype(BF16)
 
     shape = (rows, PAD, half * PAD)
@@ -388,14 +369,14 @@
         mixed_ref[j] = dot(back, pair.reshape(rows * 2 * PAD, width)).astype(BF16)
 
 
-def attend(row_offset, column_offset, normed, queries, own, matrix):
+def attend(row_offset, column_offset, north, south, queries, own, matrix):
     rows, slots, width = queries.shape
     windows = slots // PAD
-    columns, features = normed.shape[1:]
+    columns, features = north.shape[1:]
     vmem = pl.BlockSpec(memory_space=pltpu.VMEM)
     return pl.pallas_call(
         attend_kernel,
-        in_specs=[pl.BlockSpec(memory_space=pltpu.SMEM)] * 2 + [vmem] * 4,
+        in_specs=[pl.BlockSpec(memory_space=pltpu.SMEM)] * 2 + [vmem] * 5,
         out_shape=jax.ShapeDtypeStruct((windows, rows * WW, width), BF16),
         scratch_shapes=[
             pltpu.VMEM((2 * BAND, slots, 2 * width), BF16),
@@ -405,11 +386,11 @@
         cost_estimate=pl.CostEstimate(
             flops=ATTEND_COST * 2 * rows * columns * (features + slots) * 2 * width
             + ATTEND_COST * 4 * windows * HEADS * rows * PAD * 2 * rows * PAD * width,
-            bytes_accessed=normed.size * 2 + rows * slots * 4 * width * 2,
+            bytes_accessed=2 * north.size * 2 + rows * slots * 4 * width * 2,
             transcendentals=windows * HEADS * rows * PAD * 2 * rows * PAD,
         ),
         name="attend",
-    )(row_offset, column_offset, normed, queries, own, matrix)
+    )(row_offset, column_offset, north, south, queries, own, matrix)
 
 
 def finish_kernel(
@@ -520,8 +501,8 @@
     patch = lax.all_to_all(patch, ("y_lo", "lat"), 0, 0, tiled=True)
     patch = patch.reshape(far + patch_weight.shape)
 
-    rows_tokens, top, bottom, tiles = embed(fields[0], affine, patch, swap(patch, "core"))
-    _, rest = after(rows_tokens, rest)
+    top, bottom, tiles = embed(fields[0], affine, patch, swap(patch, "core"))
+    _, rest = after(top, rest)
     north = lax.ppermute(bottom, "lat", [(i, i + 1) for i in range(lats - 1)])
     south = lax.ppermute(top, "lat", [(i + 1, i) for i in range(lats - 1)])
     tiles = tiles.reshape(-1, WH * WW, features)
@@ -529,9 +510,8 @@
 
     near = rest[:, 8 * LINES :]
     near = near, swap(near, "core")
-    window_queries, own, matrix = project(column_offset, rows_tokens, near)
-    normed = choose(row_offset, north, south)
-    mixed = attend(row_offset, column_offset, normed, window_queries, own, matrix)
+    window_queries, own, matrix = project(column_offset, top, bottom, near)
+    mixed = attend(row_offset, column_offset, north, south, window_queries, own, matrix)
     _, mixed = after(tile_tokens, mixed)
     _, hidden_weight = after(mixed, rest[:, : 8 * LINES])
     tile_mixed = lax.all_to_all(mixed, ("y_hi", "x"), 0, 0, tiled=True)

time: 143 us -> 142 us (level)
  the two profiles are of different devices: /device:TPU:1 before, /device:TPU:8 now
where the time goes in v5:
time: 142 us; the launch traced here: 141 us
  starting transfers between devices  45.6 us (32%)
  waiting for transfers between devices  44.3 us (31%)
  Pallas kernels  29 us (20%)
  between operations  13.6 us (10%)
  local copies, waits for them, and re-layouts  8.14 us (6%)
    ppermute x4, starting transfers between devices, swap(): return lax.ppermute(values, axis, [(0, 1), (1, 0)])  13.5 us
    all_to_all x1, waiting for transfers between devices, shards(): tile_mixed = lax.all_to_all(mixed, ('y_hi', 'x'), 0, 0, tiled=True)  12.5 us
    all_to_all x1, waiting for transfers between devices, shards(): patch = lax.all_to_all(patch, ('y_lo', 'lat'), 0, 0, tiled=True)  12.2 us
    pallas_call x1, Pallas kernels, attend(): pl.pallas_call(attend_kernel, in_specs=[pl.BlockSpec(memory_space=pltpu.S...  10.6 us
    all_to_all x1, starting transfers between devices, shards(): tile_tokens = lax.all_to_all(tiles, ('y_hi', 'x'), 0, 0, tiled=True)  9.71 us
    all_to_all x1, starting transfers between devices, shards(): tile_mixed = lax.all_to_all(mixed, ('y_hi', 'x'), 0, 0, tiled=True)  9.06 us
    all_gather x1, waiting for transfers between devices, shards(): rest = lax.all_gather(packed, 'lat', axis=0)  7.28 us
    pallas_call x1, Pallas kernels, finish(): pl.pallas_call(finish_kernel, grid=(cells // block,), in_specs=[pl.BlockS...  6.7 us
  transfers between devices with their start and end apart: 10, of which 7 were waited for; matrix products, arithmetic and copies ran while one was open for 2% of the time, Pallas kernels for 15%

profile of v5, /device:TPU:8, one launch (start us, length us, event | category | flops | bytes accessed | tf_op | source)
XLA Modules:
  0.0 140.6 jit_solution(10083449717801634324)
XLA Ops:
  6.5 1.7 %pack.1 = (bf16[16,32,512]{2,1,0:T(8,128)(2,1)}, bf16[96,512]{1,0:T(8,128)(2,1)}) custom-call(bf16[32,512]{1,0:T(8,128)(2,1)} %patch_ref.1, bf16[16,1024]{1,0:T(8,128)(2,1)} %hidden_in_ref.1, bf16[32,512]{1,0:T(8,128)(2,1)} %hidden_out_ref.1, bf16[8,512]{1,0:T(8,128)(2,1)} %attention_out_ref.1, bf16[16,768]{1,0:T(8,128)(2,1)} %attention_in_ref.1), custom_call_target="tpu_custom_call" | custom-call | tf_op jit(solution)/shard_map/pack/pallas_call | solution.py:101
  8.2 7.7 %collective-permute-start.3 = (bf16[96,512]{1,0:T(8,128)(2,1)}, bf16[96,512]{1,0:T(8,128)(2,1)S(1)}, u32[]{:S(2)}, u32[]{:S(2)}) collective-permute-start(bf16[96,512]{1,0:T(8,128)(2,1)} %get-tuple-element.20.own_ref), channel_id=1, source_target_pairs={{0,256},{256,0},{1,257},{257,1},{2,258},{258,2},{3,259},{259,3},{4... | collective-permute-start | bytes 294920 | tf_op jit(solution)/shard_map/ppermute | solution.py:464
  16.0 6.5 %all-to-all-start = ((bf16[16,32,512]{2,1,0:T(8,128)(2,1)}), bf16[16,32,512]{2,1,0:T(8,128)(2,1)S(1)}, u32[]{:S(2)}, u32[]{:S(2)}) async-start(bf16[16,32,512]{2,1,0:T(8,128)(2,1)} %get-tuple-element.16), calls=%async_computation | async-start | bytes 1048576 | tf_op jit(solution)/shard_map/all_to_all | solution.py:501
  23.2 1.6 %join.1 = bf16[192,512]{1,0:T(8,128)(2,1)} custom-call(bf16[96,512]{1,0:T(8,128)(2,1)} %get-tuple-element.20.own_ref, bf16[96,512]{1,0:T(8,128)(2,1)} %copy-done.7), custom_call_target="tpu_custom_call" | custom-call | tf_op jit(solution)/shard_map/join/pallas_call | solution.py:122
  24.9 12.2 %all-to-all-done = bf16[16,32,512]{2,1,0:T(8,128)(2,1)S(1)} async-done(((bf16[16,32,512]{2,1,0:T(8,128)(2,1)}), bf16[16,32,512]{2,1,0:T(8,128)(2,1)S(1)}, u32[]{:S(2)}, u32[]{:S(2)}) %all-to-all-start) | async-done | bytes 524320 | tf_op jit(solution)/shard_map/all_to_all | solution.py:501
  37.0 1.9 %collective-permute-start = (bf16[2,8,32,512]{3,2,1,0:T(8,128)(2,1)S(1)}, bf16[2,8,32,512]{3,2,1,0:T(8,128)(2,1)S(1)}, u32[]{:S(2)}, u32[]{:S(2)}) collective-permute-start(bf16[2,8,32,512]{3,2,1,0:T(8,128)(2,1)S(1)} %bitcast.7), channel_id=1, source_target_pairs={{0,128},{128,0},{1,129},{129,1},{2,130},{130,2},{3,131},{131,3},{4... | collective-permute-start | bytes 1572872 | tf_op jit(solution)/shard_map/ppermute | solution.py:464
  39.2 1.6 %collective-permute-done.other_ref = bf16[2,8,32,512]{3,2,1,0:T(8,128)(2,1)S(1)} collective-permute-done((bf16[2,8,32,512]{3,2,1,0:T(8,128)(2,1)S(1)}, bf16[2,8,32,512]{3,2,1,0:T(8,128)(2,1)S(1)}, u32[]{:S(2)}, u32[]{:S(2)}) %collective-permute-start) | collective-permute-done | bytes 524320 | tf_op jit(solution)/shard_map/ppermute | solution.py:464
  40.8 1.7 %copy-done = bf16[1,24,192,256]{3,2,1,0:T(8,128)(2,1)S(1)} copy-done((bf16[1,24,192,256]{3,2,1,0:T(8,128)(2,1)S(1)}, bf16[1,24,192,256]{3,2,1,0:T(8,128)(2,1)}, u32[]{:S(2)}) %copy-start) | copy-done | bytes 2359320
  42.5 4.4 %embed.1 = (bf16[5,192,512]{2,1,0:T(8,128)(2,1)}, bf16[5,192,512]{2,1,0:T(8,128)(2,1)S(1)}, bf16[1152,512]{1,0:T(8,128)(2,1)}) custom-call(bf16[24,192,256]{2,1,0:T(8,128)(2,1)S(1)} %bitcast.9, f32[2,256]{1,0:T(2,128)S(1)} %pad_maximum_fusion.affine_ref, bf16[2,8,32,512]{3,2,1,0:T(8,128)(2,1)S(1)} %bitcast.8, ...), custom_call_target="tpu_custom_call" | custom-call | flops 8000000000 | tf_op jit(solution)/shard_map/embed/pallas_call | solution.py:179
  46.9 9.7 %all-to-all-start.1 = ((bf16[16,72,512]{2,1,0:T(8,128)(2,1)}), bf16[16,72,512]{2,1,0:T(8,128)(2,1)S(1)}, u32[]{:S(2)}, u32[]{:S(2)}) async-start(bf16[16,72,512]{2,1,0:T(8,128)(2,1)} %bitcast.2), calls=%async_computation.1 | async-start | bytes 2359296 | tf_op jit(solution)/shard_map/all_to_all | solution.py:509
  56.6 1.3 collective-permute-start.2
  57.9 5.5 %collective-permute-start.1 = (bf16[5,192,512]{2,1,0:T(8,128)(2,1)S(1)}, bf16[5,192,512]{2,1,0:T(8,128)(2,1)}, u32[]{:S(2)}, u32[]{:S(2)}) collective-permute-start(bf16[5,192,512]{2,1,0:T(8,128)(2,1)S(1)} %get-tuple-element.18.bottom_ref), channel_id=1, source_target_pairs={{0,16},{16,32},{32,48},{48,64},{64,80},{80,96},{96,112},{1,17},{17... | collective-permute-start | bytes 2949128 | tf_op jit(solution)/shard_map/ppermute | solution.py:506
  63.4 7.3 %all-gather.3.cloned.1.call-done = bf16[1536,512]{1,0:T(8,128)(2,1)} async-done(((bf16[192,512]{1,0:T(8,128)(2,1)}), bf16[1536,512]{1,0:T(8,128)(2,1)}) %all-gather.3.cloned.1.call-update) | async-done | bytes 1572880 | tf_op jit(solution)/shard_map/all_gather | solution.py:500
  71.8 1.9 %collective-permute-start.4 = (bf16[8,64,512]{2,1,0:T(8,128)(2,1)S(1)}, bf16[8,64,512]{2,1,0:T(8,128)(2,1)S(1)}, u32[]{:S(2)}, u32[]{:S(2)}) collective-permute-start(bf16[8,64,512]{2,1,0:T(8,128)(2,1)S(1)} %slice.6.weight_ref.near_ref), channel_id=1, source_target_pairs={{0,128},{128,0},{1,129},{129,1},{2,130},{130,2},{3,131},{131,3},{4... | collective-permute-start | bytes 1572872 | tf_op jit(solution)/shard_map/ppermute | solution.py:464
  73.8 1.9 %collective-permute-done.4.other_ref.near_other_ref = bf16[8,64,512]{2,1,0:T(8,128)(2,1)S(1)} collective-permute-done((bf16[8,64,512]{2,1,0:T(8,128)(2,1)S(1)}, bf16[8,64,512]{2,1,0:T(8,128)(2,1)S(1)}, u32[]{:S(2)}, u32[]{:S(2)}) %collective-permute-start.4) | collective-permute-done | bytes 524320 | tf_op jit(solution)/shard_map/ppermute | solution.py:464
  75.6 4.0 %project.1 = (bf16[6,256,256]{2,1,0:T(8,128)(2,1)S(1)}, bf16[6,256,512]{2,1,0:T(8,128)(2,1)S(1)}, bf16[512,512]{1,0:T(8,128)(2,1)S(1)}) custom-call(s32[16]{0:T(128)S(1)} %copy-done.6, bf16[5,192,512]{2,1,0:T(8,128)(2,1)} %get-tuple-element.19.top_ref, bf16[5,192,512]{2,1,0:T(8,128)(2,1)S(1)} %get-tuple-element.18.bottom_ref, ...), custom_call_target="tpu_custom_call" | custom-call | flops 1358954496 | bytes 3538944 | tf_op jit(solution)/shard_map/project/pallas_call | solution.py:260
  79.7 6.2 %collective-permute-done.2.south_ref = bf16[5,192,512]{2,1,0:T(8,128)(2,1)} collective-permute-done((bf16[5,192,512]{2,1,0:T(8,128)(2,1)}, bf16[5,192,512]{2,1,0:T(8,128)(2,1)}, u32[]{:S(2)}, u32[]{:S(2)}) %collective-permute-start.2) | collective-permute-done | bytes 983072 | tf_op jit(solution)/shard_map/ppermute | solution.py:507
  85.8 10.6 %attend.1 = bf16[16,72,256]{2,1,0:T(8,128)(2,1)} custom-call(s32[16]{0:T(128)S(1)} %copy-done.5, s32[16]{0:T(128)S(1)} %copy-done.6, bf16[5,192,512]{2,1,0:T(8,128)(2,1)} %collective-permute-done.1.north_ref, bf16[5,192,512]{2,1,0:T(8,128)(2,1)} %collective-permute-done.2.south_ref, bf16[6,256,256]{2,1,0:T(8,128)(2,1)S(1)} %get-tuple-element.22.query_ref, ...), custom_call_target="tpu_custom_call" | custom-call | flops 10569646080 | bytes 5111808 | tf_op jit(solution)/shard_map/attend/pallas_call | solution.py:377
  96.4 9.1 %all-to-all-start.2 = ((bf16[16,72,256]{2,1,0:T(8,128)(2,1)}), bf16[16,72,256]{2,1,0:T(8,128)(2,1)S(1)}, u32[]{:S(2)}, u32[]{:S(2)}) async-start(bf16[16,72,256]{2,1,0:T(8,128)(2,1)} %attend.1), calls=%async_computation.2 | async-start | bytes 1179648 | tf_op jit(solution)/shard_map/all_to_all | solution.py:517
  105.5 1.3 slice.7.hidden_ref
  106.8 1.9 %collective-permute-start.5 = (bf16[8,128,512]{2,1,0:T(8,128)(2,1)S(1)}, bf16[8,128,512]{2,1,0:T(8,128)(2,1)S(1)}, u32[]{:S(2)}, u32[]{:S(2)}) collective-permute-start(bf16[8,128,512]{2,1,0:T(8,128)(2,1)S(1)} %slice.7.hidden_ref), channel_id=1, source_target_pairs={{0,128},{128,0},{1,129},{129,1},{2,130},{130,2},{3,131},{131,3},{4... | collective-permute-start | bytes 3145736 | tf_op jit(solution)/shard_map/ppermute | solution.py:464
  108.7 2.6 %collective-permute-done.5.hidden_other_ref = bf16[8,128,512]{2,1,0:T(8,128)(2,1)S(1)} collective-permute-done((bf16[8,128,512]{2,1,0:T(8,128)(2,1)S(1)}, bf16[8,128,512]{2,1,0:T(8,128)(2,1)S(1)}, u32[]{:S(2)}, u32[]{:S(2)}) %collective-permute-start.5) | collective-permute-done | bytes 1048608 | tf_op jit(solution)/shard_map/ppermute | solution.py:464
  112.3 12.5 %all-to-all-done.2.mixed_ref = bf16[16,72,256]{2,1,0:T(8,128)(2,1)S(1)} async-done(((bf16[16,72,256]{2,1,0:T(8,128)(2,1)}), bf16[16,72,256]{2,1,0:T(8,128)(2,1)S(1)}, u32[]{:S(2)}, u32[]{:S(2)}) %all-to-all-start.2) | async-done | bytes 589856 | tf_op jit(solution)/shard_map/all_to_all | solution.py:517
  127.1 6.7 %finish.1 = bf16[72,16,512]{2,1,0:T(8,128)(2,1)} custom-call(bf16[16,72,512]{2,1,0:T(8,128)(2,1)S(1)} %all-to-all-done.1.tokens_ref, bf16[16,72,256]{2,1,0:T(8,128)(2,1)S(1)} %all-to-all-done.2.mixed_ref, bf16[8,128,512]{2,1,0:T(8,128)(2,1)S(1)} %slice.7.hidden_ref, bf16[8,128,512]{2,1,0:T(8,128)(2,1)S(1)} %copy-done.2, ...), custom_call_target="tpu_custom_call" | custom-call | flops 2717908992 | bytes 6094848 | tf_op jit(solution)/shard_map/finish/pallas_call | solution.py:437
  (33 shorter events, 5.2 us)
Async XLA Ops:
  6.5 32.4 %copy-start.9 = (s32[64]{0:T(128)S(1)}, s32[64]{0:T(128)}, u32[]{:S(2)}) copy-start(s32[64]{0:T(128)} %param.12) | copy-start | bytes 772
  6.5 32.4 %copy-start.10 = (f32[64]{0:T(128)S(1)}, f32[64]{0:T(128)}, u32[]{:S(2)}) copy-start(f32[64]{0:T(128)} %param.13) | copy-start | bytes 772
  6.5 32.4 %copy-start.8 = (f32[64]{0:T(128)S(1)}, f32[64]{0:T(128)}, u32[]{:S(2)}) copy-start(f32[64]{0:T(128)} %param.14) | copy-start | bytes 772
  8.2 14.3 %collective-permute-start.3 = (bf16[96,512]{1,0:T(8,128)(2,1)}, bf16[96,512]{1,0:T(8,128)(2,1)S(1)}, u32[]{:S(2)}, u32[]{:S(2)}) collective-permute-start(bf16[96,512]{1,0:T(8,128)(2,1)} %get-tuple-element.20.own_ref), channel_id=1, source_target_pairs={{0,256},{256,0},{1,257},{257,1},{2,258},{258,2},{3,259},{259,3},{4... | collective-permute-start | bytes 294920 | tf_op jit(solution)/shard_map/ppermute | solution.py:464
  16.0 21.1 %all-to-all-start = ((bf16[16,32,512]{2,1,0:T(8,128)(2,1)}), bf16[16,32,512]{2,1,0:T(8,128)(2,1)S(1)}, u32[]{:S(2)}, u32[]{:S(2)}) async-start(bf16[16,32,512]{2,1,0:T(8,128)(2,1)} %get-tuple-element.16), calls=%async_computation | async-start | bytes 1048576 | tf_op jit(solution)/shard_map/all_to_all | solution.py:501
  22.5 48.2 %all-gather.3.cloned.1.call-start = ((), (), s32[]{:S(2)}) async-start(), calls=%async_computation.3 | async-start | bytes 1769472 | tf_op jit(solution)/shard_map/all_gather | solution.py:500
  22.6 0.6 copy-start.7
  37.0 3.8 %collective-permute-start = (bf16[2,8,32,512]{3,2,1,0:T(8,128)(2,1)S(1)}, bf16[2,8,32,512]{3,2,1,0:T(8,128)(2,1)S(1)}, u32[]{:S(2)}, u32[]{:S(2)}) collective-permute-start(bf16[2,8,32,512]{3,2,1,0:T(8,128)(2,1)S(1)} %bitcast.7), channel_id=1, source_target_pairs={{0,128},{128,0},{1,129},{129,1},{2,130},{130,2},{3,131},{131,3},{4... | collective-permute-start | bytes 1572872 | tf_op jit(solution)/shard_map/ppermute | solution.py:464
  40.8 1.7 %copy-start = (bf16[1,24,192,256]{3,2,1,0:T(8,128)(2,1)S(1)}, bf16[1,24,192,256]{3,2,1,0:T(8,128)(2,1)}, u32[]{:S(2)}) copy-start(bf16[1,24,192,256]{3,2,1,0:T(8,128)(2,1)} %param.11) | copy-start | bytes 7077892
  46.9 28.7 %copy-start.6 = (s32[16]{0:T(128)S(1)}, s32[16]{0:T(128)}, u32[]{:S(2)}) copy-start(s32[16]{0:T(128)} %column_offset_ref.3) | copy-start | bytes 196
  46.9 49.5 %all-to-all-start.1 = ((bf16[16,72,512]{2,1,0:T(8,128)(2,1)}), bf16[16,72,512]{2,1,0:T(8,128)(2,1)S(1)}, u32[]{:S(2)}, u32[]{:S(2)}) async-start(bf16[16,72,512]{2,1,0:T(8,128)(2,1)} %bitcast.2), calls=%async_computation.1 | async-start | bytes 2359296 | tf_op jit(solution)/shard_map/all_to_all | solution.py:509
  56.6 29.2 %collective-permute-start.2 = (bf16[5,192,512]{2,1,0:T(8,128)(2,1)}, bf16[5,192,512]{2,1,0:T(8,128)(2,1)}, u32[]{:S(2)}, u32[]{:S(2)}) collective-permute-start(bf16[5,192,512]{2,1,0:T(8,128)(2,1)} %get-tuple-element.19.top_ref), channel_id=1, source_target_pairs={{16,0},{32,16},{48,32},{64,48},{80,64},{96,80},{112,96},{17,1},{33... | collective-permute-start | bytes 2949128 | tf_op jit(solution)/shard_map/ppermute | solution.py:507
  57.9 27.9 %collective-permute-start.1 = (bf16[5,192,512]{2,1,0:T(8,128)(2,1)S(1)}, bf16[5,192,512]{2,1,0:T(8,128)(2,1)}, u32[]{:S(2)}, u32[]{:S(2)}) collective-permute-start(bf16[5,192,512]{2,1,0:T(8,128)(2,1)S(1)} %get-tuple-element.18.bottom_ref), channel_id=1, source_target_pairs={{0,16},{16,32},{32,48},{48,64},{64,80},{80,96},{96,112},{1,17},{17... | collective-permute-start | bytes 2949128 | tf_op jit(solution)/shard_map/ppermute | solution.py:506
  71.8 14.0 %copy-start.5 = (s32[16]{0:T(128)S(1)}, s32[16]{0:T(128)}, u32[]{:S(2)}) copy-start(s32[16]{0:T(128)} %row_offset_ref.1) | copy-start | bytes 196
  71.8 3.8 %collective-permute-start.4 = (bf16[8,64,512]{2,1,0:T(8,128)(2,1)S(1)}, bf16[8,64,512]{2,1,0:T(8,128)(2,1)S(1)}, u32[]{:S(2)}, u32[]{:S(2)}) collective-permute-start(bf16[8,64,512]{2,1,0:T(8,128)(2,1)S(1)} %slice.6.weight_ref.near_ref), channel_id=1, source_target_pairs={{0,128},{128,0},{1,129},{129,1},{2,130},{130,2},{3,131},{131,3},{4... | collective-permute-start | bytes 1572872 | tf_op jit(solution)/shard_map/ppermute | solution.py:464
  75.6 4.0 %copy-start.3 = (bf16[8,64,512]{2,1,0:T(8,128)(2,1)}, bf16[8,64,512]{2,1,0:T(8,128)(2,1)S(1)}, u32[]{:S(2)}) copy-start(bf16[8,64,512]{2,1,0:T(8,128)(2,1)S(1)} %collective-permute-done.4.other_ref.near_other_ref) | copy-start | bytes 1572868
  96.4 28.4 %all-to-all-start.2 = ((bf16[16,72,256]{2,1,0:T(8,128)(2,1)}), bf16[16,72,256]{2,1,0:T(8,128)(2,1)S(1)}, u32[]{:S(2)}, u32[]{:S(2)}) async-start(bf16[16,72,256]{2,1,0:T(8,128)(2,1)} %attend.1), calls=%async_computation.2 | async-start | bytes 1179648 | tf_op jit(solution)/shard_map/all_to_all | solution.py:517
  106.8 4.6 %collective-permute-start.5 = (bf16[8,128,512]{2,1,0:T(8,128)(2,1)S(1)}, bf16[8,128,512]{2,1,0:T(8,128)(2,1)S(1)}, u32[]{:S(2)}, u32[]{:S(2)}) collective-permute-start(bf16[8,128,512]{2,1,0:T(8,128)(2,1)S(1)} %slice.7.hidden_ref), channel_id=1, source_target_pairs={{0,128},{128,0},{1,129},{129,1},{2,130},{130,2},{3,131},{131,3},{4... | collective-permute-start | bytes 3145736 | tf_op jit(solution)/shard_map/ppermute | solution.py:464
  111.4 1.0 copy-start.1
  124.8 1.2 copy-start.2
  126.0 1.0 copy-start.4
Sparse Core Ops, SparseCore 0:
  25.4 45.2 all-gather.2

commit v6 on v5

--- a/solution.py
+++ b/solution.py
@@ -22,6 +22,7 @@
 GROUP = 4
 ATTEND_COST = 5
 EMBED_COST = 8 * 10**9
+UNROLL = 16
 LINES = 16
 
 
@@ -351,11 +352,11 @@
         made_ref[:, pl.ds(pl.multiple_of((m + 1) * PAD, PAD), PAD), :] = mixed
 
     def some_windows(step, carry):
-        for inner in range(GROUP):
-            window(step * GROUP + inner)
+        for inner in range(UNROLL):
+            window(step * UNROLL + inner)
         return carry
 
-    lax.fori_loop(0, windows // GROUP, some_windows, 0)
+    lax.fori_loop(0, windows // UNROLL, some_windows, 0)
     made_ref[:, :PAD, :] = made_ref[:, windows * PAD :, :]
 
     def source(k):
@@ -433,7 +434,7 @@
     count, cells, features = tokens.shape
     width = mixed.shape[2]
     hidden = 2 * features
-    block = 24
+    block = 72
     return pl.pallas_call(
         finish_kernel,
         grid=(cells // block,),
@@ -450,7 +451,7 @@
             pltpu.VMEM((hidden, features), BF16),
             pltpu.VMEM((count * block, count * block), BF16),
         ],
-        compiler_params=pltpu.CompilerParams(vmem_limit_bytes=24 * 1024 * 1024),
+        compiler_params=pltpu.CompilerParams(vmem_limit_bytes=40 * 1024 * 1024),
         cost_estimate=pl.CostEstimate(
             flops=2 * count * cells * features * (width + 2 * hidden),
             bytes_accessed=count * cells * (4 * features + 2 * width) + weights[0].size * 6,

time: 142 us -> 139 us (0.979)
  Pallas kernels: 29 us -> 26.6 us
    pallas_call x1, Pallas kernels: 10.6 us -> 8.61 us  [attend(): pl.pallas_call(attend_kernel, in_specs=[pl.BlockSpec(memory_space=pltpu.S...]
  transfers between devices with their start and end apart: 10 -> 10, of which waited for: 7 -> 7; matrix products, arithmetic and copies ran while one was open for 2% -> 2% of each run, Pallas kernels for 15% -> 14%
where the time goes in v6:
time: 139 us; the launch traced here: 138 us
  starting transfers between devices  45.8 us (33%)
  waiting for transfers between devices  44.1 us (32%)
  Pallas kernels  26.6 us (19%)
  between operations  13.6 us (10%)
  local copies, waits for them, and re-layouts  8.14 us (6%)
    ppermute x4, starting transfers between devices, swap(): return lax.ppermute(values, axis, [(0, 1), (1, 0)])  13.6 us
    all_to_all x1, waiting for transfers between devices, shards(): tile_mixed = lax.all_to_all(mixed, ('y_hi', 'x'), 0, 0, tiled=True)  12.5 us
    all_to_all x1, waiting for transfers between devices, shards(): patch = lax.all_to_all(patch, ('y_lo', 'lat'), 0, 0, tiled=True)  12.2 us
    all_to_all x1, starting transfers between devices, shards(): tile_tokens = lax.all_to_all(tiles, ('y_hi', 'x'), 0, 0, tiled=True)  9.66 us
    all_to_all x1, starting transfers between devices, shards(): tile_mixed = lax.all_to_all(mixed, ('y_hi', 'x'), 0, 0, tiled=True)  9.06 us
    pallas_call x1, Pallas kernels, attend(): pl.pallas_call(attend_kernel, in_specs=[pl.BlockSpec(memory_space=pltpu.S...  8.61 us
    all_gather x1, waiting for transfers between devices, shards(): rest = lax.all_gather(packed, 'lat', axis=0)  7.06 us
    all_to_all x1, starting transfers between devices, shards(): patch = lax.all_to_all(patch, ('y_lo', 'lat'), 0, 0, tiled=True)  6.55 us
  transfers between devices with their start and end apart: 10, of which 7 were waited for; matrix products, arithmetic and copies ran while one was open for 2% of the time, Pallas kernels for 14%

profile of v6, /device:TPU:8, one launch (start us, length us, event | category | flops | bytes accessed | tf_op | source)
XLA Modules:
  0.0 138.2 jit_solution(10215688726822926229)
XLA Ops:
  6.5 1.7 %pack.1 = (bf16[16,32,512]{2,1,0:T(8,128)(2,1)}, bf16[96,512]{1,0:T(8,128)(2,1)}) custom-call(bf16[32,512]{1,0:T(8,128)(2,1)} %patch_ref.1, bf16[16,1024]{1,0:T(8,128)(2,1)} %hidden_in_ref.1, bf16[32,512]{1,0:T(8,128)(2,1)} %hidden_out_ref.1, bf16[8,512]{1,0:T(8,128)(2,1)} %attention_out_ref.1, bf16[16,768]{1,0:T(8,128)(2,1)} %attention_in_ref.1), custom_call_target="tpu_custom_call" | custom-call | tf_op jit(solution)/shard_map/pack/pallas_call | solution.py:102
  8.2 7.7 %collective-permute-start.3 = (bf16[96,512]{1,0:T(8,128)(2,1)}, bf16[96,512]{1,0:T(8,128)(2,1)S(1)}, u32[]{:S(2)}, u32[]{:S(2)}) collective-permute-start(bf16[96,512]{1,0:T(8,128)(2,1)} %get-tuple-element.20.own_ref), channel_id=1, source_target_pairs={{0,256},{256,0},{1,257},{257,1},{2,258},{258,2},{3,259},{259,3},{4... | collective-permute-start | bytes 294920 | tf_op jit(solution)/shard_map/ppermute | solution.py:465
  16.0 6.5 %all-to-all-start = ((bf16[16,32,512]{2,1,0:T(8,128)(2,1)}), bf16[16,32,512]{2,1,0:T(8,128)(2,1)S(1)}, u32[]{:S(2)}, u32[]{:S(2)}) async-start(bf16[16,32,512]{2,1,0:T(8,128)(2,1)} %get-tuple-element.16), calls=%async_computation | async-start | bytes 1048576 | tf_op jit(solution)/shard_map/all_to_all | solution.py:502
  23.2 1.6 %join.1 = bf16[192,512]{1,0:T(8,128)(2,1)} custom-call(bf16[96,512]{1,0:T(8,128)(2,1)} %get-tuple-element.20.own_ref, bf16[96,512]{1,0:T(8,128)(2,1)} %copy-done.7), custom_call_target="tpu_custom_call" | custom-call | tf_op jit(solution)/shard_map/join/pallas_call | solution.py:123
  24.9 12.2 %all-to-all-done = bf16[16,32,512]{2,1,0:T(8,128)(2,1)S(1)} async-done(((bf16[16,32,512]{2,1,0:T(8,128)(2,1)}), bf16[16,32,512]{2,1,0:T(8,128)(2,1)S(1)}, u32[]{:S(2)}, u32[]{:S(2)}) %all-to-all-start) | async-done | bytes 524320 | tf_op jit(solution)/shard_map/all_to_all | solution.py:502
  37.0 1.9 %collective-permute-start = (bf16[2,8,32,512]{3,2,1,0:T(8,128)(2,1)S(1)}, bf16[2,8,32,512]{3,2,1,0:T(8,128)(2,1)S(1)}, u32[]{:S(2)}, u32[]{:S(2)}) collective-permute-start(bf16[2,8,32,512]{3,2,1,0:T(8,128)(2,1)S(1)} %bitcast.7), channel_id=1, source_target_pairs={{0,128},{128,0},{1,129},{129,1},{2,130},{130,2},{3,131},{131,3},{4... | collective-permute-start | bytes 1572872 | tf_op jit(solution)/shard_map/ppermute | solution.py:465
  39.2 1.6 %collective-permute-done.other_ref = bf16[2,8,32,512]{3,2,1,0:T(8,128)(2,1)S(1)} collective-permute-done((bf16[2,8,32,512]{3,2,1,0:T(8,128)(2,1)S(1)}, bf16[2,8,32,512]{3,2,1,0:T(8,128)(2,1)S(1)}, u32[]{:S(2)}, u32[]{:S(2)}) %collective-permute-start) | collective-permute-done | bytes 524320 | tf_op jit(solution)/shard_map/ppermute | solution.py:465
  40.8 1.7 %copy-done = bf16[1,24,192,256]{3,2,1,0:T(8,128)(2,1)S(1)} copy-done((bf16[1,24,192,256]{3,2,1,0:T(8,128)(2,1)S(1)}, bf16[1,24,192,256]{3,2,1,0:T(8,128)(2,1)}, u32[]{:S(2)}) %copy-start) | copy-done | bytes 2359320
  42.5 4.4 %embed.1 = (bf16[5,192,512]{2,1,0:T(8,128)(2,1)}, bf16[5,192,512]{2,1,0:T(8,128)(2,1)S(1)}, bf16[1152,512]{1,0:T(8,128)(2,1)}) custom-call(bf16[24,192,256]{2,1,0:T(8,128)(2,1)S(1)} %bitcast.9, f32[2,256]{1,0:T(2,128)S(1)} %pad_maximum_fusion.affine_ref, bf16[2,8,32,512]{3,2,1,0:T(8,128)(2,1)S(1)} %bitcast.8, ...), custom_call_target="tpu_custom_call" | custom-call | flops 8000000000 | tf_op jit(solution)/shard_map/embed/pallas_call | solution.py:180
  46.9 9.7 %all-to-all-start.1 = ((bf16[16,72,512]{2,1,0:T(8,128)(2,1)}), bf16[16,72,512]{2,1,0:T(8,128)(2,1)S(1)}, u32[]{:S(2)}, u32[]{:S(2)}) async-start(bf16[16,72,512]{2,1,0:T(8,128)(2,1)} %bitcast.2), calls=%async_computation.1 | async-start | bytes 2359296 | tf_op jit(solution)/shard_map/all_to_all | solution.py:510
  56.6 1.3 collective-permute-start.2
  57.9 5.5 %collective-permute-start.1 = (bf16[5,192,512]{2,1,0:T(8,128)(2,1)S(1)}, bf16[5,192,512]{2,1,0:T(8,128)(2,1)}, u32[]{:S(2)}, u32[]{:S(2)}) collective-permute-start(bf16[5,192,512]{2,1,0:T(8,128)(2,1)S(1)} %get-tuple-element.18.bottom_ref), channel_id=1, source_target_pairs={{0,16},{16,32},{32,48},{48,64},{64,80},{80,96},{96,112},{1,17},{17... | collective-permute-start | bytes 2949128 | tf_op jit(solution)/shard_map/ppermute | solution.py:507
  63.4 7.1 %all-gather.3.cloned.1.call-done = bf16[1536,512]{1,0:T(8,128)(2,1)} async-done(((bf16[192,512]{1,0:T(8,128)(2,1)}), bf16[1536,512]{1,0:T(8,128)(2,1)}) %all-gather.3.cloned.1.call-update) | async-done | bytes 1572880 | tf_op jit(solution)/shard_map/all_gather | solution.py:501
  71.6 1.9 %collective-permute-start.4 = (bf16[8,64,512]{2,1,0:T(8,128)(2,1)S(1)}, bf16[8,64,512]{2,1,0:T(8,128)(2,1)S(1)}, u32[]{:S(2)}, u32[]{:S(2)}) collective-permute-start(bf16[8,64,512]{2,1,0:T(8,128)(2,1)S(1)} %slice.6.weight_ref.near_ref), channel_id=1, source_target_pairs={{0,128},{128,0},{1,129},{129,1},{2,130},{130,2},{3,131},{131,3},{4... | collective-permute-start | bytes 1572872 | tf_op jit(solution)/shard_map/ppermute | solution.py:465
  73.5 1.9 %collective-permute-done.4.other_ref.near_other_ref = bf16[8,64,512]{2,1,0:T(8,128)(2,1)S(1)} collective-permute-done((bf16[8,64,512]{2,1,0:T(8,128)(2,1)S(1)}, bf16[8,64,512]{2,1,0:T(8,128)(2,1)S(1)}, u32[]{:S(2)}, u32[]{:S(2)}) %collective-permute-start.4) | collective-permute-done | bytes 524320 | tf_op jit(solution)/shard_map/ppermute | solution.py:465
  75.4 4.0 %project.1 = (bf16[6,256,256]{2,1,0:T(8,128)(2,1)S(1)}, bf16[6,256,512]{2,1,0:T(8,128)(2,1)S(1)}, bf16[512,512]{1,0:T(8,128)(2,1)S(1)}) custom-call(s32[16]{0:T(128)S(1)} %copy-done.6, bf16[5,192,512]{2,1,0:T(8,128)(2,1)} %get-tuple-element.19.top_ref, bf16[5,192,512]{2,1,0:T(8,128)(2,1)S(1)} %get-tuple-element.18.bottom_ref, ...), custom_call_target="tpu_custom_call" | custom-call | flops 1358954496 | bytes 3538944 | tf_op jit(solution)/shard_map/project/pallas_call | solution.py:261
  79.4 6.4 %collective-permute-done.2.south_ref = bf16[5,192,512]{2,1,0:T(8,128)(2,1)} collective-permute-done((bf16[5,192,512]{2,1,0:T(8,128)(2,1)}, bf16[5,192,512]{2,1,0:T(8,128)(2,1)}, u32[]{:S(2)}, u32[]{:S(2)}) %collective-permute-start.2) | collective-permute-done | bytes 983072 | tf_op jit(solution)/shard_map/ppermute | solution.py:508
  85.8 8.6 %attend.1 = bf16[16,72,256]{2,1,0:T(8,128)(2,1)} custom-call(s32[16]{0:T(128)S(1)} %copy-done.5, s32[16]{0:T(128)S(1)} %copy-done.6, bf16[5,192,512]{2,1,0:T(8,128)(2,1)} %collective-permute-done.1.north_ref, bf16[5,192,512]{2,1,0:T(8,128)(2,1)} %collective-permute-done.2.south_ref, bf16[6,256,256]{2,1,0:T(8,128)(2,1)S(1)} %get-tuple-element.22.query_ref, ...), custom_call_target="tpu_custom_call" | custom-call | flops 10569646080 | bytes 5111808 | tf_op jit(solution)/shard_map/attend/pallas_call | solution.py:378
  94.4 9.1 %all-to-all-start.2 = ((bf16[16,72,256]{2,1,0:T(8,128)(2,1)}), bf16[16,72,256]{2,1,0:T(8,128)(2,1)S(1)}, u32[]{:S(2)}, u32[]{:S(2)}) async-start(bf16[16,72,256]{2,1,0:T(8,128)(2,1)} %attend.1), calls=%async_computation.2 | async-start | bytes 1179648 | tf_op jit(solution)/shard_map/all_to_all | solution.py:518
  103.5 1.3 slice.7.hidden_ref
  104.8 2.1 %collective-permute-start.5 = (bf16[8,128,512]{2,1,0:T(8,128)(2,1)S(1)}, bf16[8,128,512]{2,1,0:T(8,128)(2,1)S(1)}, u32[]{:S(2)}, u32[]{:S(2)}) collective-permute-start(bf16[8,128,512]{2,1,0:T(8,128)(2,1)S(1)} %slice.7.hidden_ref), channel_id=1, source_target_pairs={{0,128},{128,0},{1,129},{129,1},{2,130},{130,2},{3,131},{131,3},{4... | collective-permute-start | bytes 3145736 | tf_op jit(solution)/shard_map/ppermute | solution.py:465
  106.9 2.4 %collective-permute-done.5.hidden_other_ref = bf16[8,128,512]{2,1,0:T(8,128)(2,1)S(1)} collective-permute-done((bf16[8,128,512]{2,1,0:T(8,128)(2,1)S(1)}, bf16[8,128,512]{2,1,0:T(8,128)(2,1)S(1)}, u32[]{:S(2)}, u32[]{:S(2)}) %collective-permute-start.5) | collective-permute-done | bytes 1048608 | tf_op jit(solution)/shard_map/ppermute | solution.py:465
  110.3 12.5 %all-to-all-done.2.mixed_ref = bf16[16,72,256]{2,1,0:T(8,128)(2,1)S(1)} async-done(((bf16[16,72,256]{2,1,0:T(8,128)(2,1)}), bf16[16,72,256]{2,1,0:T(8,128)(2,1)S(1)}, u32[]{:S(2)}, u32[]{:S(2)}) %all-to-all-start.2) | async-done | bytes 589856 | tf_op jit(solution)/shard_map/all_to_all | solution.py:518
  125.1 6.3 %finish.1 = bf16[72,16,512]{2,1,0:T(8,128)(2,1)} custom-call(bf16[16,72,512]{2,1,0:T(8,128)(2,1)S(1)} %all-to-all-done.1.tokens_ref, bf16[16,72,256]{2,1,0:T(8,128)(2,1)S(1)} %all-to-all-done.2.mixed_ref, bf16[8,128,512]{2,1,0:T(8,128)(2,1)S(1)} %slice.7.hidden_ref, bf16[8,128,512]{2,1,0:T(8,128)(2,1)S(1)} %copy-done.2, ...), custom_call_target="tpu_custom_call" | custom-call | flops 2717908992 | bytes 6094848 | tf_op jit(solution)/shard_map/finish/pallas_call | solution.py:438
  (33 shorter events, 5.2 us)
Async XLA Ops:
  6.5 32.4 %copy-start.9 = (s32[64]{0:T(128)S(1)}, s32[64]{0:T(128)}, u32[]{:S(2)}) copy-start(s32[64]{0:T(128)} %param.12) | copy-start | bytes 772
  6.5 32.4 %copy-start.10 = (f32[64]{0:T(128)S(1)}, f32[64]{0:T(128)}, u32[]{:S(2)}) copy-start(f32[64]{0:T(128)} %param.13) | copy-start | bytes 772
  6.5 32.4 %copy-start.8 = (f32[64]{0:T(128)S(1)}, f32[64]{0:T(128)}, u32[]{:S(2)}) copy-start(f32[64]{0:T(128)} %param.14) | copy-start | bytes 772
  8.2 14.3 %collective-permute-start.3 = (bf16[96,512]{1,0:T(8,128)(2,1)}, bf16[96,512]{1,0:T(8,128)(2,1)S(1)}, u32[]{:S(2)}, u32[]{:S(2)}) collective-permute-start(bf16[96,512]{1,0:T(8,128)(2,1)} %get-tuple-element.20.own_ref), channel_id=1, source_target_pairs={{0,256},{256,0},{1,257},{257,1},{2,258},{258,2},{3,259},{259,3},{4... | collective-permute-start | bytes 294920 | tf_op jit(solution)/shard_map/ppermute | solution.py:465
  16.0 21.1 %all-to-all-start = ((bf16[16,32,512]{2,1,0:T(8,128)(2,1)}), bf16[16,32,512]{2,1,0:T(8,128)(2,1)S(1)}, u32[]{:S(2)}, u32[]{:S(2)}) async-start(bf16[16,32,512]{2,1,0:T(8,128)(2,1)} %get-tuple-element.16), calls=%async_computation | async-start | bytes 1048576 | tf_op jit(solution)/shard_map/all_to_all | solution.py:502
  22.5 48.0 %all-gather.3.cloned.1.call-start = ((), (), s32[]{:S(2)}) async-start(), calls=%async_computation.3 | async-start | bytes 1769472 | tf_op jit(solution)/shard_map/all_gather | solution.py:501
  22.6 0.6 copy-start.7
  37.0 3.8 %collective-permute-start = (bf16[2,8,32,512]{3,2,1,0:T(8,128)(2,1)S(1)}, bf16[2,8,32,512]{3,2,1,0:T(8,128)(2,1)S(1)}, u32[]{:S(2)}, u32[]{:S(2)}) collective-permute-start(bf16[2,8,32,512]{3,2,1,0:T(8,128)(2,1)S(1)} %bitcast.7), channel_id=1, source_target_pairs={{0,128},{128,0},{1,129},{129,1},{2,130},{130,2},{3,131},{131,3},{4... | collective-permute-start | bytes 1572872 | tf_op jit(solution)/shard_map/ppermute | solution.py:465
  40.8 1.7 %copy-start = (bf16[1,24,192,256]{3,2,1,0:T(8,128)(2,1)S(1)}, bf16[1,24,192,256]{3,2,1,0:T(8,128)(2,1)}, u32[]{:S(2)}) copy-start(bf16[1,24,192,256]{3,2,1,0:T(8,128)(2,1)} %param.11) | copy-start | bytes 7077892
  46.9 28.5 %copy-start.6 = (s32[16]{0:T(128)S(1)}, s32[16]{0:T(128)}, u32[]{:S(2)}) copy-start(s32[16]{0:T(128)} %column_offset_ref.3) | copy-start | bytes 196
  46.9 47.5 %all-to-all-start.1 = ((bf16[16,72,512]{2,1,0:T(8,128)(2,1)}), bf16[16,72,512]{2,1,0:T(8,128)(2,1)S(1)}, u32[]{:S(2)}, u32[]{:S(2)}) async-start(bf16[16,72,512]{2,1,0:T(8,128)(2,1)} %bitcast.2), calls=%async_computation.1 | async-start | bytes 2359296 | tf_op jit(solution)/shard_map/all_to_all | solution.py:510
  56.6 29.2 %collective-permute-start.2 = (bf16[5,192,512]{2,1,0:T(8,128)(2,1)}, bf16[5,192,512]{2,1,0:T(8,128)(2,1)}, u32[]{:S(2)}, u32[]{:S(2)}) collective-permute-start(bf16[5,192,512]{2,1,0:T(8,128)(2,1)} %get-tuple-element.19.top_ref), channel_id=1, source_target_pairs={{16,0},{32,16},{48,32},{64,48},{80,64},{96,80},{112,96},{17,1},{33... | collective-permute-start | bytes 2949128 | tf_op jit(solution)/shard_map/ppermute | solution.py:508
  57.9 27.9 %collective-permute-start.1 = (bf16[5,192,512]{2,1,0:T(8,128)(2,1)S(1)}, bf16[5,192,512]{2,1,0:T(8,128)(2,1)}, u32[]{:S(2)}, u32[]{:S(2)}) collective-permute-start(bf16[5,192,512]{2,1,0:T(8,128)(2,1)S(1)} %get-tuple-element.18.bottom_ref), channel_id=1, source_target_pairs={{0,16},{16,32},{32,48},{48,64},{64,80},{80,96},{96,112},{1,17},{17... | collective-permute-start | bytes 2949128 | tf_op jit(solution)/shard_map/ppermute | solution.py:507
  71.6 14.2 %copy-start.5 = (s32[16]{0:T(128)S(1)}, s32[16]{0:T(128)}, u32[]{:S(2)}) copy-start(s32[16]{0:T(128)} %row_offset_ref.1) | copy-start | bytes 196
  71.6 3.8 %collective-permute-start.4 = (bf16[8,64,512]{2,1,0:T(8,128)(2,1)S(1)}, bf16[8,64,512]{2,1,0:T(8,128)(2,1)S(1)}, u32[]{:S(2)}, u32[]{:S(2)}) collective-permute-start(bf16[8,64,512]{2,1,0:T(8,128)(2,1)S(1)} %slice.6.weight_ref.near_ref), channel_id=1, source_target_pairs={{0,128},{128,0},{1,129},{129,1},{2,130},{130,2},{3,131},{131,3},{4... | collective-permute-start | bytes 1572872 | tf_op jit(solution)/shard_map/ppermute | solution.py:465
  75.4 4.0 %copy-start.3 = (bf16[8,64,512]{2,1,0:T(8,128)(2,1)}, bf16[8,64,512]{2,1,0:T(8,128)(2,1)S(1)}, u32[]{:S(2)}) copy-start(bf16[8,64,512]{2,1,0:T(8,128)(2,1)S(1)} %collective-permute-done.4.other_ref.near_other_ref) | copy-start | bytes 1572868
  94.4 28.4 %all-to-all-start.2 = ((bf16[16,72,256]{2,1,0:T(8,128)(2,1)}), bf16[16,72,256]{2,1,0:T(8,128)(2,1)S(1)}, u32[]{:S(2)}, u32[]{:S(2)}) async-start(bf16[16,72,256]{2,1,0:T(8,128)(2,1)} %attend.1), calls=%async_computation.2 | async-start | bytes 1179648 | tf_op jit(solution)/shard_map/all_to_all | solution.py:518
  104.8 4.6 %collective-permute-start.5 = (bf16[8,128,512]{2,1,0:T(8,128)(2,1)S(1)}, bf16[8,128,512]{2,1,0:T(8,128)(2,1)S(1)}, u32[]{:S(2)}, u32[]{:S(2)}) collective-permute-start(bf16[8,128,512]{2,1,0:T(8,128)(2,1)S(1)} %slice.7.hidden_ref), channel_id=1, source_target_pairs={{0,128},{128,0},{1,129},{129,1},{2,130},{130,2},{3,131},{131,3},{4... | collective-permute-start | bytes 3145736 | tf_op jit(solution)/shard_map/ppermute | solution.py:465
  109.4 1.0 copy-start.1
  122.8 1.2 copy-start.2
  124.0 1.0 copy-start.4
Sparse Core Ops, SparseCore 0:
  25.4 45.0 all-gather.2
